TPU v7x, 32 devices: a whole 2x2x4 slice. The times are simulated.
32 devices in a mesh: row: 8 (over z, core), col: 4 (over y, x).
Axes of the slice: x: 2, y: 2, z: 4, core: 2. Of those that a mesh axis runs over, the one named last changes fastest.
Arguments:
- sources: float32 [64, 16384], P(None, 'row'), may hold values from -8 to 8
- targets: float32 [64, 8192], P(None, 'col'), may hold values from -8 to 8
- source_mass: float32 [16384], P('row'), may hold values from 0.1 to 10
- target_mass: float32 [8192], P('col'), may hold values from 0.1 to 10
Outputs:
- source_potential: float32 [16384], P('row')
- target_potential: float32 [8192], P('col')
- source_map: float32 [64, 16384], P(None, 'row')
- target_map: float32 [64, 8192], P(None, 'col')
All inputs are finite; a program needn't handle non-finite values.
Results may differ from a plain program's by a relative error of at most 0.0003.
Values sent between devices are 32-bit elements; how exact they have to be, the bound alone decides.
No kernel may reach another device: no remote copies, remote signals or barrier semaphores. Data moves between devices by JAX's collectives and lax.ppermute only.
A program may use at most 64 MiB of HBM per device.

v0:
```python
import jax
import jax.numpy as jnp
from jax import lax
from jax.sharding import PartitionSpec as P

ITERS = 3


entropy_scale = 0.25
lowest_start = -1e30


def joined(part, axis, combine):
    gathered = jax.tree.map(lambda a: lax.all_gather(a, axis), part)

    def take(source):
        return jax.tree.map(lambda a: lax.dynamic_index_in_dim(a, source, 0, False), gathered)

    return lax.fori_loop(
        1, lax.axis_size(axis), lambda source, state: combine(state, take(source)), take(0)
    )


def tile_sweep(sources, targets, src_term, tgt_term, with_maps):
    block_rows = min(512, sources.shape[1])
    count = sources.shape[1] // block_rows
    depth = sources.shape[0]
    width = targets.shape[1]
    src_norms = jnp.sum(sources * sources, axis=0)
    tgt_norms = jnp.sum(targets * targets, axis=0)

    def one_block(carry, block_index):
        col_peak, col_total, col_vector = carry
        start = block_index * block_rows
        src_block = lax.dynamic_slice_in_dim(sources, start, block_rows, 1)
        norm_block = lax.dynamic_slice_in_dim(src_norms, start, block_rows, 0)
        term_block = lax.dynamic_slice_in_dim(src_term, start, block_rows, 0)
        cross = lax.dot_general(
            src_block,
            targets,
            (((0,), (0,)), ((), ())),
            precision=lax.Precision.HIGHEST,
            preferred_element_type=jnp.float32,
        )
        scores = (2.0 * cross - norm_block[:, None] - tgt_norms[None, :]) / entropy_scale
        row_scores = scores + tgt_term[None, :]
        row_peak = jnp.max(row_scores, axis=1)
        row_weights = jnp.exp(row_scores - row_peak[:, None])
        row_total = jnp.sum(row_weights, axis=1)
        col_scores = scores + term_block[:, None]
        new_peak = jnp.maximum(col_peak, jnp.max(col_scores, axis=0))
        col_weights = jnp.exp(col_scores - new_peak[None, :])
        decay = jnp.exp(col_peak - new_peak)
        col_total = col_total * decay + jnp.sum(col_weights, axis=0)
        if with_maps:
            row_vector = lax.dot_general(
                targets,
                row_weights,
                (((1,), (1,)), ((), ())),
                precision=lax.Precision.HIGHEST,
                preferred_element_type=jnp.float32,
            )
            col_vector = col_vector * decay[None, :] + jnp.dot(
                src_block,
                col_weights,
                precision=lax.Precision.HIGHEST,
                preferred_element_type=jnp.float32,
            )
            return ((new_peak, col_total, col_vector), (row_peak, row_total, row_vector))
        return ((new_peak, col_total, col_vector), (row_peak, row_total))

    start_carry = (
        jnp.full((width,), lowest_start, jnp.float32),
        jnp.zeros((width,), jnp.float32),
        jnp.zeros((depth, width), jnp.float32),
    )
    final, stacked = lax.scan(one_block, start_carry, jnp.arange(count, dtype=jnp.int32))
    row_peak = stacked[0].reshape(-1)
    row_total = stacked[1].reshape(-1)
    if with_maps:
        row_vector = jnp.transpose(stacked[2], (1, 0, 2)).reshape(depth, -1)
        return ((row_peak, row_total, row_vector), final)
    return ((row_peak, row_total), (final[0], final[1]))


def combine(first, second):
    peak = jnp.maximum(first[0], second[0])
    left = jnp.exp(first[0] - peak)
    right = jnp.exp(second[0] - peak)
    rest = tuple((one * left + other * right for one, other in zip(first[1:], second[1:])))
    return (peak,) + rest


def reduce_rows(stats, with_maps):
    if with_maps:
        return joined((stats[0], stats[1], stats[2]), "col", combine)
    return joined((stats[0], stats[1]), "col", combine)


def reduce_cols(stats, with_maps):
    if with_maps:
        return joined((stats[0], stats[1], stats[2]), "row", combine)
    return joined((stats[0], stats[1]), "row", combine)


def body(sources, targets, source_mass, target_mass):
    src_log = jnp.log(source_mass)
    tgt_log = jnp.log(target_mass)
    src_pot = jnp.zeros(source_mass.shape, jnp.float32)
    tgt_pot = jnp.zeros(target_mass.shape, jnp.float32)
    for sweep_index in range(ITERS):
        rows, cols = tile_sweep(
            sources,
            targets,
            src_pot / entropy_scale + src_log,
            tgt_pot / entropy_scale + tgt_log,
            False,
        )
        rows = reduce_rows(rows, False)
        cols = reduce_cols(cols, False)
        src_next = 0.5 * (src_pot - entropy_scale * (rows[0] + jnp.log(rows[1])))
        tgt_next = 0.5 * (tgt_pot - entropy_scale * (cols[0] + jnp.log(cols[1])))
        src_pot, tgt_pot = (src_next, tgt_next)
    rows, cols = tile_sweep(
        sources, targets, src_pot / entropy_scale + src_log, tgt_pot / entropy_scale + tgt_log, True
    )
    rows = reduce_rows(rows, True)
    cols = reduce_cols(cols, True)
    source_map = rows[2] / rows[1][None, :]
    target_map = cols[2] / cols[1][None, :]
    return (src_pot, tgt_pot, source_map, target_map)


def solution(mesh):
    in_specs = (P(None, "row"), P(None, "col"), P("row"), P("col"))
    out_specs = (P("row"), P("col"), P(None, "row"), P(None, "col"))
    return jax.shard_map(body, mesh=mesh, in_specs=in_specs, out_specs=out_specs, check_vma=False)
```

profile of v0, /device:TPU:0, one launch (start us, length us, event | category | flops | bytes accessed | tf_op | source)
XLA Modules:
  0.0 497.2 jit_solution(13440438933905337382)
XLA Ops:
  10.0 50.3 %while.220 = (s32[]{:T(128)}, f32[2048]{0:T(1024)S(1)}, f32[2048]{0:T(1024)S(1)}, f32[4,512]{1,0:T(4,128)S(1)}, f32[4,512]{1,0:T(4,128)S(1)}, /*index=5*/s32[4]{...) while((s32[]{:T(128)}, f32[2048]{0:T(1024)S(1)}, ...), condition=%wide.region_7.8_spmd.clone, body=%wide.region_2.7_spmd.clone.sunk | while | flops 819995648 | bytes 9203958 | solution.py:77
  24.1 7.5 %add_reduce_fusion.12 = (f32[512]{0:T(512)S(1)}, f32[2048]{0:T(1024)S(1)}, f32[512,2048]{1,0:T(8,128)}) fusion(f32[2048]{0:T(1024)S(1)} %get-tuple-element.2615, f32[512]{0:T(512)S(1)} %dynamic_slice.398, f32[2048]{0:T(1024)S(1)} %get-tuple-element.2613, f32[512]{0:T(512)S(1)} %dynamic_slice.399, f32[64,2048]{1,0:T(8,128)} %get-tuple-element.2611, ...), kind=kOutput, calls=%fused_computation.35.clone.1 | convolution fusion | flops 813692416 | bytes 4880388 | tf_op jit(solution)/shard_map/while/body/eval_jaxpr/dot_general | solution.py:38
  60.4 9.6 %all-gather.9 = f32[4,1,2048]{2,1,0:T(1,128)S(1)} all-gather(f32[1,1,2048]{2,1,0:T(1,128)S(1)} %reshape.74), channel_id=1, replica_groups=mesh['row'=8,'col'=4] {'col'}, dimensions={0}, use_global_device_ids=true | all-gather | bytes 40960 | tf_op jit(solution)/shard_map/all_gather | solution.py:14
  70.0 8.1 %all-gather.10 = f32[4,1,2048]{2,1,0:T(1,128)S(1)} all-gather(f32[1,1,2048]{2,1,0:T(1,128)S(1)} %reshape.76), channel_id=1, replica_groups=mesh['row'=8,'col'=4] {'col'}, dimensions={0}, use_global_device_ids=true | all-gather | bytes 40960 | tf_op jit(solution)/shard_map/all_gather | solution.py:14
  78.2 14.2 %all-gather = f32[16384]{0:T(1024)S(1)} all-gather(f32[2048]{0:T(1024)S(1)} %get-tuple-element.1432), channel_id=2, replica_groups=mesh['row'=8,'col'=4] {'row'}, dimensions={0}, use_global_device_ids=true | all-gather | bytes 73728 | tf_op jit(solution)/shard_map/all_gather | solution.py:14
  92.4 14.5 %all-gather.1 = f32[16384]{0:T(1024)S(1)} all-gather(f32[2048]{0:T(1024)S(1)} %get-tuple-element.1433), channel_id=3, replica_groups=mesh['row'=8,'col'=4] {'row'}, dimensions={0}, use_global_device_ids=true | all-gather | bytes 73728 | tf_op jit(solution)/shard_map/all_gather | solution.py:14
  107.7 49.7 %while.221 = (s32[]{:T(128)}, f32[2048]{0:T(1024)S(1)}, f32[2048]{0:T(1024)S(1)}, f32[4,512]{1,0:T(4,128)S(1)}, f32[4,512]{1,0:T(4,128)S(1)}, /*index=5*/s32[4]{...) while((s32[]{:T(128)}, f32[2048]{0:T(1024)S(1)}, ...), condition=%wide.region_17.18_spmd.clone, body=%wide.region_12.0_spmd.clone.sunk | while | flops 819995648 | bytes 9203958 | solution.py:77
  164.7 8.1 %all-gather.12 = f32[4,1,2048]{2,1,0:T(1,128)S(1)} all-gather(f32[1,1,2048]{2,1,0:T(1,128)S(1)} %reshape.80), channel_id=1, replica_groups=mesh['row'=8,'col'=4] {'col'}, dimensions={0}, use_global_device_ids=true | all-gather | bytes 40960 | tf_op jit(solution)/shard_map/all_gather | solution.py:14
  172.9 14.0 %all-gather.2 = f32[16384]{0:T(1024)S(1)} all-gather(f32[2048]{0:T(1024)S(1)} %get-tuple-element.1440), channel_id=4, replica_groups=mesh['row'=8,'col'=4] {'row'}, dimensions={0}, use_global_device_ids=true | all-gather | bytes 73728 | tf_op jit(solution)/shard_map/all_gather | solution.py:14
  186.9 14.2 %all-gather.3 = f32[16384]{0:T(1024)S(1)} all-gather(f32[2048]{0:T(1024)S(1)} %get-tuple-element.1441), channel_id=5, replica_groups=mesh['row'=8,'col'=4] {'row'}, dimensions={0}, use_global_device_ids=true | all-gather | bytes 73728 | tf_op jit(solution)/shard_map/all_gather | solution.py:14
  201.8 49.7 %while.222 = (s32[]{:T(128)}, f32[2048]{0:T(1024)S(1)}, f32[2048]{0:T(1024)S(1)}, f32[4,512]{1,0:T(4,128)S(1)}, f32[4,512]{1,0:T(4,128)S(1)}, /*index=5*/s32[4]{...) while((s32[]{:T(128)}, f32[2048]{0:T(1024)S(1)}, ...), condition=%wide.region_27.28_spmd.clone, body=%wide.region_22.0_spmd.clone.sunk | while | flops 819995648 | bytes 9203958 | solution.py:77
  258.8 8.1 %all-gather.14 = f32[4,1,2048]{2,1,0:T(1,128)S(1)} all-gather(f32[1,1,2048]{2,1,0:T(1,128)S(1)} %reshape.84), channel_id=1, replica_groups=mesh['row'=8,'col'=4] {'col'}, dimensions={0}, use_global_device_ids=true | all-gather | bytes 40960 | tf_op jit(solution)/shard_map/all_gather | solution.py:14
  267.0 14.0 %all-gather.4 = f32[16384]{0:T(1024)S(1)} all-gather(f32[2048]{0:T(1024)S(1)} %get-tuple-element.1448), channel_id=6, replica_groups=mesh['row'=8,'col'=4] {'row'}, dimensions={0}, use_global_device_ids=true | all-gather | bytes 73728 | tf_op jit(solution)/shard_map/all_gather | solution.py:14
  281.0 14.0 %all-gather.5 = f32[16384]{0:T(1024)S(1)} all-gather(f32[2048]{0:T(1024)S(1)} %get-tuple-element.1449), channel_id=7, replica_groups=mesh['row'=8,'col'=4] {'row'}, dimensions={0}, use_global_device_ids=true | all-gather | bytes 73728 | tf_op jit(solution)/shard_map/all_gather | solution.py:14
  296.9 95.9 %while.223 = (s32[]{:T(128)}, f32[2048]{0:T(1024)S(1)}, f32[2048]{0:T(1024)S(1)}, f32[64,2048]{1,0:T(8,128)S(1)}, f32[4,512]{1,0:T(4,128)S(1)}, /*index=5*/f32[4...) while((s32[]{:T(128)}, f32[2048]{0:T(1024)S(1)}, ...), condition=%wide.region_37.38_spmd.clone, body=%wide.region_32.0_spmd.clone.sunk | while | flops 2435195904 | bytes 38338884 | solution.py:77
  298.5 7.5 %add_reduce_fusion.15 = (f32[512]{0:T(512)S(1)}, f32[2048]{0:T(1024)S(1)}, f32[512,2048]{1,0:T(8,128)}) fusion(f32[2048]{0:T(1024)S(1)} %get-tuple-element.2909, f32[512]{0:T(512)S(1)} %dynamic_slice.411, f32[2048]{0:T(1024)S(1)} %get-tuple-element.2907, f32[512]{0:T(512)S(1)} %dynamic_slice.412, f32[64,2048]{1,0:T(8,128)} %get-tuple-element.2905, ...), kind=kOutput, calls=%fused_computation.65.clone.1 | convolution fusion | flops 813692416 | bytes 4880388 | tf_op jit(solution)/shard_map/while/body/eval_jaxpr/dot_general | solution.py:38
  322.4 7.5 %add_reduce_fusion.15 = (f32[512]{0:T(512)S(1)}, f32[2048]{0:T(1024)S(1)}, f32[512,2048]{1,0:T(8,128)}) fusion(f32[2048]{0:T(1024)S(1)} %get-tuple-element.2909, f32[512]{0:T(512)S(1)} %dynamic_slice.411, f32[2048]{0:T(1024)S(1)} %get-tuple-element.2907, f32[512]{0:T(512)S(1)} %dynamic_slice.412, f32[64,2048]{1,0:T(8,128)} %get-tuple-element.2905, ...), kind=kOutput, calls=%fused_computation.65.clone.1 | convolution fusion | flops 813692416 | bytes 4880388 | tf_op jit(solution)/shard_map/while/body/eval_jaxpr/dot_general | solution.py:38
  346.2 7.5 %add_reduce_fusion.15 = (f32[512]{0:T(512)S(1)}, f32[2048]{0:T(1024)S(1)}, f32[512,2048]{1,0:T(8,128)}) fusion(f32[2048]{0:T(1024)S(1)} %get-tuple-element.2909, f32[512]{0:T(512)S(1)} %dynamic_slice.411, f32[2048]{0:T(1024)S(1)} %get-tuple-element.2907, f32[512]{0:T(512)S(1)} %dynamic_slice.412, f32[64,2048]{1,0:T(8,128)} %get-tuple-element.2905, ...), kind=kOutput, calls=%fused_computation.65.clone.1 | convolution fusion | flops 813692416 | bytes 4880388 | tf_op jit(solution)/shard_map/while/body/eval_jaxpr/dot_general | solution.py:38
  370.1 7.5 %add_reduce_fusion.15 = (f32[512]{0:T(512)S(1)}, f32[2048]{0:T(1024)S(1)}, f32[512,2048]{1,0:T(8,128)}) fusion(f32[2048]{0:T(1024)S(1)} %get-tuple-element.2909, f32[512]{0:T(512)S(1)} %dynamic_slice.411, f32[2048]{0:T(1024)S(1)} %get-tuple-element.2907, f32[512]{0:T(512)S(1)} %dynamic_slice.412, f32[64,2048]{1,0:T(8,128)} %get-tuple-element.2905, ...), kind=kOutput, calls=%fused_computation.65.clone.1 | convolution fusion | flops 813692416 | bytes 4880388 | tf_op jit(solution)/shard_map/while/body/eval_jaxpr/dot_general | solution.py:38
  402.4 8.3 %all-gather.16 = f32[4,1,2048]{2,1,0:T(1,128)S(1)} all-gather(f32[1,1,2048]{2,1,0:T(1,128)S(1)} %reshape.88), channel_id=1, replica_groups=mesh['row'=8,'col'=4] {'col'}, dimensions={0}, use_global_device_ids=true | all-gather | bytes 40960 | tf_op jit(solution)/shard_map/all_gather | solution.py:14
  410.7 14.0 %all-gather.6 = f32[16384]{0:T(1024)S(1)} all-gather(f32[2048]{0:T(1024)S(1)} %get-tuple-element.1457), channel_id=8, replica_groups=mesh['row'=8,'col'=4] {'row'}, dimensions={0}, use_global_device_ids=true | all-gather | bytes 73728 | tf_op jit(solution)/shard_map/all_gather | solution.py:14
  424.7 14.0 %all-gather.7 = f32[16384]{0:T(1024)S(1)} all-gather(f32[2048]{0:T(1024)S(1)} %get-tuple-element.1458), channel_id=9, replica_groups=mesh['row'=8,'col'=4] {'row'}, dimensions={0}, use_global_device_ids=true | all-gather | bytes 73728 | tf_op jit(solution)/shard_map/all_gather | solution.py:14
  444.8 34.1 %all-gather.22.cloned.1.call-done = f32[512,2048]{1,0:T(8,128)} async-done(((f32[64,2048]{1,0:T(8,128)}), f32[512,2048]{1,0:T(8,128)}) %all-gather.22.cloned.1.call-update) | async-done | bytes 4194320 | tf_op jit(solution)/shard_map/all_gather | solution.py:14
  479.9 9.3 %while.219 = (s32[]{:T(128)}, f32[2048]{0:T(1024)S(1)}, f32[2048]{0:T(1024)S(1)}, f32[64,2048]{1,0:T(8,128)S(1)}, f32[8,2048]{1,0:T(8,128)S(1)}, /*index=5*/f32[...) while((s32[]{:T(128)}, f32[2048]{0:T(1024)S(1)}, f32[2048]{0:T(1024)S(1)}, ...), condition=%wide.region_41.42_spmd, body=%wide.region_40.41_spmd.sunk | while | flops 405509 | bytes 1687703 | solution.py:19
  (367 shorter events, 248.6 us)
Async XLA Ops:
  7.2 431.6 %all-gather.20.cloned.1.call-start = ((), (), s32[]{:S(2)}) async-start(), calls=%async_computation | async-start | bytes 2621440 | tf_op jit(solution)/shard_map/all_gather | solution.py:14
  10.0 97.6 %copy-start.3 = (f32[2048]{0:T(1024)S(1)}, f32[2048]{0:T(1024)}, u32[]{:S(2)}) copy-start(f32[2048]{0:T(1024)} %param.30) | copy-start | bytes 24580
  10.0 97.6 %copy-start.4 = (f32[2048]{0:T(1024)S(1)}, f32[2048]{0:T(1024)}, u32[]{:S(2)}) copy-start(f32[2048]{0:T(1024)} %param.31) | copy-start | bytes 24580
  306.0 3.7 copy-start
  306.0 8.0 %copy-start.2 = (f32[64,2048]{1,0:T(8,128)S(1)}, f32[64,2048]{1,0:T(8,128)}, u32[]{:S(2)}) copy-start(f32[64,2048]{1,0:T(8,128)} %get-tuple-element.2905) | copy-start | bytes 1572868 | tf_op jit(solution)/shard_map/while
  329.9 3.7 copy-start
  329.9 8.1 %copy-start.2 = (f32[64,2048]{1,0:T(8,128)S(1)}, f32[64,2048]{1,0:T(8,128)}, u32[]{:S(2)}) copy-start(f32[64,2048]{1,0:T(8,128)} %get-tuple-element.2905) | copy-start | bytes 1572868 | tf_op jit(solution)/shard_map/while
  353.7 3.7 copy-start
  353.7 8.1 %copy-start.2 = (f32[64,2048]{1,0:T(8,128)S(1)}, f32[64,2048]{1,0:T(8,128)}, u32[]{:S(2)}) copy-start(f32[64,2048]{1,0:T(8,128)} %get-tuple-element.2905) | copy-start | bytes 1572868 | tf_op jit(solution)/shard_map/while
  377.6 3.7 copy-start
  377.6 8.1 %copy-start.2 = (f32[64,2048]{1,0:T(8,128)S(1)}, f32[64,2048]{1,0:T(8,128)}, u32[]{:S(2)}) copy-start(f32[64,2048]{1,0:T(8,128)} %get-tuple-element.2905) | copy-start | bytes 1572868 | tf_op jit(solution)/shard_map/while
  392.8 1.6 copy-start.1
  394.4 84.5 %all-gather.22.cloned.1.call-start = ((), (), s32[]{:S(2)}) async-start(), calls=%async_computation.1 | async-start | bytes 4718592 | tf_op jit(solution)/shard_map/all_gather | solution.py:14
Sparse Core Ops, SparseCore 0:
  394.5 35.5 all-gather.19
  431.7 47.1 all-gather.21
where the time goes:
time: 504 us; the launch traced here: 497 us
  blocking collectives  177 us (35%)
  matrix products  164 us (33%)
  other arithmetic  73.5 us (15%)
  waiting for transfers between devices  34.8 us (7%)
  local copies, waits for them, and re-layouts  20.1 us (4%)
  between operations  14.7 us (3%)
  loops' own time  13.3 us (3%)
    all_gather x16, blocking collectives, joined(): gathered = jax.tree.map(lambda a: lax.all_gather(a, axis), part)  177 us
    dot_general x16, matrix products, one_block(): lax.dot_general(src_block, targets, (((0,), (0,)), ((), ())), precision=l...  120 us
    reduce_sum x16, other arithmetic, one_block(): row_total = jnp.sum(row_weights, axis=1)  55.7 us
    all_gather x2, waiting for transfers between devices, joined(): gathered = jax.tree.map(lambda a: lax.all_gather(a, axis), part)  34.1 us
    dot_general x4, matrix products, one_block(): lax.dot_general(targets, row_weights, (((1,), (1,)), ((), ())), precision...  27.6 us
    dot_general x4, matrix products, one_block(): jnp.dot(src_block, col_weights, precision=lax.Precision.HIGHEST, preferre...  16.8 us
    add x50, other arithmetic, combine(): one * left + other * right  13.2 us
    another operation x4, loops' own time, tile_sweep(): lax.scan(one_block, start_carry, jnp.arange(count, dtype=jnp.int32))  11.9 us
  transfers between devices with their start and end apart: 2, of which 1 were waited for; matrix products, arithmetic and copies ran while one was open for 1% of the time, Pallas kernels for 0%

commit v1 on v0

v1 whole, which is shorter than its diff:
```python
import functools

import jax
import jax.numpy as jnp
from jax import lax
from jax.experimental import pallas as pl
from jax.experimental.pallas import tpu as pltpu
from jax.sharding import PartitionSpec as P

ITERS = 3
EPS = 0.25
LOG2E = 1.4426950408889634
LN2 = 0.6931471805599453
SHIFT = 85.0
SMALLEST = 2.0**-85
FACTOR_RANGE = 60.0 * LN2
LANES = 128
F32 = jnp.float32
BF16 = jnp.bfloat16
HIGH = lax.Precision.HIGHEST


def split2(a):
    a1 = a.astype(BF16).astype(F32)
    return a1, a - a1


def split3(a):
    a1, rest = split2(a)
    a2, rest = split2(rest)
    return a1, a2, rest


def spread(u, ub):
    for b in range(u.shape[0]):
        ub[b * LANES : (b + 1) * LANES, :] = jnp.broadcast_to(u[b : b + 1, :], (LANES, LANES)).T


def lane_sums(acc, out):
    for b in range(out.shape[0]):
        out[b : b + 1, :] = jnp.sum(acc[b * LANES : (b + 1) * LANES, :].T, axis=0, keepdims=True)


def fold(a):
    return jnp.sum(a.reshape(a.shape[0] // 8, 8, a.shape[1]), axis=0)


def build_operands(x_ref, y_ref, xa, ya):
    d, ns = x_ref.shape
    nt = y_ref.shape[1]
    y = y_ref[...]
    yn = jnp.sum(y * y, axis=0, keepdims=True) * (LOG2E / EPS)
    y1, y2, y3 = (part.astype(BF16) for part in split3(y * (2.0 * LOG2E / EPS)))
    for at, part in enumerate((y1, y2, y1, y2, y3, y1)):
        ya[at * d : (at + 1) * d, :] = part
    m1, m2, m3 = split3(SHIFT - yn)
    row = lax.broadcasted_iota(jnp.int32, (2 * d, nt), 0)
    tail = jnp.where(
        row == 0, m1, jnp.where(row == 1, m2, jnp.where(row == 2, m3, jnp.where(row < 6, 1.0, 0.0)))
    )
    ya[6 * d : 8 * d, :] = tail.astype(BF16)
    lane = lax.broadcasted_iota(jnp.int32, (LANES, 2 * d), 1)

    def block(b, _):
        at = pl.multiple_of(b * LANES, LANES)
        xb = x_ref[:, pl.ds(at, LANES)]
        both = jnp.concatenate([xb, xb], axis=0).T
        norm = jnp.sum(jnp.where(lane < d, both * both, 0.0), axis=1, keepdims=True) * (-LOG2E / EPS)
        x1, x2, x3 = split3(both)
        n1, n2, n3 = split3(norm)
        rows = pl.ds(at, LANES)
        xa[rows, 0 : 2 * d] = x1.astype(BF16)
        xa[rows, 2 * d : 4 * d] = x2.astype(BF16)
        xa[rows, 4 * d : 6 * d] = jnp.where(lane < d, x1, x3).astype(BF16)
        xa[rows, 6 * d : 8 * d] = jnp.where(
            lane < 3,
            1.0,
            jnp.where(lane == 3, n1, jnp.where(lane == 4, n2, jnp.where(lane == 5, n3, 0.0))),
        ).astype(BF16)
        return 0

    lax.fori_loop(0, ns // LANES, block, 0)


def as_row(ref):
    return jnp.concatenate([ref[b : b + 1, :] for b in range(ref.shape[0])], axis=1)


def put_row(row, ref):
    for b in range(ref.shape[0]):
        ref[b : b + 1, :] = row[:, b * LANES : (b + 1) * LANES]


def general_sweep(x_ref, y_ref, r_ref, t_ref, row_lse, col_lse, row_map, col_map, ub):
    d, ns = x_ref.shape
    nt = y_ref.shape[1]
    with_maps = row_map is not None
    spread(r_ref[...], ub)
    y = y_ref[...]
    yn = jnp.sum(y * y, axis=0, keepdims=True)
    t = as_row(t_ref)

    def block(b, carry):
        at = pl.multiple_of(b * LANES, LANES)
        xb = x_ref[:, pl.ds(at, LANES)]
        xt = xb.T
        xn = jnp.sum(xt * xt, axis=1, keepdims=True)
        cross = jnp.dot(xt, y, precision=HIGH, preferred_element_type=F32)
        scores = (2.0 * cross - xn - yn) / EPS
        row_scores = scores + t
        peak = jnp.max(row_scores, axis=1, keepdims=True)
        weights = jnp.exp(row_scores - peak)
        total = jnp.sum(weights, axis=1, keepdims=True)
        row_lse[pl.ds(b, 1), :] = jnp.broadcast_to(peak + jnp.log(total), (LANES, LANES)).T[0:1, :]
        if with_maps:
            vector = lax.dot_general(
                weights / total, y, (((1,), (1,)), ((), ())), precision=HIGH, preferred_element_type=F32
            )
            row_map[0:d, pl.ds(at, LANES)] = jnp.concatenate([vector, vector], axis=1).T[0:d, :]
        col_scores = scores + ub[pl.ds(at, LANES), 0:1]
        new_peak = jnp.maximum(carry[0], jnp.max(col_scores, axis=0, keepdims=True))
        decay = jnp.exp(carry[0] - new_peak)
        col_weights = jnp.exp(col_scores - new_peak)
        total = carry[1] * decay + jnp.sum(col_weights, axis=0, keepdims=True)
        if with_maps:
            col_map[0:d, :] = col_map[0:d, :] * decay + jnp.dot(
                xb, col_weights, precision=HIGH, preferred_element_type=F32
            )
        return new_peak, total

    if with_maps:
        col_map[0:d, :] = jnp.zeros((d, nt), F32)
    start = (jnp.full((1, nt), -1e30, F32), jnp.zeros((1, nt), F32))
    peak, total = lax.fori_loop(0, ns // LANES, block, start)
    put_row(peak + jnp.log(total), col_lse)
    if with_maps:
        col_map[0:d, :] = col_map[0:d, :] / total


def factors(term):
    top = jnp.max(term)
    return jnp.exp(term - top), top, top - jnp.min(term) <= FACTOR_RANGE


def finish(row_ref, col_ref, r_top, t_top, fine):
    rows, cols = row_ref[...], col_ref[...]
    fine = fine & (jnp.min(rows) >= SMALLEST) & (jnp.min(cols) >= SMALLEST)
    row_ref[...] = jnp.log(rows) + (t_top - SHIFT * LN2)
    col_ref[...] = jnp.log(cols) + (r_top - SHIFT * LN2)
    return fine


def form_kernel(x_ref, y_ref, a_ref, b_ref, k_ref, row_ref, col_ref, xa, ya, ub, acc, r_s, t_s, *, rows):
    ns, nt = x_ref.shape[1], y_ref.shape[1]
    r_s[...] = jnp.log(a_ref[...])
    t_s[...] = jnp.log(b_ref[...])
    u, r_top, u_fine = factors(r_s[...])
    v, t_top, v_fine = factors(t_s[...])
    build_operands(x_ref, y_ref, xa, ya)
    spread(u, ub)
    col_ref[...] = v
    acc[...] = jnp.zeros_like(acc)
    wide = 2 * LANES

    def block(cb, _):
        at = pl.multiple_of(cb * wide, wide)
        v0 = col_ref[pl.ds(cb * 2, 1), :]
        v1 = col_ref[pl.ds(cb * 2 + 1, 1), :]
        c0 = jnp.zeros((8, LANES), F32)
        c1 = jnp.zeros((8, LANES), F32)
        for r in range(0, ns, rows):
            z = jnp.dot(xa[r : r + rows, :], ya[:, pl.ds(at, wide)], preferred_element_type=F32)
            k = jnp.exp2(z)
            k_ref[r : r + rows, pl.ds(at, wide)] = k
            k0, k1 = k[:, :LANES], k[:, LANES:]
            acc[r : r + rows, :] += k0 * v0 + k1 * v1
            ur = ub[r : r + rows, :]
            c0 += fold(k0 * ur)
            c1 += fold(k1 * ur)
        col_ref[pl.ds(cb * 2, 1), :] = jnp.sum(c0, axis=0, keepdims=True)
        col_ref[pl.ds(cb * 2 + 1, 1), :] = jnp.sum(c1, axis=0, keepdims=True)
        return 0

    lax.fori_loop(0, nt // wide, block, 0)
    lane_sums(acc, row_ref)
    fine = finish(row_ref, col_ref, r_top, t_top, u_fine & v_fine)

    @pl.when(jnp.logical_not(fine))
    def _():
        general_sweep(x_ref, y_ref, r_s, t_s, row_ref, col_ref, None, None, ub)


def update(pot_ref, lse_ref, mass_ref, new_ref, term):
    new_ref[...] = 0.5 * (pot_ref[...] - EPS * lse_ref[...])
    term[...] = new_ref[...] / EPS + jnp.log(mass_ref[...])


def sums_kernel(
    k_ref, x_ref, y_ref, f_ref, g_ref, rl_ref, cl_ref, a_ref, b_ref,
    fn_ref, gn_ref, row_ref, col_ref, ub, acc, vs, r_s, t_s, *, rows,
):
    update(f_ref, rl_ref, a_ref, fn_ref, r_s)
    update(g_ref, cl_ref, b_ref, gn_ref, t_s)
    u, r_top, u_fine = factors(r_s[...])
    v, t_top, v_fine = factors(t_s[...])
    spread(u, ub)
    vs[...] = v
    ns, nt = k_ref.shape
    tiles = nt // LANES

    def block(rb, cs):
        at = pl.multiple_of(rb * rows, rows)
        ur = ub[pl.ds(at, rows), :]
        total = jnp.zeros((rows, LANES), F32)
        out = []
        for c in range(tiles):
            k = k_ref[pl.ds(at, rows), c * LANES : (c + 1) * LANES]
            total += k * vs[c : c + 1, :]
            out.append(cs[c] + fold(k * ur))
        acc[pl.ds(at, rows), :] = total
        return tuple(out)

    cs = lax.fori_loop(0, ns // rows, block, (jnp.zeros((8, LANES), F32),) * tiles)
    for c in range(tiles):
        col_ref[c : c + 1, :] = jnp.sum(cs[c], axis=0, keepdims=True)
    lane_sums(acc, row_ref)
    fine = finish(row_ref, col_ref, r_top, t_top, u_fine & v_fine)

    @pl.when(jnp.logical_not(fine))
    def _():
        general_sweep(x_ref, y_ref, r_s, t_s, row_ref, col_ref, None, None, ub)


def maps_kernel(
    k_ref, x_ref, y_ref, f_ref, g_ref, rl_ref, cl_ref, a_ref, b_ref,
    fn_ref, gn_ref, rowm_ref, colm_ref, row_s, col_s, ub, wy, xu, acc, cacc, r_s, t_s, *, rows,
):
    d = x_ref.shape[0]
    ns, nt = k_ref.shape
    update(f_ref, rl_ref, a_ref, fn_ref, r_s)
    update(g_ref, cl_ref, b_ref, gn_ref, t_s)
    u, r_top, u_fine = factors(r_s[...])
    v, t_top, v_fine = factors(t_s[...])
    lane = lax.broadcasted_iota(jnp.int32, (LANES, 2 * d), 1)
    sub = lax.broadcasted_iota(jnp.int32, (16, LANES), 0)
    for b in range(nt // LANES):
        at = slice(b * LANES, (b + 1) * LANES)
        vb = v[b : b + 1, :]
        yb = y_ref[:, at] * vb
        p1, p2 = split2(jnp.concatenate([yb, yb], axis=0).T)
        wy[at, 0 : 2 * d] = jnp.where(lane < d, p1, p2).astype(BF16)
        p1, p2 = split2(jnp.broadcast_to(vb, (2 * d, LANES)).T)
        wy[at, 2 * d : 4 * d] = jnp.where(lane == 0, p1, jnp.where(lane == 1, p2, 0.0)).astype(BF16)
    for b in range(ns // LANES):
        at = slice(b * LANES, (b + 1) * LANES)
        uv = u[b : b + 1, :]
        p1, p2 = split2(x_ref[:, at] * uv)
        xu[0:d, at] = p1.astype(BF16)
        xu[d : 2 * d, at] = p2.astype(BF16)
        p1, p2 = split2(jnp.broadcast_to(uv, (16, LANES)))
        xu[2 * d : 2 * d + 16, at] = jnp.where(sub == 0, p1, jnp.where(sub == 1, p2, 0.0)).astype(BF16)
    wide = 2 * LANES
    acc[...] = jnp.zeros_like(acc)

    def block(cb, _):
        at = pl.multiple_of(cb * wide, wide)
        w = wy[pl.ds(at, wide), :]
        ww = jnp.concatenate([w, w], axis=0)
        total = jnp.zeros((xu.shape[0], wide), F32)
        for r in range(0, ns, rows):
            k = k_ref[r : r + rows, pl.ds(at, wide)]
            k1 = k.astype(BF16)
            k2 = (k - k1.astype(F32)).astype(BF16)
            acc[r : r + rows, :] += jnp.dot(
                jnp.concatenate([k1, k2], axis=1), ww, preferred_element_type=F32
            )
            xr = xu[:, r : r + rows]
            total += jnp.dot(
                jnp.concatenate([xr, xr], axis=1),
                jnp.concatenate([k1, k2], axis=0),
                preferred_element_type=F32,
            )
        cacc[:, pl.ds(at, wide)] = total
        return 0

    lax.fori_loop(0, nt // wide, block, 0)
    for b in range(ns // LANES):
        at = slice(b * LANES, (b + 1) * LANES)
        num = acc[at, 0 : 2 * d].T
        den = acc[at, 2 * d : 4 * d].T
        den = den[0:1, :] + den[1:2, :]
        rowm_ref[0:d, at] = (num[0:d, :] + num[d : 2 * d, :]) / den
        row_s[b : b + 1, :] = den
    for b in range(nt // LANES):
        at = slice(b * LANES, (b + 1) * LANES)
        den = cacc[2 * d : 2 * d + 1, at] + cacc[2 * d + 1 : 2 * d + 2, at]
        colm_ref[0:d, at] = (cacc[0:d, at] + cacc[d : 2 * d, at]) / den
        col_s[b : b + 1, :] = den
    fine = finish(row_s, col_s, r_top, t_top, u_fine & v_fine)

    @pl.when(jnp.logical_not(fine))
    def _():
        general_sweep(x_ref, y_ref, r_s, t_s, row_s, col_s, rowm_ref, colm_ref, ub)

    for ref, lse in ((rowm_ref, row_s), (colm_ref, col_s)):
        for b in range(lse.shape[0]):
            ref[d : d + 8, b * LANES : (b + 1) * LANES] = jnp.broadcast_to(lse[b : b + 1, :], (8, LANES))


VM = pl.BlockSpec(memory_space=pltpu.VMEM)
PARAMS = pltpu.CompilerParams(vmem_limit_bytes=36 * 2**20)


def vector(n):
    return jax.ShapeDtypeStruct((n // LANES, LANES), F32)


def scratch(n):
    return pltpu.VMEM((n // LANES, LANES), F32)


def form(x, y, a, b):
    d, ns = x.shape
    nt = y.shape[1]
    return pl.pallas_call(
        functools.partial(form_kernel, rows=256),
        out_shape=(pltpu.VMEM((ns, nt), F32), vector(ns), vector(nt)),
        in_specs=[VM] * 4,
        out_specs=(VM,) * 3,
        scratch_shapes=[
            pltpu.VMEM((ns, 8 * d), BF16),
            pltpu.VMEM((8 * d, nt), BF16),
            pltpu.VMEM((ns, LANES), F32),
            pltpu.VMEM((ns, LANES), F32),
            scratch(ns),
            scratch(nt),
        ],
        compiler_params=PARAMS,
        name="form",
    )(x, y, a, b)


def sums(k, x, y, *vectors):
    ns, nt = k.shape
    return pl.pallas_call(
        functools.partial(sums_kernel, rows=64),
        out_shape=(vector(ns), vector(nt), vector(ns), vector(nt)),
        in_specs=[VM] * 9,
        out_specs=(VM,) * 4,
        scratch_shapes=[
            pltpu.VMEM((ns, LANES), F32),
            pltpu.VMEM((ns, LANES), F32),
            scratch(nt),
            scratch(ns),
            scratch(nt),
        ],
        compiler_params=PARAMS,
        name="sums",
    )(k, x, y, *vectors)


def maps(k, x, y, *vectors):
    d = x.shape[0]
    ns, nt = k.shape
    return pl.pallas_call(
        functools.partial(maps_kernel, rows=512),
        out_shape=(
            vector(ns),
            vector(nt),
            jax.ShapeDtypeStruct((d + 8, ns), F32),
            jax.ShapeDtypeStruct((d + 8, nt), F32),
        ),
        in_specs=[VM] * 9,
        out_specs=(VM,) * 4,
        scratch_shapes=[
            scratch(ns),
            scratch(nt),
            pltpu.VMEM((ns, LANES), F32),
            pltpu.VMEM((nt, 4 * d), BF16),
            pltpu.VMEM((2 * d + 16, ns), BF16),
            pltpu.VMEM((ns, 4 * d), F32),
            pltpu.VMEM((2 * d + 16, nt), F32),
            scratch(ns),
            scratch(nt),
        ],
        compiler_params=PARAMS,
        name="maps",
    )(k, x, y, *vectors)


def merged(first, second):
    peak = jnp.maximum(first, second)
    return peak + jnp.log(jnp.exp(first - peak) + jnp.exp(second - peak))


def lse_over(axis, part):
    n = lax.axis_size(axis)
    step = 1
    while step < n:
        part = merged(part, lax.ppermute(part, axis, [(i, i ^ step) for i in range(n)]))
        step *= 2
    return part


def weighed(parts):
    d = parts[0].shape[0] - 8
    peak = functools.reduce(jnp.maximum, [p[d : d + 1] for p in parts])
    weights = [jnp.exp(p[d : d + 1] - peak) for p in parts]
    total = sum(weights)
    return sum(p[:d] * w for p, w in zip(parts, weights)) / total, peak + jnp.log(total)


def piece(a, index, count):
    width = a.shape[1] // count
    return lax.dynamic_slice_in_dim(a, index * width, width, 1)


def map_over(axis, group, stride, part):
    n = lax.axis_size(axis)
    me = lax.axis_index(axis)
    place = (me // stride) % group

    def pairs(k):
        return [
            (i, i + (((i // stride) + k) % group - (i // stride) % group) * stride) for i in range(n)
        ]

    got = [piece(part, place, group)]
    for k in range(1, group):
        got.append(lax.ppermute(piece(part, (place + k) % group, group), axis, pairs(k)))
    own, _ = weighed(got)
    return gathered(axis, group, pairs, place, own)


def gathered(axis, group, pairs, place, own):
    width = own.shape[1]
    out = jnp.zeros((own.shape[0], width * group), F32)
    out = lax.dynamic_update_slice_in_dim(out, own, place * width, 1)
    for k in range(1, group):
        other = lax.ppermute(own, axis, pairs(k))
        out = lax.dynamic_update_slice_in_dim(out, other, ((place - k) % group) * width, 1)
    return out


def body(sources, targets, source_mass, target_mass):
    a = source_mass.reshape(-1, LANES)
    b = target_mass.reshape(-1, LANES)
    f = jnp.zeros_like(a)
    g = jnp.zeros_like(b)
    k, row_part, col_part = form(sources, targets, a, b)
    for sweep in range(ITERS):
        col_lse = lse_over("row", col_part)
        row_lse = lse_over("col", row_part)
        if sweep < ITERS - 1:
            f, g, row_part, col_part = sums(k, sources, targets, f, g, row_lse, col_lse, a, b)
        else:
            f, g, row_map, col_map = maps(k, sources, targets, f, g, row_lse, col_lse, a, b)
    rows = lax.axis_size("row")
    me = lax.axis_index("row")
    half = me % 2
    pair = [(i, i ^ 1) for i in range(rows)]
    mine = piece(col_map, half, 2)
    other = lax.ppermute(piece(col_map, 1 - half, 2), "row", pair)
    values, lse = weighed([mine, other])
    chip = jnp.concatenate([values, jnp.broadcast_to(lse, (8, lse.shape[1]))], axis=0)
    ours = map_over("row", rows // 2, 2, chip)
    theirs = lax.ppermute(ours, "row", pair)
    target_map = jnp.where(
        half == 0, jnp.concatenate([ours, theirs], axis=1), jnp.concatenate([theirs, ours], axis=1)
    )
    source_map = map_over("col", lax.axis_size("col"), 1, row_map)
    return f.reshape(-1), g.reshape(-1), source_map, target_map


def solution(mesh):
    in_specs = (P(None, "row"), P(None, "col"), P("row"), P("col"))
    out_specs = (P("row"), P("col"), P(None, "row"), P(None, "col"))
    return jax.shard_map(body, mesh=mesh, in_specs=in_specs, out_specs=out_specs, check_vma=False)
```

time: 504 us -> 238 us (0.47); the launches traced: 497 us -> 237 us
  blocking collectives: 177 us -> 0 us
  Pallas kernels: 0 us -> 172 us
  matrix products: 164 us -> 0 us
  other arithmetic: 73.5 us -> 1.33 us
  starting transfers between devices: 0.08 us -> 43.5 us
  waiting for transfers between devices: 34.8 us -> 15.1 us
  local copies, waits for them, and re-layouts: 20.1 us -> 3.7 us
  between operations: 14.7 us -> 1.26 us
  loops' own time: 13.3 us -> 0 us
    all_gather x16 -> x0, blocking collectives: 177 us -> none  [joined(): gathered = jax.tree.map(lambda a: lax.all_gather(a, axis), part)]
    pallas_call x0 -> x4, Pallas kernels: none -> 172 us  [the longest x1 75.7 us: maps(): pl.pallas_call(functools.partial(maps_kernel, rows=512), out_shape=(vecto...]
    dot_general x24 -> x0, matrix products: 164 us -> none  [the longest x16 120 us: one_block(): lax.dot_general(src_block, targets, (((0,), (0,)), ((), ())), precision=l...]
    reduce_sum x17 -> x0, other arithmetic: 57 us -> none  [the longest x16 55.7 us: one_block(): row_total = jnp.sum(row_weights, axis=1)]
    ppermute x0 -> x29, starting transfers between devices: none -> 43.5 us  [the longest x15 23.6 us: lse_over(): lax.ppermute(part, axis, [(i, i ^ step) for i in range(n)])]
    all_gather x2 -> x0, waiting for transfers between devices: 34.1 us -> none  [joined(): gathered = jax.tree.map(lambda a: lax.all_gather(a, axis), part)]
    ppermute x0 -> x29, waiting for transfers between devices: none -> 15.1 us  [the longest x15 7.24 us: lse_over(): lax.ppermute(part, axis, [(i, i ^ step) for i in range(n)])]
    add x72 -> x18, other arithmetic: 14.7 us -> 0.29 us  [the longest x15 0.22 us: merged(): return peak + jnp.log(jnp.exp(first - peak) + jnp.exp(second - peak))]
  transfers between devices with their start and end apart: 2 -> 29, of which waited for: 1 -> 9; matrix products, arithmetic and copies ran while one was open for 1% -> 0% of each run, Pallas kernels for 0% -> 0%
where the time goes in v1:
time: 238 us; the launch traced here: 237 us
  Pallas kernels  172 us (72%)
  starting transfers between devices  43.5 us (18%)
  waiting for transfers between devices  15.1 us (6%)
  local copies, waits for them, and re-layouts  3.7 us (2%)
    pallas_call x1, Pallas kernels, maps(): pl.pallas_call(functools.partial(maps_kernel, rows=512), out_shape=(vecto...  75.7 us
    pallas_call x2, Pallas kernels, sums(): pl.pallas_call(functools.partial(sums_kernel, rows=64), out_shape=(vector...  59.7 us
    pallas_call x1, Pallas kernels, form(): pl.pallas_call(functools.partial(form_kernel, rows=256), out_shape=(pltpu...  37 us
    ppermute x15, starting transfers between devices, lse_over(): lax.ppermute(part, axis, [(i, i ^ step) for i in range(n)])  23.6 us
    ppermute x6, starting transfers between devices, map_over(): lax.ppermute(piece(part, (place + k) % group, group), axis, pairs(k))  11.1 us
    ppermute x6, starting transfers between devices, gathered(): other = lax.ppermute(own, axis, pairs(k))  8.6 us
    ppermute x15, waiting for transfers between devices, lse_over(): lax.ppermute(part, axis, [(i, i ^ step) for i in range(n)])  7.24 us
  transfers between devices with their start and end apart: 29, of which 9 were waited for; matrix products, arithmetic and copies ran while one was open for 0% of the time, Pallas kernels for 0%

profile of v1, /device:TPU:0, one launch (start us, length us, event | category | flops | bytes accessed | tf_op | source)
XLA Modules:
  0.0 237.2 jit_solution(12943515559761173220)
XLA Ops:
  4.1 37.0 %form.1 = (f32[2048,2048]{1,0:T(8,128)S(1)}, f32[16,128]{1,0:T(8,128)S(1)}, f32[16,128]{1,0:T(8,128)S(1)}) custom-call(f32[64,2048]{1,0:T(8,128)S(1)} %copy-done.1, f32[64,2048]{1,0:T(8,128)S(1)} %copy-done.3, f32[16,128]{1,0:T(8,128)S(1)} %bitcast.18, f32[16,128]{1,0:T(8,128)S(1)} %bitcast.22), custom_call_target="tpu_custom_call" | custom-call | tf_op jit(solution)/shard_map/form/pallas_call | solution.py:325
  41.6 2.6 %collective-permute-start = (f32[16,128]{1,0:T(8,128)S(1)}, f32[16,128]{1,0:T(8,128)S(1)}, u32[]{:S(2)}, u32[]{:S(2)}) collective-permute-start(f32[16,128]{1,0:T(8,128)S(1)} %get-tuple-element.20), channel_id=1, source_target_pairs={{0,1},{1,0},{2,3},{3,2},{4,5},{5,4},{6,7},{7,6},{8,9},{9,8},{10,11... | collective-permute-start | bytes 24584 | tf_op jit(solution)/shard_map/ppermute | solution.py:400
  44.2 1.6 collective-permute-start.3
  45.8 2.1 collective-permute-start.1
  47.9 2.7 %collective-permute-start.4 = (f32[16,128]{1,0:T(8,128)S(1)}, f32[16,128]{1,0:T(8,128)S(1)}, u32[]{:S(2)}, u32[]{:S(2)}) collective-permute-start(f32[16,128]{1,0:T(8,128)S(1)} %log_add_fusion.11), channel_id=1, source_target_pairs={{0,16},{4,20},{8,24},{12,28},{16,0},{20,4},{24,8},{28,12},{1,17},{... | collective-permute-start | bytes 24584 | tf_op jit(solution)/shard_map/ppermute | solution.py:400
  50.6 1.9 collective-permute-done.4
  52.6 29.8 %sums.2 = (f32[16,128]{1,0:T(8,128)S(1)}, f32[16,128]{1,0:T(8,128)S(1)}, f32[16,128]{1,0:T(8,128)S(1)}, f32[16,128]{1,0:T(8,128)S(1)}) custom-call(f32[2048,2048]{1,0:T(8,128)S(1)} %get-tuple-element.19.k_ref, f32[64,2048]{1,0:T(8,128)S(1)} %copy-done.1, f32[64,2048]{1,0:T(8,128)S(1)} %copy-done.3, f32[16,128]{1,0:T(8,128)S(1)} %broadcast_1_f_ref_g_ref.2.f_ref.g_ref, ...), custom_call_target="tpu_custom_call" | custom-call | tf_op jit(solution)/shard_map/sums/pallas_call | solution.py:345
  84.1 1.6 collective-permute-start.8
  87.8 2.7 %collective-permute-start.9 = (f32[16,128]{1,0:T(8,128)S(1)}, f32[16,128]{1,0:T(8,128)S(1)}, u32[]{:S(2)}, u32[]{:S(2)}) collective-permute-start(f32[16,128]{1,0:T(8,128)S(1)} %log_add_fusion.6), channel_id=1, source_target_pairs={{0,16},{4,20},{8,24},{12,28},{16,0},{20,4},{24,8},{28,12},{1,17},{... | collective-permute-start | bytes 24584 | tf_op jit(solution)/shard_map/ppermute | solution.py:400
  90.5 1.9 collective-permute-done.9
  92.5 29.8 %sums.3 = (f32[16,128]{1,0:T(8,128)S(1)}, f32[16,128]{1,0:T(8,128)S(1)}, f32[16,128]{1,0:T(8,128)S(1)}, f32[16,128]{1,0:T(8,128)S(1)}) custom-call(f32[2048,2048]{1,0:T(8,128)S(1)} %get-tuple-element.19.k_ref, f32[64,2048]{1,0:T(8,128)S(1)} %copy-done.1, f32[64,2048]{1,0:T(8,128)S(1)} %copy-done.3, f32[16,128]{1,0:T(8,128)S(1)} %get-tuple-element.22.f_ref, ...), custom_call_target="tpu_custom_call" | custom-call | tf_op jit(solution)/shard_map/sums/pallas_call | solution.py:345
  123.6 1.6 collective-permute-start.13
  127.3 2.7 %collective-permute-start.14 = (f32[16,128]{1,0:T(8,128)S(1)}, f32[16,128]{1,0:T(8,128)S(1)}, u32[]{:S(2)}, u32[]{:S(2)}) collective-permute-start(f32[16,128]{1,0:T(8,128)S(1)} %log_add_fusion.1), channel_id=1, source_target_pairs={{0,16},{4,20},{8,24},{12,28},{16,0},{20,4},{24,8},{28,12},{1,17},{... | collective-permute-start | bytes 24584 | tf_op jit(solution)/shard_map/ppermute | solution.py:400
  130.0 1.9 collective-permute-done.14
  132.0 75.7 %maps.1 = (f32[16,128]{1,0:T(8,128)}, f32[16,128]{1,0:T(8,128)}, f32[72,2048]{1,0:T(8,128)S(1)}, f32[72,2048]{1,0:T(8,128)S(1)}) custom-call(f32[2048,2048]{1,0:T(8,128)} %copy-done, f32[64,2048]{1,0:T(8,128)S(1)} %copy-done.2, f32[64,2048]{1,0:T(8,128)S(1)} %copy-done.4, f32[16,128]{1,0:T(8,128)S(1)} %get-tuple-element.26.f_ref, ...), custom_call_target="tpu_custom_call" | custom-call | tf_op jit(solution)/shard_map/maps/pallas_call | solution.py:365
  210.4 1.9 collective-permute-start.17
  212.4 1.6 collective-permute-start.22
  214.0 2.6 %collective-permute-start.23 = (f32[72,256]{1,0:T(8,128)S(1)}, f32[72,256]{1,0:T(8,128)S(1)}, u32[]{:S(2)}, u32[]{:S(2)}) collective-permute-start(f32[72,256]{1,0:T(8,128)S(1)} %get-tuple-element.57), channel_id=1, source_target_pairs={{0,16},{4,20},{8,24},{12,28},{16,0},{20,4},{24,8},{28,12},{1,17},{... | collective-permute-start | bytes 221192 | tf_op jit(solution)/shard_map/ppermute | solution.py:430
  216.6 2.8 %collective-permute-start.24 = (f32[72,256]{1,0:T(8,128)S(1)}, f32[72,256]{1,0:T(8,128)S(1)}, u32[]{:S(2)}, u32[]{:S(2)}) collective-permute-start(f32[72,256]{1,0:T(8,128)S(1)} %get-tuple-element.58), channel_id=1, source_target_pairs={{0,24},{4,28},{8,0},{12,4},{16,8},{20,12},{24,16},{28,20},{1,25},{... | collective-permute-start | bytes 221192 | tf_op jit(solution)/shard_map/ppermute | solution.py:430
  219.5 2.2 collective-permute-done.23
  224.5 2.7 %collective-permute-start.20 = (f32[64,512]{1,0:T(8,128)S(1)}, f32[64,512]{1,0:T(8,128)S(1)}, u32[]{:S(2)}, u32[]{:S(2)}) collective-permute-start(f32[64,512]{1,0:T(8,128)S(1)} %get-tuple-element.46), channel_id=1, source_target_pairs={{0,3},{1,0},{2,1},{3,2},{4,7},{5,4},{6,5},{7,6},{8,11},{9,8},{10,9... | collective-permute-start | bytes 393224 | tf_op jit(solution)/shard_map/ppermute | solution.py:440
  227.3 3.2 %collective-permute-start.26 = (f32[64,256]{1,0:T(8,128)S(1)}, f32[64,256]{1,0:T(8,128)S(1)}, u32[]{:S(2)}, u32[]{:S(2)}) collective-permute-start(f32[64,256]{1,0:T(8,128)S(1)} %get-tuple-element.35), channel_id=1, source_target_pairs={{0,16},{4,20},{8,24},{12,28},{16,0},{20,4},{24,8},{28,12},{1,17},{... | collective-permute-start | bytes 196616 | tf_op jit(solution)/shard_map/ppermute | solution.py:440
  230.5 2.5 %collective-permute-done.26 = f32[64,256]{1,0:T(8,128)S(1)} collective-permute-done((f32[64,256]{1,0:T(8,128)S(1)}, f32[64,256]{1,0:T(8,128)S(1)}, u32[]{:S(2)}, u32[]{:S(2)}) %collective-permute-start.26) | collective-permute-done | bytes 65568 | tf_op jit(solution)/shard_map/ppermute | solution.py:440
  233.0 1.8 collective-permute-done.27
  (93 shorter events, 18.9 us)
Async XLA Ops:
  41.6 4.2 %collective-permute-start = (f32[16,128]{1,0:T(8,128)S(1)}, f32[16,128]{1,0:T(8,128)S(1)}, u32[]{:S(2)}, u32[]{:S(2)}) collective-permute-start(f32[16,128]{1,0:T(8,128)S(1)} %get-tuple-element.20), channel_id=1, source_target_pairs={{0,1},{1,0},{2,3},{3,2},{4,5},{5,4},{6,7},{7,6},{8,9},{9,8},{10,11... | collective-permute-start | bytes 24584 | tf_op jit(solution)/shard_map/ppermute | solution.py:400
  44.2 3.7 %collective-permute-start.3 = (f32[16,128]{1,0:T(8,128)S(1)}, f32[16,128]{1,0:T(8,128)S(1)}, u32[]{:S(2)}, u32[]{:S(2)}) collective-permute-start(f32[16,128]{1,0:T(8,128)S(1)} %log_add_fusion.12), channel_id=1, source_target_pairs={{0,8},{4,12},{8,0},{12,4},{16,24},{20,28},{24,16},{28,20},{1,9},{5... | collective-permute-start | bytes 24584 | tf_op jit(solution)/shard_map/ppermute | solution.py:400
  45.8 4.8 %collective-permute-start.1 = (f32[16,128]{1,0:T(8,128)S(1)}, f32[16,128]{1,0:T(8,128)S(1)}, u32[]{:S(2)}, u32[]{:S(2)}) collective-permute-start(f32[16,128]{1,0:T(8,128)S(1)} %log_add_fusion.14), channel_id=1, source_target_pairs={{0,2},{1,3},{2,0},{3,1},{4,6},{5,7},{6,4},{7,5},{8,10},{9,11},{10,... | collective-permute-start | bytes 24584 | tf_op jit(solution)/shard_map/ppermute | solution.py:400
  47.9 4.6 %collective-permute-start.4 = (f32[16,128]{1,0:T(8,128)S(1)}, f32[16,128]{1,0:T(8,128)S(1)}, u32[]{:S(2)}, u32[]{:S(2)}) collective-permute-start(f32[16,128]{1,0:T(8,128)S(1)} %log_add_fusion.11), channel_id=1, source_target_pairs={{0,16},{4,20},{8,24},{12,28},{16,0},{20,4},{24,8},{28,12},{1,17},{... | collective-permute-start | bytes 24584 | tf_op jit(solution)/shard_map/ppermute | solution.py:400
  82.5 3.7 %collective-permute-start.5 = (f32[16,128]{1,0:T(8,128)S(1)}, f32[16,128]{1,0:T(8,128)S(1)}, u32[]{:S(2)}, u32[]{:S(2)}) collective-permute-start(f32[16,128]{1,0:T(8,128)S(1)} %get-tuple-element.24), channel_id=1, source_target_pairs={{0,1},{1,0},{2,3},{3,2},{4,5},{5,4},{6,7},{7,6},{8,9},{9,8},{10,11... | collective-permute-start | bytes 24584 | tf_op jit(solution)/shard_map/ppermute | solution.py:400
  84.1 3.7 %collective-permute-start.8 = (f32[16,128]{1,0:T(8,128)S(1)}, f32[16,128]{1,0:T(8,128)S(1)}, u32[]{:S(2)}, u32[]{:S(2)}) collective-permute-start(f32[16,128]{1,0:T(8,128)S(1)} %log_add_fusion.7), channel_id=1, source_target_pairs={{0,8},{4,12},{8,0},{12,4},{16,24},{20,28},{24,16},{28,20},{1,9},{5... | collective-permute-start | bytes 24584 | tf_op jit(solution)/shard_map/ppermute | solution.py:400
  86.3 4.2 %collective-permute-start.6 = (f32[16,128]{1,0:T(8,128)S(1)}, f32[16,128]{1,0:T(8,128)S(1)}, u32[]{:S(2)}, u32[]{:S(2)}) collective-permute-start(f32[16,128]{1,0:T(8,128)S(1)} %log_add_fusion.9), channel_id=1, source_target_pairs={{0,2},{1,3},{2,0},{3,1},{4,6},{5,7},{6,4},{7,5},{8,10},{9,11},{10,... | collective-permute-start | bytes 24584 | tf_op jit(solution)/shard_map/ppermute | solution.py:400
  87.8 4.6 %collective-permute-start.9 = (f32[16,128]{1,0:T(8,128)S(1)}, f32[16,128]{1,0:T(8,128)S(1)}, u32[]{:S(2)}, u32[]{:S(2)}) collective-permute-start(f32[16,128]{1,0:T(8,128)S(1)} %log_add_fusion.6), channel_id=1, source_target_pairs={{0,16},{4,20},{8,24},{12,28},{16,0},{20,4},{24,8},{28,12},{1,17},{... | collective-permute-start | bytes 24584 | tf_op jit(solution)/shard_map/ppermute | solution.py:400
  122.4 3.7 %collective-permute-start.10 = (f32[16,128]{1,0:T(8,128)S(1)}, f32[16,128]{1,0:T(8,128)S(1)}, u32[]{:S(2)}, u32[]{:S(2)}) collective-permute-start(f32[16,128]{1,0:T(8,128)S(1)} %get-tuple-element.28), channel_id=1, source_target_pairs={{0,1},{1,0},{2,3},{3,2},{4,5},{5,4},{6,7},{7,6},{8,9},{9,8},{10,11... | collective-permute-start | bytes 24584 | tf_op jit(solution)/shard_map/ppermute | solution.py:400
  126.1 3.8 %collective-permute-start.11 = (f32[16,128]{1,0:T(8,128)S(1)}, f32[16,128]{1,0:T(8,128)S(1)}, u32[]{:S(2)}, u32[]{:S(2)}) collective-permute-start(f32[16,128]{1,0:T(8,128)S(1)} %log_add_fusion.4), channel_id=1, source_target_pairs={{0,2},{1,3},{2,0},{3,1},{4,6},{5,7},{6,4},{7,5},{8,10},{9,11},{10,... | collective-permute-start | bytes 24584 | tf_op jit(solution)/shard_map/ppermute | solution.py:400
  127.3 4.6 %collective-permute-start.14 = (f32[16,128]{1,0:T(8,128)S(1)}, f32[16,128]{1,0:T(8,128)S(1)}, u32[]{:S(2)}, u32[]{:S(2)}) collective-permute-start(f32[16,128]{1,0:T(8,128)S(1)} %log_add_fusion.1), channel_id=1, source_target_pairs={{0,16},{4,20},{8,24},{12,28},{16,0},{20,4},{24,8},{28,12},{1,17},{... | collective-permute-start | bytes 24584 | tf_op jit(solution)/shard_map/ppermute | solution.py:400
  207.7 4.5 %collective-permute-start.21 = (f32[72,1024]{1,0:T(8,128)S(1)}, f32[72,1024]{1,0:T(8,128)S(1)}, u32[]{:S(2)}, u32[]{:S(2)}) collective-permute-start(f32[72,1024]{1,0:T(8,128)S(1)} %constant_dynamic-slice_fusion), channel_id=1, source_target_pairs={{0,4},{4,0},{8,12},{12,8},{16,20},{20,16},{24,28},{28,24},{1,5},{5... | collective-permute-start | bytes 884744 | tf_op jit(solution)/shard_map/ppermute | solution.py:463
  208.2 8.4 %collective-permute-start.15 = (f32[72,512]{1,0:T(8,128)S(1)}, f32[72,512]{1,0:T(8,128)S(1)}, u32[]{:S(2)}, u32[]{:S(2)}) collective-permute-start(f32[72,512]{1,0:T(8,128)S(1)} %get-tuple-element.52), channel_id=1, source_target_pairs={{0,1},{1,2},{2,3},{3,0},{4,5},{5,6},{6,7},{7,4},{8,9},{9,10},{10,1... | collective-permute-start | bytes 442376 | tf_op jit(solution)/shard_map/ppermute | solution.py:430
  209.3 10.2 %collective-permute-start.16 = (f32[72,512]{1,0:T(8,128)S(1)}, f32[72,512]{1,0:T(8,128)S(1)}, u32[]{:S(2)}, u32[]{:S(2)}) collective-permute-start(f32[72,512]{1,0:T(8,128)S(1)} %get-tuple-element.54), channel_id=1, source_target_pairs={{0,2},{1,3},{2,0},{3,1},{4,6},{5,7},{6,4},{7,5},{8,10},{9,11},{10,... | collective-permute-start | bytes 442376 | tf_op jit(solution)/shard_map/ppermute | solution.py:430
  210.4 9.1 %collective-permute-start.17 = (f32[72,512]{1,0:T(8,128)S(1)}, f32[72,512]{1,0:T(8,128)S(1)}, u32[]{:S(2)}, u32[]{:S(2)}) collective-permute-start(f32[72,512]{1,0:T(8,128)S(1)} %get-tuple-element.53), channel_id=1, source_target_pairs={{0,3},{1,0},{2,1},{3,2},{4,7},{5,4},{6,5},{7,6},{8,11},{9,8},{10,9... | collective-permute-start | bytes 442376 | tf_op jit(solution)/shard_map/ppermute | solution.py:430
  212.4 7.1 %collective-permute-start.22 = (f32[72,256]{1,0:T(8,128)S(1)}, f32[72,256]{1,0:T(8,128)S(1)}, u32[]{:S(2)}, u32[]{:S(2)}) collective-permute-start(f32[72,256]{1,0:T(8,128)S(1)} %get-tuple-element.56), channel_id=1, source_target_pairs={{0,8},{4,12},{8,16},{12,20},{16,24},{20,28},{24,0},{28,4},{1,9},{5... | collective-permute-start | bytes 221192 | tf_op jit(solution)/shard_map/ppermute | solution.py:430
  214.0 7.7 %collective-permute-start.23 = (f32[72,256]{1,0:T(8,128)S(1)}, f32[72,256]{1,0:T(8,128)S(1)}, u32[]{:S(2)}, u32[]{:S(2)}) collective-permute-start(f32[72,256]{1,0:T(8,128)S(1)} %get-tuple-element.57), channel_id=1, source_target_pairs={{0,16},{4,20},{8,24},{12,28},{16,0},{20,4},{24,8},{28,12},{1,17},{... | collective-permute-start | bytes 221192 | tf_op jit(solution)/shard_map/ppermute | solution.py:430
  216.6 5.1 %collective-permute-start.24 = (f32[72,256]{1,0:T(8,128)S(1)}, f32[72,256]{1,0:T(8,128)S(1)}, u32[]{:S(2)}, u32[]{:S(2)}) collective-permute-start(f32[72,256]{1,0:T(8,128)S(1)} %get-tuple-element.58), channel_id=1, source_target_pairs={{0,24},{4,28},{8,0},{12,4},{16,8},{20,12},{24,16},{28,20},{1,25},{... | collective-permute-start | bytes 221192 | tf_op jit(solution)/shard_map/ppermute | solution.py:430
  221.8 8.7 %collective-permute-start.25 = (f32[64,256]{1,0:T(8,128)S(1)}, f32[64,256]{1,0:T(8,128)S(1)}, u32[]{:S(2)}, u32[]{:S(2)}) collective-permute-start(f32[64,256]{1,0:T(8,128)S(1)} %get-tuple-element.35), channel_id=1, source_target_pairs={{0,8},{4,12},{8,16},{12,20},{16,24},{20,28},{24,0},{28,4},{1,9},{5... | collective-permute-start | bytes 196616 | tf_op jit(solution)/shard_map/ppermute | solution.py:440
  223.4 11.5 %collective-permute-start.18 = (f32[64,512]{1,0:T(8,128)S(1)}, f32[64,512]{1,0:T(8,128)S(1)}, u32[]{:S(2)}, u32[]{:S(2)}) collective-permute-start(f32[64,512]{1,0:T(8,128)S(1)} %get-tuple-element.46), channel_id=1, source_target_pairs={{0,1},{1,2},{2,3},{3,0},{4,5},{5,6},{6,7},{7,4},{8,9},{9,10},{10,1... | collective-permute-start | bytes 393224 | tf_op jit(solution)/shard_map/ppermute | solution.py:440
  223.6 11.3 %collective-permute-start.19 = (f32[64,512]{1,0:T(8,128)S(1)}, f32[64,512]{1,0:T(8,128)S(1)}, u32[]{:S(2)}, u32[]{:S(2)}) collective-permute-start(f32[64,512]{1,0:T(8,128)S(1)} %get-tuple-element.46), channel_id=1, source_target_pairs={{0,2},{1,3},{2,0},{3,1},{4,6},{5,7},{6,4},{7,5},{8,10},{9,11},{10,... | collective-permute-start | bytes 393224 | tf_op jit(solution)/shard_map/ppermute | solution.py:440
  224.5 10.4 %collective-permute-start.20 = (f32[64,512]{1,0:T(8,128)S(1)}, f32[64,512]{1,0:T(8,128)S(1)}, u32[]{:S(2)}, u32[]{:S(2)}) collective-permute-start(f32[64,512]{1,0:T(8,128)S(1)} %get-tuple-element.46), channel_id=1, source_target_pairs={{0,3},{1,0},{2,1},{3,2},{4,7},{5,4},{6,5},{7,6},{8,11},{9,8},{10,9... | collective-permute-start | bytes 393224 | tf_op jit(solution)/shard_map/ppermute | solution.py:440
  227.3 5.7 %collective-permute-start.26 = (f32[64,256]{1,0:T(8,128)S(1)}, f32[64,256]{1,0:T(8,128)S(1)}, u32[]{:S(2)}, u32[]{:S(2)}) collective-permute-start(f32[64,256]{1,0:T(8,128)S(1)} %get-tuple-element.35), channel_id=1, source_target_pairs={{0,16},{4,20},{8,24},{12,28},{16,0},{20,4},{24,8},{28,12},{1,17},{... | collective-permute-start | bytes 196616 | tf_op jit(solution)/shard_map/ppermute | solution.py:440
  230.5 4.3 %collective-permute-start.27 = (f32[64,256]{1,0:T(8,128)S(1)}, f32[64,256]{1,0:T(8,128)S(1)}, u32[]{:S(2)}, u32[]{:S(2)}) collective-permute-start(f32[64,256]{1,0:T(8,128)S(1)} %get-tuple-element.35), channel_id=1, source_target_pairs={{0,24},{4,28},{8,0},{12,4},{16,8},{20,12},{24,16},{28,20},{1,25},{... | collective-permute-start | bytes 196616 | tf_op jit(solution)/shard_map/ppermute | solution.py:440
  (15 other events, 415.7 us)

commit v2 on v1

--- a/solution.py
+++ b/solution.py
@@ -197,7 +197,7 @@
 
 def sums_kernel(
     k_ref, x_ref, y_ref, f_ref, g_ref, rl_ref, cl_ref, a_ref, b_ref,
-    fn_ref, gn_ref, row_ref, col_ref, ub, acc, vs, r_s, t_s, *, rows,
+    kept_ref, fn_ref, gn_ref, row_ref, col_ref, ub, acc, vs, r_s, t_s, *, rows,
 ):
     update(f_ref, rl_ref, a_ref, fn_ref, r_s)
     update(g_ref, cl_ref, b_ref, gn_ref, t_s)
@@ -308,7 +308,7 @@
 
 
 VM = pl.BlockSpec(memory_space=pltpu.VMEM)
-PARAMS = pltpu.CompilerParams(vmem_limit_bytes=36 * 2**20)
+PARAMS = pltpu.CompilerParams(vmem_limit_bytes=24 * 2**20)
 
 
 def vector(n):
@@ -344,9 +344,10 @@
     ns, nt = k.shape
     return pl.pallas_call(
         functools.partial(sums_kernel, rows=64),
-        out_shape=(vector(ns), vector(nt), vector(ns), vector(nt)),
+        out_shape=(pltpu.VMEM((ns, nt), F32), vector(ns), vector(nt), vector(ns), vector(nt)),
         in_specs=[VM] * 9,
-        out_specs=(VM,) * 4,
+        out_specs=(VM,) * 5,
+        input_output_aliases={0: 0},
         scratch_shapes=[
             pltpu.VMEM((ns, LANES), F32),
             pltpu.VMEM((ns, LANES), F32),
@@ -395,10 +396,10 @@
 
 def lse_over(axis, part):
     n = lax.axis_size(axis)
-    step = 1
-    while step < n:
+    step = n // 2
+    while step:
         part = merged(part, lax.ppermute(part, axis, [(i, i ^ step) for i in range(n)]))
-        step *= 2
+        step //= 2
     return part
 
 
@@ -410,39 +411,52 @@
     return sum(p[:d] * w for p, w in zip(parts, weights)) / total, peak + jnp.log(total)
 
 
-def piece(a, index, count):
-    width = a.shape[1] // count
-    return lax.dynamic_slice_in_dim(a, index * width, width, 1)
-
-
-def map_over(axis, group, stride, part):
-    n = lax.axis_size(axis)
-    me = lax.axis_index(axis)
-    place = (me // stride) % group
-
-    def pairs(k):
-        return [
-            (i, i + (((i // stride) + k) % group - (i // stride) % group) * stride) for i in range(n)
-        ]
-
-    got = [piece(part, place, group)]
+def pairs(n, group, stride, k):
+    return [(i, i + (((i // stride) + k) % group - (i // stride) % group) * stride) for i in range(n)]
+
+
+def places(index, group, stride, width):
+    own = (index // stride) % group
+    return [(own + k) % group * width for k in range(group)]
+
+
+def piece(a, at, count):
+    zero = jnp.zeros((), at.dtype)
+    return lax.dynamic_slice(
+        a, (zero, at), (a.shape[0], a.shape[1] // count), allow_negative_indices=False
+    )
+
+
+def put(a, part, at):
+    zero = jnp.zeros((), at.dtype)
+    return lax.dynamic_update_slice(a, part, (zero, at), allow_negative_indices=False)
+
+
+def map_over(axis, place, stride, part):
+    n, group = lax.axis_size(axis), len(place)
+    got = [piece(part, place[0], group)]
     for k in range(1, group):
-        got.append(lax.ppermute(piece(part, (place + k) % group, group), axis, pairs(k)))
+        got.append(lax.ppermute(piece(part, place[k], group), axis, pairs(n, group, stride, k)))
     own, _ = weighed(got)
-    return gathered(axis, group, pairs, place, own)
-
-
-def gathered(axis, group, pairs, place, own):
     width = own.shape[1]
     out = jnp.zeros((own.shape[0], width * group), F32)
-    out = lax.dynamic_update_slice_in_dim(out, own, place * width, 1)
+    out = put(out, own, place[0])
     for k in range(1, group):
-        other = lax.ppermute(own, axis, pairs(k))
-        out = lax.dynamic_update_slice_in_dim(out, other, ((place - k) % group) * width, 1)
+        other = lax.ppermute(own, axis, pairs(n, group, stride, k))
+        out = put(out, other, place[-k])
     return out
 
 
 def body(sources, targets, source_mass, target_mass):
+    rows, cols = lax.axis_size("row"), lax.axis_size("col")
+    index = lax.axis_index("row")
+    ns, nt = sources.shape[1], targets.shape[1]
+    halves = places(index, 2, 1, nt // 2)
+    row_places = places(index, rows // 2, 2, nt // rows)
+    col_places = places(lax.axis_index("col"), cols, 1, ns // cols)
+    sources, halves, row_places, col_places = lax.optimization_barrier(
+        (sources, halves, row_places, col_places)
+    )
     a = source_mass.reshape(-1, LANES)
     b = target_mass.reshape(-1, LANES)
     f = jnp.zeros_like(a)
@@ -452,23 +466,20 @@
         col_lse = lse_over("row", col_part)
         row_lse = lse_over("col", row_part)
         if sweep < ITERS - 1:
-            f, g, row_part, col_part = sums(k, sources, targets, f, g, row_lse, col_lse, a, b)
+            k, f, g, row_part, col_part = sums(k, sources, targets, f, g, row_lse, col_lse, a, b)
         else:
             f, g, row_map, col_map = maps(k, sources, targets, f, g, row_lse, col_lse, a, b)
-    rows = lax.axis_size("row")
-    me = lax.axis_index("row")
-    half = me % 2
-    pair = [(i, i ^ 1) for i in range(rows)]
-    mine = piece(col_map, half, 2)
-    other = lax.ppermute(piece(col_map, 1 - half, 2), "row", pair)
+    pair = pairs(rows, 2, 1, 1)
+    mine = piece(col_map, halves[0], 2)
+    other = lax.ppermute(piece(col_map, halves[1], 2), "row", pair)
     values, lse = weighed([mine, other])
     chip = jnp.concatenate([values, jnp.broadcast_to(lse, (8, lse.shape[1]))], axis=0)
-    ours = map_over("row", rows // 2, 2, chip)
+    ours = map_over("row", row_places, 2, chip)
     theirs = lax.ppermute(ours, "row", pair)
     target_map = jnp.where(
-        half == 0, jnp.concatenate([ours, theirs], axis=1), jnp.concatenate([theirs, ours], axis=1)
+        halves[0] == 0, jnp.concatenate([ours, theirs], axis=1), jnp.concatenate([theirs, ours], axis=1)
     )
-    source_map = map_over("col", lax.axis_size("col"), 1, row_map)
+    source_map = map_over("col", col_places, 1, row_map)
     return f.reshape(-1), g.reshape(-1), source_map, target_map
 
 

time: 238 us -> 238 us (level)
  local copies, waits for them, and re-layouts: 3.7 us -> 10.6 us
  Pallas kernels: 172 us -> 167 us
    dynamic_update_slice x6 -> x8, local copies, waits for them, and re-layouts: 0.07 us -> 6.08 us  [put(): lax.dynamic_update_slice(a, part, (zero, at), allow_negative_indices=False)]
    pallas_call x1, Pallas kernels: 75.7 us -> 70 us  [maps(): pl.pallas_call(functools.partial(maps_kernel, rows=512), out_shape=(vecto...]
  transfers between devices with their start and end apart: 29 -> 29, of which waited for: 9 -> 17; matrix products, arithmetic and copies ran while one was open for 0% -> 3% of each run, Pallas kernels for 0% -> 0%
where the time goes in v2:
time: 238 us
  Pallas kernels  167 us (70%)
  starting transfers between devices  41.6 us (17%)
  waiting for transfers between devices  15.7 us (7%)
  local copies, waits for them, and re-layouts  10.6 us (4%)
    pallas_call x1, Pallas kernels, maps(): pl.pallas_call(functools.partial(maps_kernel, rows=512), out_shape=(vecto...  70 us
    pallas_call x2, Pallas kernels, sums(): pl.pallas_call(functools.partial(sums_kernel, rows=64), out_shape=(pltpu....  59.7 us
    pallas_call x1, Pallas kernels, form(): pl.pallas_call(functools.partial(form_kernel, rows=256), out_shape=(pltpu...  37 us
    ppermute x15, starting transfers between devices, lse_over(): lax.ppermute(part, axis, [(i, i ^ step) for i in range(n)])  23.1 us
    ppermute x6, starting transfers between devices, map_over(): lax.ppermute(piece(part, place[k], group), axis, pairs(n, group, stride, k))  9.59 us
    ppermute x6, starting transfers between devices, map_over(): other = lax.ppermute(own, axis, pairs(n, group, stride, k))  8.57 us
    ppermute x15, waiting for transfers between devices, lse_over(): lax.ppermute(part, axis, [(i, i ^ step) for i in range(n)])  7.75 us
    dynamic_update_slice x8, local copies, waits for them, and re-layouts, put(): lax.dynamic_update_slice(a, part, (zero, at), allow_negative_indices=False)  6.08 us
  transfers between devices with their start and end apart: 29, of which 17 were waited for; matrix products, arithmetic and copies ran while one was open for 3% of the time, Pallas kernels for 0%

profile of v2, /device:TPU:0, one launch (start us, length us, event | category | flops | bytes accessed | tf_op | source)
XLA Modules:
  0.0 237.5 jit_solution(8791872069070751195)
XLA Ops:
  4.3 37.0 %form.1 = (f32[2048,2048]{1,0:T(8,128)S(1)}, f32[16,128]{1,0:T(8,128)S(1)}, f32[16,128]{1,0:T(8,128)S(1)}) custom-call(f32[64,2048]{1,0:T(8,128)S(1)} %copy-done, f32[64,2048]{1,0:T(8,128)S(1)} %copy-done.1, f32[16,128]{1,0:T(8,128)S(1)} %bitcast.18, f32[16,128]{1,0:T(8,128)S(1)} %bitcast.22), custom_call_target="tpu_custom_call" | custom-call | tf_op jit(solution)/shard_map/form/pallas_call | solution.py:325
  41.3 4.1 %collective-permute-start.2 = (f32[16,128]{1,0:T(8,128)S(1)}, f32[16,128]{1,0:T(8,128)S(1)}, u32[]{:S(2)}, u32[]{:S(2)}) collective-permute-start(f32[16,128]{1,0:T(8,128)S(1)} %get-tuple-element.35), channel_id=1, source_target_pairs={{0,16},{4,20},{8,24},{12,28},{16,0},{20,4},{24,8},{28,12},{1,17},{... | collective-permute-start | bytes 24584 | tf_op jit(solution)/shard_map/ppermute | solution.py:401
  47.0 2.0 collective-permute-start.3
  49.0 1.6 collective-permute-start.1
  50.8 1.9 collective-permute-done.1
  53.5 29.8 %sums.2 = (f32[2048,2048]{1,0:T(8,128)S(1)}, f32[16,128]{1,0:T(8,128)S(1)}, f32[16,128]{1,0:T(8,128)S(1)}, f32[16,128]{1,0:T(8,128)S(1)}, f32[16,128]{1,0:T(8,128)S(1)}) custom-call(f32[2048,2048]{1,0:T(8,128)S(1)} %get-tuple-element.33.k_ref, f32[64,2048]{1,0:T(8,128)S(1)} %copy-done, f32[64,2048]{1,0:T(8,128)S(1)} %copy-done.1, ...), custom_call_target="tpu_custom_call", output_to_operand_aliasing={{0}: (0, {})} | custom-call | tf_op jit(solution)/shard_map/sums/pallas_call | solution.py:345
  83.3 2.6 %collective-permute-start.7 = (f32[16,128]{1,0:T(8,128)S(1)}, f32[16,128]{1,0:T(8,128)S(1)}, u32[]{:S(2)}, u32[]{:S(2)}) collective-permute-start(f32[16,128]{1,0:T(8,128)S(1)} %get-tuple-element.40), channel_id=1, source_target_pairs={{0,16},{4,20},{8,24},{12,28},{16,0},{20,4},{24,8},{28,12},{1,17},{... | collective-permute-start | bytes 24584 | tf_op jit(solution)/shard_map/ppermute | solution.py:401
  88.0 1.6 collective-permute-start.8
  89.6 1.6 collective-permute-start.6
  91.8 1.6 collective-permute-done.6
  93.4 29.8 %sums.3 = (f32[2048,2048]{1,0:T(8,128)S(1)}, f32[16,128]{1,0:T(8,128)S(1)}, f32[16,128]{1,0:T(8,128)S(1)}, f32[16,128]{1,0:T(8,128)S(1)}, f32[16,128]{1,0:T(8,128)S(1)}) custom-call(f32[2048,2048]{1,0:T(8,128)S(1)} %get-tuple-element.36.k_ref, f32[64,2048]{1,0:T(8,128)S(1)} %copy-done, f32[64,2048]{1,0:T(8,128)S(1)} %copy-done.1, ...), custom_call_target="tpu_custom_call", output_to_operand_aliasing={{0}: (0, {})} | custom-call | tf_op jit(solution)/shard_map/sums/pallas_call | solution.py:345
  123.2 2.2 collective-permute-start.12
  129.1 1.6 collective-permute-start.11
  132.8 70.0 %maps.1 = (f32[16,128]{1,0:T(8,128)}, f32[16,128]{1,0:T(8,128)}, f32[72,2048]{1,0:T(8,128)S(1)}, f32[72,2048]{1,0:T(8,128)S(1)}) custom-call(f32[2048,2048]{1,0:T(8,128)S(1)} %get-tuple-element.41.k_ref, f32[64,2048]{1,0:T(8,128)S(1)} %copy-done, f32[64,2048]{1,0:T(8,128)S(1)} %copy-done.1, f32[16,128]{1,0:T(8,128)S(1)} %get-tuple-element.42.f_ref, ...), custom_call_target="tpu_custom_call" | custom-call | tf_op jit(solution)/shard_map/maps/pallas_call | solution.py:366
  206.3 2.1 collective-permute-start.23
  208.4 1.8 collective-permute-start.24
  210.4 1.5 collective-permute-start.15
  211.9 1.5 collective-permute-start.16
  214.9 1.7 collective-permute-start.25
  221.6 1.6 collective-permute-done.26
  224.7 1.5 collective-permute-start.18
  226.2 1.5 collective-permute-start.19
  230.3 1.7 collective-permute-done.18
  232.6 1.8 collective-permute-done.19
  (89 shorter events, 32.3 us)
Async XLA Ops:
  41.3 5.7 %collective-permute-start.2 = (f32[16,128]{1,0:T(8,128)S(1)}, f32[16,128]{1,0:T(8,128)S(1)}, u32[]{:S(2)}, u32[]{:S(2)}) collective-permute-start(f32[16,128]{1,0:T(8,128)S(1)} %get-tuple-element.35), channel_id=1, source_target_pairs={{0,16},{4,20},{8,24},{12,28},{16,0},{20,4},{24,8},{28,12},{1,17},{... | collective-permute-start | bytes 24584 | tf_op jit(solution)/shard_map/ppermute | solution.py:401
  47.0 3.7 %collective-permute-start.3 = (f32[16,128]{1,0:T(8,128)S(1)}, f32[16,128]{1,0:T(8,128)S(1)}, u32[]{:S(2)}, u32[]{:S(2)}) collective-permute-start(f32[16,128]{1,0:T(8,128)S(1)} %log_add_fusion.12), channel_id=1, source_target_pairs={{0,8},{4,12},{8,0},{12,4},{16,24},{20,28},{24,16},{28,20},{1,9},{5... | collective-permute-start | bytes 24584 | tf_op jit(solution)/shard_map/ppermute | solution.py:401
  49.0 3.7 %collective-permute-start.1 = (f32[16,128]{1,0:T(8,128)S(1)}, f32[16,128]{1,0:T(8,128)S(1)}, u32[]{:S(2)}, u32[]{:S(2)}) collective-permute-start(f32[16,128]{1,0:T(8,128)S(1)} %log_add_fusion.14), channel_id=1, source_target_pairs={{0,1},{1,0},{2,3},{3,2},{4,5},{5,4},{6,7},{7,6},{8,9},{9,8},{10,11... | collective-permute-start | bytes 24584 | tf_op jit(solution)/shard_map/ppermute | solution.py:401
  83.3 4.6 %collective-permute-start.7 = (f32[16,128]{1,0:T(8,128)S(1)}, f32[16,128]{1,0:T(8,128)S(1)}, u32[]{:S(2)}, u32[]{:S(2)}) collective-permute-start(f32[16,128]{1,0:T(8,128)S(1)} %get-tuple-element.40), channel_id=1, source_target_pairs={{0,16},{4,20},{8,24},{12,28},{16,0},{20,4},{24,8},{28,12},{1,17},{... | collective-permute-start | bytes 24584 | tf_op jit(solution)/shard_map/ppermute | solution.py:401
  85.9 3.7 %collective-permute-start.5 = (f32[16,128]{1,0:T(8,128)S(1)}, f32[16,128]{1,0:T(8,128)S(1)}, u32[]{:S(2)}, u32[]{:S(2)}) collective-permute-start(f32[16,128]{1,0:T(8,128)S(1)} %get-tuple-element.39), channel_id=1, source_target_pairs={{0,2},{1,3},{2,0},{3,1},{4,6},{5,7},{6,4},{7,5},{8,10},{9,11},{10,... | collective-permute-start | bytes 24584 | tf_op jit(solution)/shard_map/ppermute | solution.py:401
  88.0 3.7 %collective-permute-start.8 = (f32[16,128]{1,0:T(8,128)S(1)}, f32[16,128]{1,0:T(8,128)S(1)}, u32[]{:S(2)}, u32[]{:S(2)}) collective-permute-start(f32[16,128]{1,0:T(8,128)S(1)} %log_add_fusion.7), channel_id=1, source_target_pairs={{0,8},{4,12},{8,0},{12,4},{16,24},{20,28},{24,16},{28,20},{1,9},{5... | collective-permute-start | bytes 24584 | tf_op jit(solution)/shard_map/ppermute | solution.py:401
  89.6 3.7 %collective-permute-start.6 = (f32[16,128]{1,0:T(8,128)S(1)}, f32[16,128]{1,0:T(8,128)S(1)}, u32[]{:S(2)}, u32[]{:S(2)}) collective-permute-start(f32[16,128]{1,0:T(8,128)S(1)} %log_add_fusion.9), channel_id=1, source_target_pairs={{0,1},{1,0},{2,3},{3,2},{4,5},{5,4},{6,7},{7,6},{8,9},{9,8},{10,11... | collective-permute-start | bytes 24584 | tf_op jit(solution)/shard_map/ppermute | solution.py:401
  123.2 4.6 %collective-permute-start.12 = (f32[16,128]{1,0:T(8,128)S(1)}, f32[16,128]{1,0:T(8,128)S(1)}, u32[]{:S(2)}, u32[]{:S(2)}) collective-permute-start(f32[16,128]{1,0:T(8,128)S(1)} %get-tuple-element.45), channel_id=1, source_target_pairs={{0,16},{4,20},{8,24},{12,28},{16,0},{20,4},{24,8},{28,12},{1,17},{... | collective-permute-start | bytes 24584 | tf_op jit(solution)/shard_map/ppermute | solution.py:401
  125.4 3.7 %collective-permute-start.10 = (f32[16,128]{1,0:T(8,128)S(1)}, f32[16,128]{1,0:T(8,128)S(1)}, u32[]{:S(2)}, u32[]{:S(2)}) collective-permute-start(f32[16,128]{1,0:T(8,128)S(1)} %get-tuple-element.44), channel_id=1, source_target_pairs={{0,2},{1,3},{2,0},{3,1},{4,6},{5,7},{6,4},{7,5},{8,10},{9,11},{10,... | collective-permute-start | bytes 24584 | tf_op jit(solution)/shard_map/ppermute | solution.py:401
  127.8 3.7 %collective-permute-start.13 = (f32[16,128]{1,0:T(8,128)S(1)}, f32[16,128]{1,0:T(8,128)S(1)}, u32[]{:S(2)}, u32[]{:S(2)}) collective-permute-start(f32[16,128]{1,0:T(8,128)S(1)} %log_add_fusion.2), channel_id=1, source_target_pairs={{0,8},{4,12},{8,0},{12,4},{16,24},{20,28},{24,16},{28,20},{1,9},{5... | collective-permute-start | bytes 24584 | tf_op jit(solution)/shard_map/ppermute | solution.py:401
  129.1 3.7 %collective-permute-start.11 = (f32[16,128]{1,0:T(8,128)S(1)}, f32[16,128]{1,0:T(8,128)S(1)}, u32[]{:S(2)}, u32[]{:S(2)}) collective-permute-start(f32[16,128]{1,0:T(8,128)S(1)} %log_add_fusion.4), channel_id=1, source_target_pairs={{0,1},{1,0},{2,3},{3,2},{4,5},{5,4},{6,7},{7,6},{8,9},{9,8},{10,11... | collective-permute-start | bytes 24584 | tf_op jit(solution)/shard_map/ppermute | solution.py:401
  205.1 8.4 %collective-permute-start.22 = (f32[72,256]{1,0:T(8,128)S(1)}, f32[72,256]{1,0:T(8,128)S(1)}, u32[]{:S(2)}, u32[]{:S(2)}) collective-permute-start(f32[72,256]{1,0:T(8,128)S(1)} %get-tuple-element.78), channel_id=1, source_target_pairs={{0,8},{4,12},{8,16},{12,20},{16,24},{20,28},{24,0},{28,4},{1,9},{5... | collective-permute-start | bytes 221192 | tf_op jit(solution)/shard_map/ppermute | solution.py:439
  206.3 8.6 %collective-permute-start.23 = (f32[72,256]{1,0:T(8,128)S(1)}, f32[72,256]{1,0:T(8,128)S(1)}, u32[]{:S(2)}, u32[]{:S(2)}) collective-permute-start(f32[72,256]{1,0:T(8,128)S(1)} %get-tuple-element.79), channel_id=1, source_target_pairs={{0,16},{4,20},{8,24},{12,28},{16,0},{20,4},{24,8},{28,12},{1,17},{... | collective-permute-start | bytes 221192 | tf_op jit(solution)/shard_map/ppermute | solution.py:439
  208.4 6.5 %collective-permute-start.24 = (f32[72,256]{1,0:T(8,128)S(1)}, f32[72,256]{1,0:T(8,128)S(1)}, u32[]{:S(2)}, u32[]{:S(2)}) collective-permute-start(f32[72,256]{1,0:T(8,128)S(1)} %get-tuple-element.80), channel_id=1, source_target_pairs={{0,24},{4,28},{8,0},{12,4},{16,8},{20,12},{24,16},{28,20},{1,25},{... | collective-permute-start | bytes 221192 | tf_op jit(solution)/shard_map/ppermute | solution.py:439
  210.4 7.6 %collective-permute-start.15 = (f32[72,512]{1,0:T(8,128)S(1)}, f32[72,512]{1,0:T(8,128)S(1)}, u32[]{:S(2)}, u32[]{:S(2)}) collective-permute-start(f32[72,512]{1,0:T(8,128)S(1)} %get-tuple-element.74), channel_id=1, source_target_pairs={{0,1},{1,2},{2,3},{3,0},{4,5},{5,6},{6,7},{7,4},{8,9},{9,10},{10,1... | collective-permute-start | bytes 442376 | tf_op jit(solution)/shard_map/ppermute | solution.py:439
  211.9 7.6 %collective-permute-start.16 = (f32[72,512]{1,0:T(8,128)S(1)}, f32[72,512]{1,0:T(8,128)S(1)}, u32[]{:S(2)}, u32[]{:S(2)}) collective-permute-start(f32[72,512]{1,0:T(8,128)S(1)} %get-tuple-element.76), channel_id=1, source_target_pairs={{0,2},{1,3},{2,0},{3,1},{4,6},{5,7},{6,4},{7,5},{8,10},{9,11},{10,... | collective-permute-start | bytes 442376 | tf_op jit(solution)/shard_map/ppermute | solution.py:439
  213.4 6.2 %collective-permute-start.17 = (f32[72,512]{1,0:T(8,128)S(1)}, f32[72,512]{1,0:T(8,128)S(1)}, u32[]{:S(2)}, u32[]{:S(2)}) collective-permute-start(f32[72,512]{1,0:T(8,128)S(1)} %get-tuple-element.75), channel_id=1, source_target_pairs={{0,3},{1,0},{2,1},{3,2},{4,7},{5,4},{6,5},{7,6},{8,11},{9,8},{10,9... | collective-permute-start | bytes 442376 | tf_op jit(solution)/shard_map/ppermute | solution.py:439
  214.9 6.3 %collective-permute-start.25 = (f32[64,256]{1,0:T(8,128)S(1)}, f32[64,256]{1,0:T(8,128)S(1)}, u32[]{:S(2)}, u32[]{:S(2)}) collective-permute-start(f32[64,256]{1,0:T(8,128)S(1)} %fusion.11), channel_id=1, source_target_pairs={{0,8},{4,12},{8,16},{12,20},{16,24},{20,28},{24,0},{28,4},{1,9},{5... | collective-permute-start | bytes 196616 | tf_op jit(solution)/shard_map/ppermute | solution.py:445
  216.6 6.6 %collective-permute-start.26 = (f32[64,256]{1,0:T(8,128)S(1)}, f32[64,256]{1,0:T(8,128)S(1)}, u32[]{:S(2)}, u32[]{:S(2)}) collective-permute-start(f32[64,256]{1,0:T(8,128)S(1)} %fusion.11), channel_id=1, source_target_pairs={{0,16},{4,20},{8,24},{12,28},{16,0},{20,4},{24,8},{28,12},{1,17},{... | collective-permute-start | bytes 196616 | tf_op jit(solution)/shard_map/ppermute | solution.py:445
  218.0 5.8 %collective-permute-start.27 = (f32[64,256]{1,0:T(8,128)S(1)}, f32[64,256]{1,0:T(8,128)S(1)}, u32[]{:S(2)}, u32[]{:S(2)}) collective-permute-start(f32[64,256]{1,0:T(8,128)S(1)} %fusion.11), channel_id=1, source_target_pairs={{0,24},{4,28},{8,0},{12,4},{16,8},{20,12},{24,16},{28,20},{1,25},{... | collective-permute-start | bytes 196616 | tf_op jit(solution)/shard_map/ppermute | solution.py:445
  224.5 12.0 %collective-permute-start.28 = (f32[64,1024]{1,0:T(8,128)S(1)}, f32[64,1024]{1,0:T(8,128)S(1)}, u32[]{:S(2)}, u32[]{:S(2)}) collective-permute-start(f32[64,1024]{1,0:T(8,128)S(1)} %dynamic_update_slice.31), channel_id=1, source_target_pairs={{0,4},{4,0},{8,12},{12,8},{16,20},{20,16},{24,28},{28,24},{1,5},{5... | collective-permute-start | bytes 786440 | tf_op jit(solution)/shard_map/ppermute | solution.py:478
  224.7 7.3 %collective-permute-start.18 = (f32[64,512]{1,0:T(8,128)S(1)}, f32[64,512]{1,0:T(8,128)S(1)}, u32[]{:S(2)}, u32[]{:S(2)}) collective-permute-start(f32[64,512]{1,0:T(8,128)S(1)} %fusion.3), channel_id=1, source_target_pairs={{0,1},{1,2},{2,3},{3,0},{4,5},{5,6},{6,7},{7,4},{8,9},{9,10},{10,1... | collective-permute-start | bytes 393224 | tf_op jit(solution)/shard_map/ppermute | solution.py:445
  226.2 8.1 %collective-permute-start.19 = (f32[64,512]{1,0:T(8,128)S(1)}, f32[64,512]{1,0:T(8,128)S(1)}, u32[]{:S(2)}, u32[]{:S(2)}) collective-permute-start(f32[64,512]{1,0:T(8,128)S(1)} %fusion.3), channel_id=1, source_target_pairs={{0,2},{1,3},{2,0},{3,1},{4,6},{5,7},{6,4},{7,5},{8,10},{9,11},{10,... | collective-permute-start | bytes 393224 | tf_op jit(solution)/shard_map/ppermute | solution.py:445
  227.8 7.6 %collective-permute-start.20 = (f32[64,512]{1,0:T(8,128)S(1)}, f32[64,512]{1,0:T(8,128)S(1)}, u32[]{:S(2)}, u32[]{:S(2)}) collective-permute-start(f32[64,512]{1,0:T(8,128)S(1)} %fusion.3), channel_id=1, source_target_pairs={{0,3},{1,0},{2,1},{3,2},{4,7},{5,4},{6,5},{7,6},{8,11},{9,8},{10,9... | collective-permute-start | bytes 393224 | tf_op jit(solution)/shard_map/ppermute | solution.py:445
  (12 other events, 108.1 us)

commit v3 on v2

v3 whole, which is shorter than its diff:
```python
import functools

import jax
import jax.numpy as jnp
from jax import lax
from jax.experimental import pallas as pl
from jax.experimental.pallas import tpu as pltpu
from jax.sharding import PartitionSpec as P

ITERS = 3
EPS = 0.25
LOG2E = 1.4426950408889634
LN2 = 0.6931471805599453
SHIFT = 85.0
SMALLEST = 2.0**-85
FACTOR_RANGE = 60.0 * LN2
LANES = 128
F32 = jnp.float32
BF16 = jnp.bfloat16
HIGH = lax.Precision.HIGHEST


def split2(a):
    a1 = a.astype(BF16).astype(F32)
    return a1, a - a1


def split3(a):
    a1, rest = split2(a)
    a2, rest = split2(rest)
    return a1, a2, rest


def spread(u, ub):
    for b in range(u.shape[0]):
        ub[b * LANES : (b + 1) * LANES, :] = jnp.broadcast_to(u[b : b + 1, :], (LANES, LANES)).T


def lane_sums(acc, out):
    for b in range(out.shape[0]):
        out[b : b + 1, :] = jnp.sum(acc[b * LANES : (b + 1) * LANES, :].T, axis=0, keepdims=True)


def fold(a):
    return jnp.sum(a.reshape(a.shape[0] // 8, 8, a.shape[1]), axis=0)


def build_operands(x_ref, y_ref, xa, ya):
    d, ns = x_ref.shape
    nt = y_ref.shape[1]
    wide = 2 * LANES
    sub = lax.broadcasted_iota(jnp.int32, (16, wide), 0)
    lane = lax.broadcasted_iota(jnp.int32, (LANES, 2 * d), 1)

    def tail(row, parts):
        out = jnp.zeros(row.shape, F32)
        for at, part in enumerate(parts):
            out = jnp.where(row == at, part, out)
        return out

    def target_block(b, _):
        cols = pl.ds(pl.multiple_of(b * wide, wide), wide)
        y = y_ref[:, cols]
        norm = split3(SHIFT - jnp.sum(y * y, axis=0, keepdims=True) * (LOG2E / EPS))
        y1, y2, y3 = (part.astype(BF16) for part in split3(y * (2.0 * LOG2E / EPS)))
        for at, part in enumerate((y1, y2, y1, y2, y3, y1)):
            ya[at * d : (at + 1) * d, cols] = part
        ya[6 * d : 6 * d + 16, cols] = tail(sub, norm + (1.0, 1.0, 1.0)).astype(BF16)
        ya[6 * d + 16 : 8 * d, cols] = jnp.zeros((2 * d - 16, wide), BF16)
        return 0

    lax.fori_loop(0, nt // wide, target_block, 0, unroll=4)

    def source_block(b, _):
        rows = pl.ds(pl.multiple_of(b * LANES, LANES), LANES)
        x = x_ref[:, rows]
        norm = split3(jnp.sum(x * x, axis=0, keepdims=True) * (-LOG2E / EPS))
        x1, x2, x3 = split3(jnp.concatenate([x, x], axis=0).T)
        xa[rows, 0 : 2 * d] = x1.astype(BF16)
        xa[rows, 2 * d : 4 * d] = x2.astype(BF16)
        xa[rows, 4 * d : 6 * d] = jnp.where(lane < d, x1, x3).astype(BF16)
        last = tail(sub[:8, :LANES], (1.0, 1.0, 1.0) + norm)
        last = jnp.concatenate([last, jnp.zeros((2 * d - 8, LANES), F32)], axis=0)
        xa[rows, 6 * d : 8 * d] = last.T.astype(BF16)
        return 0

    lax.fori_loop(0, ns // LANES, source_block, 0, unroll=4)


def as_row(ref):
    return jnp.concatenate([ref[b : b + 1, :] for b in range(ref.shape[0])], axis=1)


def put_row(row, ref):
    for b in range(ref.shape[0]):
        ref[b : b + 1, :] = row[:, b * LANES : (b + 1) * LANES]


def rows_sweep(x_ref, y_ref, t_ref, lse, out):
    d, ns = x_ref.shape
    y = y_ref[...]
    yn = jnp.sum(y * y, axis=0, keepdims=True)
    t = as_row(t_ref)

    def block(b, _):
        at = pl.multiple_of(b * LANES, LANES)
        xt = jnp.concatenate([x_ref[:, pl.ds(at, LANES)]] * 2, axis=0).T[:, 0:d]
        xn = jnp.sum(xt * xt, axis=1, keepdims=True)
        cross = jnp.dot(xt, y, precision=HIGH, preferred_element_type=F32)
        scores = (2.0 * cross - xn - yn) / EPS + t
        peak = jnp.max(scores, axis=1, keepdims=True)
        weights = jnp.exp(scores - peak)
        total = jnp.sum(weights, axis=1, keepdims=True)
        lse[pl.ds(b, 1), :] = jnp.broadcast_to(peak + jnp.log(total), (LANES, LANES)).T[0:1, :]
        if out is not None:
            vector = lax.dot_general(
                weights / total, y, (((1,), (1,)), ((), ())), precision=HIGH, preferred_element_type=F32
            )
            out[0:d, pl.ds(at, LANES)] = jnp.concatenate([vector, vector], axis=1).T[0:d, :]
        return 0

    lax.fori_loop(0, ns // LANES, block, 0)


def cols_sweep(x_ref, y_ref, r_ref, lse, out, ub):
    d, ns = x_ref.shape
    nt = y_ref.shape[1]
    spread(r_ref[...], ub)
    y = y_ref[...]
    yn = jnp.sum(y * y, axis=0, keepdims=True)

    def block(b, carry):
        at = pl.multiple_of(b * LANES, LANES)
        xb = x_ref[:, pl.ds(at, LANES)]
        xt = jnp.concatenate([xb, xb], axis=0).T[:, 0:d]
        xn = jnp.sum(xt * xt, axis=1, keepdims=True)
        cross = jnp.dot(xt, y, precision=HIGH, preferred_element_type=F32)
        scores = (2.0 * cross - xn - yn) / EPS + ub[pl.ds(at, LANES), 0:1]
        peak = jnp.maximum(carry[0], jnp.max(scores, axis=0, keepdims=True))
        decay = jnp.exp(carry[0] - peak)
        weights = jnp.exp(scores - peak)
        total = carry[1] * decay + jnp.sum(weights, axis=0, keepdims=True)
        if out is not None:
            out[0:d, :] = out[0:d, :] * decay + jnp.dot(
                xb, weights, precision=HIGH, preferred_element_type=F32
            )
        return peak, total

    if out is not None:
        out[0:d, :] = jnp.zeros((d, nt), F32)
    start = (jnp.full((1, nt), -1e30, F32), jnp.zeros((1, nt), F32))
    peak, total = lax.fori_loop(0, ns // LANES, block, start)
    put_row(peak + jnp.log(total), lse)
    if out is not None:
        out[0:d, :] = out[0:d, :] / total


def factors(term):
    top = jnp.max(term)
    return jnp.exp(term - top), top, top - jnp.min(term) <= FACTOR_RANGE


def finish(ref, top, fine):
    values = ref[...]
    ref[...] = jnp.log(values) + (top - SHIFT * LN2)
    return fine & (jnp.min(values) >= SMALLEST)


def fetch(pairs, sem):
    copies = [pltpu.make_async_copy(src, dst, sem.at[i]) for i, (src, dst) in enumerate(pairs)]
    for copy in copies:
        copy.start()
    for copy in copies:
        copy.wait()


def form_kernel(
    x_hbm, y_hbm, a_hbm, b_hbm, k_ref, row_ref, col_ref, x_ref, y_ref, xa, ya, ub, acc, r_s, t_s, sem, *, rows
):
    ns, nt = x_ref.shape[1], y_ref.shape[1]
    fetch(((x_hbm, x_ref), (y_hbm, y_ref), (a_hbm, r_s), (b_hbm, t_s)), sem)
    r_s[...] = jnp.log(r_s[...])
    t_s[...] = jnp.log(t_s[...])
    u, r_top, u_fine = factors(r_s[...])
    v, t_top, v_fine = factors(t_s[...])
    build_operands(x_ref, y_ref, xa, ya)
    spread(u, ub)
    col_ref[...] = v
    acc[...] = jnp.zeros_like(acc)
    tiles = 4 if nt % (4 * LANES) == 0 else 1
    wide = tiles * LANES

    def block(cb, _):
        at = pl.multiple_of(cb * wide, wide)
        vs = [col_ref[pl.ds(cb * tiles + t, 1), :] for t in range(tiles)]
        cs = [jnp.zeros((8, LANES), F32)] * tiles
        for r in range(0, ns, rows):
            z = jnp.dot(xa[r : r + rows, :], ya[:, pl.ds(at, wide)], preferred_element_type=F32)
            k = jnp.exp2(z)
            k_ref[r : r + rows, pl.ds(at, wide)] = k
            ur = ub[r : r + rows, :]
            total = acc[r : r + rows, :]
            for t in range(tiles):
                kt = k[:, t * LANES : (t + 1) * LANES]
                total += kt * vs[t]
                cs[t] += fold(kt * ur)
            acc[r : r + rows, :] = total
        for t in range(tiles):
            col_ref[pl.ds(cb * tiles + t, 1), :] = jnp.sum(cs[t], axis=0, keepdims=True)
        return 0

    lax.fori_loop(0, nt // wide, block, 0)
    lane_sums(acc, row_ref)
    rows_fine = finish(row_ref, t_top, v_fine)
    cols_fine = finish(col_ref, r_top, u_fine)

    @pl.when(jnp.logical_not(rows_fine))
    def _():
        rows_sweep(x_ref, y_ref, t_s, row_ref, None)

    @pl.when(jnp.logical_not(cols_fine))
    def _():
        cols_sweep(x_ref, y_ref, r_s, col_ref, None, ub)


def update(pot_ref, lse_ref, mass_ref, new_ref, term):
    new_ref[...] = 0.5 * (pot_ref[...] - EPS * lse_ref[...])
    term[...] = new_ref[...] / EPS + jnp.log(mass_ref[...])


def cols_kernel(k_ref, x_hbm, y_hbm, f_ref, rl_ref, a_ref, fn_ref, col_ref, ub, r_s, x_ref, y_ref, sem, *, rows):
    update(f_ref, rl_ref, a_ref, fn_ref, r_s)
    u, r_top, fine = factors(r_s[...])
    spread(u, ub)
    ns, nt = k_ref.shape
    tiles = nt // LANES

    def block(rb, cs):
        at = pl.ds(pl.multiple_of(rb * rows, rows), rows)
        ur = ub[at, :]
        return tuple(
            cs[c] + fold(k_ref[at, c * LANES : (c + 1) * LANES] * ur) for c in range(tiles)
        )

    cs = lax.fori_loop(0, ns // rows, block, (jnp.zeros((8, LANES), F32),) * tiles)
    for c in range(tiles):
        col_ref[c : c + 1, :] = jnp.sum(cs[c], axis=0, keepdims=True)
    fine = finish(col_ref, r_top, fine)

    @pl.when(jnp.logical_not(fine))
    def _():
        fetch(((x_hbm, x_ref), (y_hbm, y_ref)), sem)
        cols_sweep(x_ref, y_ref, r_s, col_ref, None, ub)


def rows_kernel(k_ref, x_hbm, y_hbm, g_ref, cl_ref, b_ref, gn_ref, row_ref, acc, vs, t_s, x_ref, y_ref, sem, *, rows):
    update(g_ref, cl_ref, b_ref, gn_ref, t_s)
    v, t_top, fine = factors(t_s[...])
    vs[...] = v
    ns, nt = k_ref.shape

    def block(rb, _):
        at = pl.ds(pl.multiple_of(rb * rows, rows), rows)
        total = jnp.zeros((rows, LANES), F32)
        for c in range(nt // LANES):
            total += k_ref[at, c * LANES : (c + 1) * LANES] * vs[c : c + 1, :]
        acc[at, :] = total
        return 0

    lax.fori_loop(0, ns // rows, block, 0)
    lane_sums(acc, row_ref)
    fine = finish(row_ref, t_top, fine)

    @pl.when(jnp.logical_not(fine))
    def _():
        fetch(((x_hbm, x_ref), (y_hbm, y_ref)), sem)
        rows_sweep(x_ref, y_ref, t_s, row_ref, None)


def weight_rows(out, lse):
    d = out.shape[0] - 8
    for b in range(lse.shape[0]):
        out[d : d + 8, b * LANES : (b + 1) * LANES] = jnp.broadcast_to(lse[b : b + 1, :], (8, LANES))


def parts_of(k):
    k1 = k.astype(BF16)
    return k1, (k - k1.astype(F32)).astype(BF16)


def cols_map_kernel(k_ref, x_ref, y_ref, f_ref, rl_ref, a_ref, fn_ref, out_ref, lse, ub, xu, cacc, r_s, *, rows):
    d = x_ref.shape[0]
    ns, nt = k_ref.shape
    update(f_ref, rl_ref, a_ref, fn_ref, r_s)
    u, r_top, fine = factors(r_s[...])
    sub = lax.broadcasted_iota(jnp.int32, (16, LANES), 0)
    for b in range(ns // LANES):
        at = slice(b * LANES, (b + 1) * LANES)
        ur = u[b : b + 1, :]
        p1, p2 = split2(x_ref[:, at] * ur)
        xu[0:d, at] = p1.astype(BF16)
        xu[d : 2 * d, at] = p2.astype(BF16)
        p1, p2 = split2(jnp.broadcast_to(ur, (16, LANES)))
        xu[2 * d : 2 * d + 16, at] = jnp.where(sub == 0, p1, jnp.where(sub == 1, p2, 0.0)).astype(BF16)
    wide = 2 * LANES

    def block(cb, _):
        at = pl.multiple_of(cb * wide, wide)
        total = jnp.zeros((xu.shape[0], wide), F32)
        for r in range(0, ns, rows):
            xr = xu[:, r : r + rows]
            total += jnp.dot(
                jnp.concatenate([xr, xr], axis=1),
                jnp.concatenate(parts_of(k_ref[r : r + rows, pl.ds(at, wide)]), axis=0),
                preferred_element_type=F32,
            )
        cacc[:, pl.ds(at, wide)] = total
        return 0

    lax.fori_loop(0, nt // wide, block, 0)
    for b in range(nt // LANES):
        at = slice(b * LANES, (b + 1) * LANES)
        den = cacc[2 * d : 2 * d + 1, at] + cacc[2 * d + 1 : 2 * d + 2, at]
        out_ref[0:d, at] = (cacc[0:d, at] + cacc[d : 2 * d, at]) / den
        lse[b : b + 1, :] = den
    fine = finish(lse, r_top, fine)

    @pl.when(jnp.logical_not(fine))
    def _():
        cols_sweep(x_ref, y_ref, r_s, lse, out_ref, ub)

    weight_rows(out_ref, lse)


def rows_map_kernel(k_ref, x_ref, y_ref, g_ref, cl_ref, b_ref, gn_ref, out_ref, lse, wy, acc, t_s, *, rows):
    d = x_ref.shape[0]
    ns, nt = k_ref.shape
    update(g_ref, cl_ref, b_ref, gn_ref, t_s)
    v, t_top, fine = factors(t_s[...])
    lane = lax.broadcasted_iota(jnp.int32, (LANES, 2 * d), 1)
    for b in range(nt // LANES):
        at = slice(b * LANES, (b + 1) * LANES)
        vr = v[b : b + 1, :]
        yb = y_ref[:, at] * vr
        p1, p2 = split2(jnp.concatenate([yb, yb], axis=0).T)
        wy[at, 0 : 2 * d] = jnp.where(lane < d, p1, p2).astype(BF16)
        p1, p2 = split2(jnp.broadcast_to(vr, (2 * d, LANES)).T)
        wy[at, 2 * d : 4 * d] = jnp.where(lane == 0, p1, jnp.where(lane == 1, p2, 0.0)).astype(BF16)
    wide = 2 * LANES
    acc[...] = jnp.zeros_like(acc)

    def block(cb, _):
        at = pl.multiple_of(cb * wide, wide)
        w = wy[pl.ds(at, wide), :]
        ww = jnp.concatenate([w, w], axis=0)
        for r in range(0, ns, rows):
            k = jnp.concatenate(parts_of(k_ref[r : r + rows, pl.ds(at, wide)]), axis=1)
            acc[r : r + rows, :] += jnp.dot(k, ww, preferred_element_type=F32)
        return 0

    lax.fori_loop(0, nt // wide, block, 0)
    for b in range(ns // LANES):
        at = slice(b * LANES, (b + 1) * LANES)
        num = acc[at, 0 : 2 * d].T
        den = acc[at, 2 * d : 4 * d].T
        den = den[0:1, :] + den[1:2, :]
        out_ref[0:d, at] = (num[0:d, :] + num[d : 2 * d, :]) / den
        lse[b : b + 1, :] = den
    fine = finish(lse, t_top, fine)

    @pl.when(jnp.logical_not(fine))
    def _():
        rows_sweep(x_ref, y_ref, t_s, lse, out_ref)

    weight_rows(out_ref, lse)


def merge_kernel(at_ref, whole, *refs, place):
    *others, out = refs
    width = out.shape[1]
    d = whole.shape[0] - 8
    for b in range(width // LANES):
        cols = slice(b * LANES, (b + 1) * LANES)
        at = pl.ds(pl.multiple_of(at_ref[place] + b * LANES, LANES), LANES)
        logs = [whole[d : d + 1, at]] + [other[d : d + 1, cols] for other in others]
        peak = functools.reduce(jnp.maximum, logs)
        weights = [jnp.exp(log - peak) for log in logs]
        total = functools.reduce(jnp.add, weights)
        values = whole[0:d, at] * (weights[0] / total)
        for other, weight in zip(others, weights[1:]):
            values += other[0:d, cols] * (weight / total)
        out[0:d, cols] = values
        if out.shape[0] > d:
            out[d:, cols] = jnp.broadcast_to(peak + jnp.log(total), (8, LANES))


def join_kernel(at_ref, ours, theirs, *refs):
    *pieces, col_out, row_out, sem = refs
    d = col_out.shape[0]
    count = ours.shape[0] // d
    copies = []

    def lay(src, out, place):
        at = pl.multiple_of(at_ref[3 + place], LANES)
        dst = out.at[:, pl.ds(at, src.shape[1])]
        copies.append(pltpu.make_async_copy(src, dst, sem.at[len(copies)]))
        copies[-1].start()

    for which, stack in enumerate((ours, theirs)):
        for k in range(count):
            lay(stack.at[k * d : (k + 1) * d, :], col_out, which * count + k)
    for k, piece_ref in enumerate(pieces):
        lay(piece_ref, row_out, 2 * count + k)
    for copy in copies:
        copy.wait()


VM = pl.BlockSpec(memory_space=pltpu.VMEM)
ANY = pl.BlockSpec(memory_space=pl.ANY)
PARAMS = pltpu.CompilerParams(vmem_limit_bytes=24 * 2**20)


def cost(flops, size):
    return pl.CostEstimate(flops=flops, bytes_accessed=size, transcendentals=0)


def vector(n):
    return jax.ShapeDtypeStruct((n // LANES, LANES), F32)


def scratch(n):
    return pltpu.VMEM((n // LANES, LANES), F32)


def form(x, y, a, b):
    d, ns = x.shape
    nt = y.shape[1]
    return pl.pallas_call(
        functools.partial(form_kernel, rows=256),
        out_shape=(pltpu.VMEM((ns, nt), F32), vector(ns), vector(nt)),
        in_specs=[ANY] * 4,
        out_specs=(VM,) * 3,
        scratch_shapes=[
            pltpu.VMEM((d, ns), F32),
            pltpu.VMEM((d, nt), F32),
            pltpu.VMEM((ns, 8 * d), BF16),
            pltpu.VMEM((8 * d, nt), BF16),
            pltpu.VMEM((ns, LANES), F32),
            pltpu.VMEM((ns, LANES), F32),
            scratch(ns),
            scratch(nt),
            pltpu.SemaphoreType.DMA((4,)),
        ],
        compiler_params=PARAMS,
        cost_estimate=cost(20 * d * ns * nt, 4 * ns * nt),
        name="form",
    )(x, y, a, b)


def sweep_scratch(d, ns, nt):
    return [pltpu.VMEM((d, ns), F32), pltpu.VMEM((d, nt), F32), pltpu.SemaphoreType.DMA((2,))]


def cols_sums(k, x, y, f, row_lse, a):
    ns, nt = k.shape
    return pl.pallas_call(
        functools.partial(cols_kernel, rows=64),
        out_shape=(vector(ns), vector(nt)),
        in_specs=[VM, ANY, ANY, VM, VM, VM],
        out_specs=(VM,) * 2,
        scratch_shapes=[pltpu.VMEM((ns, LANES), F32), scratch(ns)] + sweep_scratch(x.shape[0], ns, nt),
        compiler_params=PARAMS,
        cost_estimate=cost(2 * ns * nt, 2 * ns * nt),
        name="cols_sums",
    )(k, x, y, f, row_lse, a)


def rows_sums(k, x, y, g, col_lse, b):
    ns, nt = k.shape
    return pl.pallas_call(
        functools.partial(rows_kernel, rows=64),
        out_shape=(vector(nt), vector(ns)),
        in_specs=[VM, ANY, ANY, VM, VM, VM],
        out_specs=(VM,) * 2,
        scratch_shapes=[pltpu.VMEM((ns, LANES), F32), scratch(nt), scratch(nt)]
        + sweep_scratch(x.shape[0], ns, nt),
        compiler_params=PARAMS,
        cost_estimate=cost(2 * ns * nt, 2 * ns * nt),
        name="rows_sums",
    )(k, x, y, g, col_lse, b)


def cols_map(k, x, y, f, row_lse, a):
    d = x.shape[0]
    ns, nt = k.shape
    return pl.pallas_call(
        functools.partial(cols_map_kernel, rows=512),
        out_shape=(vector(ns), jax.ShapeDtypeStruct((d + 8, nt), F32)),
        in_specs=[VM] * 6,
        out_specs=(VM,) * 2,
        scratch_shapes=[
            scratch(nt),
            pltpu.VMEM((ns, LANES), F32),
            pltpu.VMEM((2 * d + 16, ns), BF16),
            pltpu.VMEM((2 * d + 16, nt), F32),
            scratch(ns),
        ],
        compiler_params=PARAMS,
        cost_estimate=cost(16 * d * ns * nt, 4 * ns * nt),
        name="cols_map",
    )(k, x, y, f, row_lse, a)


def rows_map(k, x, y, g, col_lse, b):
    d = x.shape[0]
    ns, nt = k.shape
    return pl.pallas_call(
        functools.partial(rows_map_kernel, rows=512),
        out_shape=(vector(nt), jax.ShapeDtypeStruct((d + 8, ns), F32)),
        in_specs=[VM] * 6,
        out_specs=(VM,) * 2,
        scratch_shapes=[
            scratch(ns),
            pltpu.VMEM((nt, 4 * d), BF16),
            pltpu.VMEM((ns, 4 * d), F32),
            scratch(nt),
        ],
        compiler_params=PARAMS,
        cost_estimate=cost(16 * d * ns * nt, 4 * ns * nt),
        name="rows_map",
    )(k, x, y, g, col_lse, b)


def merge(at, place, whole, others, keep):
    rows, width = others[0].shape
    return pl.pallas_call(
        functools.partial(merge_kernel, place=place),
        out_shape=jax.ShapeDtypeStruct((rows if keep else rows - 8, width), F32),
        in_specs=[pl.BlockSpec(memory_space=pltpu.SMEM)] + [VM] * (1 + len(others)),
        out_specs=VM,
        compiler_params=PARAMS,
        name="merge",
    )(at, whole, *others)


def join(at, ours, theirs, pieces):
    d, width = pieces[0].shape
    nt = 2 * ours.shape[0] // d * ours.shape[1]
    ns = width * len(pieces)
    return pl.pallas_call(
        join_kernel,
        out_shape=(jax.ShapeDtypeStruct((d, nt), F32), jax.ShapeDtypeStruct((d, ns), F32)),
        in_specs=[pl.BlockSpec(memory_space=pltpu.SMEM)] + [VM] * (2 + len(pieces)),
        out_specs=(ANY,) * 2,
        scratch_shapes=[pltpu.SemaphoreType.DMA((at.shape[0] - 3,))],
        compiler_params=PARAMS,
        name="join",
    )(at, ours, theirs, *pieces)


def merged(first, second):
    peak = jnp.maximum(first, second)
    return peak + jnp.log(jnp.exp(first - peak) + jnp.exp(second - peak))


def lse_over(axis, part):
    n = lax.axis_size(axis)
    step = n // 2
    while step:
        part = merged(part, lax.ppermute(part, axis, [(i, i ^ step) for i in range(n)]))
        step //= 2
    return part


def pairs(n, group, stride, k):
    return [(i, i + (((i // stride) + k) % group - (i // stride) % group) * stride) for i in range(n)]


def places(index, group, stride, width):
    own = (index // stride) % group
    return [(own + k) % group * width for k in range(group)]


def piece(a, at, count):
    zero = jnp.zeros((), at.dtype)
    return lax.dynamic_slice(
        a, (zero, at), (a.shape[0], a.shape[1] // count), allow_negative_indices=False
    )


def merged_piece(axis, place, stride, part, at, own):
    n, group = lax.axis_size(axis), len(place)
    got = [
        lax.ppermute(piece(part, place[k], group), axis, pairs(n, group, stride, k))
        for k in range(1, group)
    ]
    return merge(at, own, part, got, False)


def all_pieces(axis, group, stride, own):
    n = lax.axis_size(axis)
    return [own] + [lax.ppermute(own, axis, pairs(n, group, stride, k)) for k in range(1, group)]


def body(sources, targets, source_mass, target_mass):
    rows, cols = lax.axis_size("row"), lax.axis_size("col")
    ns, nt = sources.shape[1], targets.shape[1]
    index = lax.axis_index("row")
    halves = places(index, 2, 1, nt // 2)
    row_places = places(index, rows // 2, 2, nt // rows)
    col_places = places(lax.axis_index("col"), cols, 1, ns // cols)
    laid = [half + row_places[-k] for half in halves for k in range(rows // 2)]
    laid = [halves[0], row_places[0], col_places[0]] + laid + [col_places[-k] for k in range(cols)]
    laid = jnp.stack(laid)
    sources, halves, row_places, col_places, laid = lax.optimization_barrier(
        (sources, halves, row_places, col_places, laid)
    )
    x, y = sources, targets
    a = source_mass.reshape(-1, LANES)
    b = target_mass.reshape(-1, LANES)
    f = jnp.zeros_like(a)
    g = jnp.zeros_like(b)
    k, row_part, col_part = form(x, y, a, b)
    for sweep in range(ITERS):
        row_lse = lse_over("col", row_part)
        col_lse = lse_over("row", col_part)
        last = sweep == ITERS - 1
        f, col_part = (cols_map if last else cols_sums)(k, x, y, f, row_lse, a)
        g, row_part = (rows_map if last else rows_sums)(k, x, y, g, col_lse, b)
    pair = pairs(rows, 2, 1, 1)
    other = lax.ppermute(piece(col_part, halves[1], 2), "row", pair)
    chip = merge(laid, 0, col_part, [other], True)
    ours = merged_piece("row", row_places, 2, chip, laid, 1)
    ours = jnp.concatenate(all_pieces("row", rows // 2, 2, ours), axis=0)
    theirs = lax.ppermute(ours, "row", pair)
    own = merged_piece("col", col_places, 1, row_part, laid, 2)
    source_pieces = all_pieces("col", cols, 1, own)
    target_map, source_map = join(laid, ours, theirs, source_pieces)
    return f.reshape(-1), g.reshape(-1), source_map, target_map


def solution(mesh):
    in_specs = (P(None, "row"), P(None, "col"), P("row"), P("col"))
    out_specs = (P("row"), P("col"), P(None, "row"), P(None, "col"))
    return jax.shard_map(body, mesh=mesh, in_specs=in_specs, out_specs=out_specs, check_vma=False)
```

time: 238 us -> 303 us (1.27)
  Pallas kernels: 167 us -> 242 us
  local copies, waits for them, and re-layouts: 10.6 us -> 4.05 us
  starting transfers between devices: 41.6 us -> 37.2 us
    pallas_call x3 -> x10, Pallas kernels: 130 us -> 194 us  [the longest x1 70.3 us: rows_map(): pl.pallas_call(functools.partial(rows_map_kernel, rows=512), out_shape=(v...]
    pallas_call x1, Pallas kernels: 37 us -> 47.9 us  [form(): pl.pallas_call(functools.partial(form_kernel, rows=256), out_shape=(pltpu...]
    dynamic_update_slice x8 -> x0, local copies, waits for them, and re-layouts: 6.08 us -> none  [put(): lax.dynamic_update_slice(a, part, (zero, at), allow_negative_indices=False)]
  transfers between devices with their start and end apart: 29 -> 29, of which waited for: 17 -> 13; matrix products, arithmetic and copies ran while one was open for 3% -> 0% of each run, Pallas kernels for 0% -> 63%
where the time goes in v3:
time: 303 us
  Pallas kernels  242 us (80%)
  starting transfers between devices  37.2 us (12%)
  waiting for transfers between devices  17.6 us (6%)
  local copies, waits for them, and re-layouts  4.05 us (1%)
    pallas_call x1, Pallas kernels, rows_map(): pl.pallas_call(functools.partial(rows_map_kernel, rows=512), out_shape=(v...  70.3 us
    pallas_call x1, Pallas kernels, form(): pl.pallas_call(functools.partial(form_kernel, rows=256), out_shape=(pltpu...  47.9 us
    pallas_call x2, Pallas kernels, rows_sums(): pl.pallas_call(functools.partial(rows_kernel, rows=64), out_shape=(vector...  47.6 us
    pallas_call x2, Pallas kernels, cols_sums(): pl.pallas_call(functools.partial(cols_kernel, rows=64), out_shape=(vector...  41.6 us
    pallas_call x1, Pallas kernels, cols_map(): pl.pallas_call(functools.partial(cols_map_kernel, rows=512), out_shape=(v...  31.4 us
    ppermute x15, starting transfers between devices, lse_over(): lax.ppermute(part, axis, [(i, i ^ step) for i in range(n)])  21.3 us
    ppermute x6, starting transfers between devices, all_pieces(): lax.ppermute(own, axis, pairs(n, group, stride, k))  8.77 us
    ppermute x15, waiting for transfers between devices, lse_over(): lax.ppermute(part, axis, [(i, i ^ step) for i in range(n)])  8.58 us
  transfers between devices with their start and end apart: 29, of which 13 were waited for; matrix products, arithmetic and copies ran while one was open for 0% of the time, Pallas kernels for 63%

profile of v3, /device:TPU:0, one launch (start us, length us, event | category | flops | bytes accessed | tf_op | source)
XLA Modules:
  0.0 302.5 jit_solution(18269822070117065084)
XLA Ops:
  4.4 47.9 %form.1 = (f32[2048,2048]{1,0:T(8,128)S(1)}, f32[16,128]{1,0:T(8,128)S(1)}, f32[16,128]{1,0:T(8,128)S(1)}) custom-call(f32[64,2048]{1,0:T(8,128)S(1)} %copy-done, f32[64,2048]{1,0:T(8,128)S(1)} %copy-done.2, f32[16,128]{1,0:T(8,128)S(1)} %bitcast.18, f32[16,128]{1,0:T(8,128)S(1)} %bitcast.22), custom_call_target="tpu_custom_call" | custom-call | flops 5368709120 | bytes 16777216 | tf_op jit(solution)/shard_map/form/pallas_call | solution.py:438
  52.3 3.0 %collective-permute-start = (f32[16,128]{1,0:T(8,128)S(1)}, f32[16,128]{1,0:T(8,128)S(1)}, u32[]{:S(2)}, u32[]{:S(2)}) collective-permute-start(f32[16,128]{1,0:T(8,128)S(1)} %get-tuple-element.32), channel_id=1, source_target_pairs={{0,2},{1,3},{2,0},{3,1},{4,6},{5,7},{6,4},{7,5},{8,10},{9,11},{10,... | collective-permute-start | bytes 24584 | tf_op jit(solution)/shard_map/ppermute | solution.py:570
  55.3 2.6 collective-permute-start.2
  57.9 1.6 collective-permute-start.1
  59.9 1.6 collective-permute-start.3
  61.7 20.7 %cols_sums.2 = (f32[16,128]{1,0:T(8,128)S(1)}, f32[16,128]{1,0:T(8,128)S(1)}) custom-call(f32[2048,2048]{1,0:T(8,128)S(1)} %get-tuple-element.31.k_ref, f32[64,2048]{1,0:T(8,128)S(1)} %copy-done, f32[64,2048]{1,0:T(8,128)S(1)} %copy-done.2, f32[16,128]{1,0:T(8,128)S(1)} %broadcast_1_f_ref_g_ref.2.f_ref.g_ref, f32[16,128]{1,0:T(8,128)S(1)} %log_add_fusion.13.rl_ref, ...), custom_call_target="tpu_custom_call" | custom-call | flops 8388608 | bytes 8388608 | tf_op jit(solution)/shard_map/cols_sums/pallas_call | solution.py:466
  82.4 2.5 collective-permute-start.7
  85.0 2.0 collective-permute-done.7
  87.0 1.6 collective-permute-start.8
  88.7 23.8 %rows_sums.2 = (f32[16,128]{1,0:T(8,128)S(1)}, f32[16,128]{1,0:T(8,128)S(1)}) custom-call(f32[2048,2048]{1,0:T(8,128)S(1)} %get-tuple-element.31.k_ref, f32[64,2048]{1,0:T(8,128)S(1)} %copy-done, f32[64,2048]{1,0:T(8,128)S(1)} %copy-done.2, f32[16,128]{1,0:T(8,128)S(1)} %broadcast_1_f_ref_g_ref.2.f_ref.g_ref, f32[16,128]{1,0:T(8,128)S(1)} %log_add_fusion.10.cl_ref, ...), custom_call_target="tpu_custom_call" | custom-call | flops 8388608 | bytes 8388608 | tf_op jit(solution)/shard_map/rows_sums/pallas_call | solution.py:480
  113.8 2.5 collective-permute-done.5
  116.3 1.6 collective-permute-start.6
  117.8 23.8 %rows_sums.3 = (f32[16,128]{1,0:T(8,128)S(1)}, f32[16,128]{1,0:T(8,128)S(1)}) custom-call(f32[2048,2048]{1,0:T(8,128)S(1)} %get-tuple-element.31.k_ref, f32[64,2048]{1,0:T(8,128)S(1)} %copy-done, f32[64,2048]{1,0:T(8,128)S(1)} %copy-done.2, f32[16,128]{1,0:T(8,128)S(1)} %get-tuple-element.37.g_ref, f32[16,128]{1,0:T(8,128)S(1)} %log_add_fusion.5.cl_ref, ...), custom_call_target="tpu_custom_call" | custom-call | flops 8388608 | bytes 8388608 | tf_op jit(solution)/shard_map/rows_sums/pallas_call | solution.py:480
  142.8 20.9 %cols_sums.3 = (f32[16,128]{1,0:T(8,128)S(1)}, f32[16,128]{1,0:T(8,128)S(1)}) custom-call(f32[2048,2048]{1,0:T(8,128)S(1)} %get-tuple-element.31.k_ref, f32[64,2048]{1,0:T(8,128)S(1)} %copy-done, f32[64,2048]{1,0:T(8,128)S(1)} %copy-done.2, f32[16,128]{1,0:T(8,128)S(1)} %get-tuple-element.33.f_ref, f32[16,128]{1,0:T(8,128)S(1)} %log_add_fusion.8.rl_ref, ...), custom_call_target="tpu_custom_call" | custom-call | flops 8388608 | bytes 8388608 | tf_op jit(solution)/shard_map/cols_sums/pallas_call | solution.py:466
  163.8 2.7 collective-permute-start.12
  170.2 31.4 %cols_map.1 = (f32[16,128]{1,0:T(8,128)}, f32[72,2048]{1,0:T(8,128)S(1)}) custom-call(f32[2048,2048]{1,0:T(8,128)S(1)} %get-tuple-element.31.k_ref, f32[64,2048]{1,0:T(8,128)S(1)} %copy-done, f32[64,2048]{1,0:T(8,128)S(1)} %copy-done.2, f32[16,128]{1,0:T(8,128)S(1)} %get-tuple-element.36.f_ref, f32[16,128]{1,0:T(8,128)S(1)} %log_add_fusion.3.rl_ref, ...), custom_call_target="tpu_custom_call" | custom-call | flops 4294967296 | bytes 16777216 | tf_op jit(solution)/shard_map/cols_map/pallas_call | solution.py:496
  204.7 2.5 collective-permute-start.17
  208.5 70.3 %rows_map.1 = (f32[16,128]{1,0:T(8,128)}, f32[72,2048]{1,0:T(8,128)S(1)}) custom-call(f32[2048,2048]{1,0:T(8,128)S(1)} %get-tuple-element.31.k_ref, f32[64,2048]{1,0:T(8,128)S(1)} %copy-done.1, f32[64,2048]{1,0:T(8,128)S(1)} %copy-done.3, f32[16,128]{1,0:T(8,128)S(1)} %get-tuple-element.41.g_ref, f32[16,128]{1,0:T(8,128)S(1)} %log_add_fusion.cl_ref, ...), custom_call_target="tpu_custom_call" | custom-call | flops 4294967296 | bytes 16777216 | tf_op jit(solution)/shard_map/rows_map/pallas_call | solution.py:517
  281.1 2.8 collective-permute-start.21
  286.1 1.6 collective-permute-start.25
  287.7 3.3 %collective-permute-done.23.refs_0_ = f32[72,512]{1,0:T(8,128)S(1)} collective-permute-done((f32[72,512]{1,0:T(8,128)S(1)}, f32[72,512]{1,0:T(8,128)S(1)}, u32[]{:S(2)}, u32[]{:S(2)}) %collective-permute-start.23) | collective-permute-done | bytes 147488 | tf_op jit(solution)/shard_map/ppermute | solution.py:594
  292.5 2.3 collective-permute-start.26
  296.7 1.7 collective-permute-done.26.refs_1_
  300.7 1.6 join.1
  (82 shorter events, 24.9 us)
Async XLA Ops:
  52.3 5.6 %collective-permute-start = (f32[16,128]{1,0:T(8,128)S(1)}, f32[16,128]{1,0:T(8,128)S(1)}, u32[]{:S(2)}, u32[]{:S(2)}) collective-permute-start(f32[16,128]{1,0:T(8,128)S(1)} %get-tuple-element.32), channel_id=1, source_target_pairs={{0,2},{1,3},{2,0},{3,1},{4,6},{5,7},{6,4},{7,5},{8,10},{9,11},{10,... | collective-permute-start | bytes 24584 | tf_op jit(solution)/shard_map/ppermute | solution.py:570
  55.3 4.5 %collective-permute-start.2 = (f32[16,128]{1,0:T(8,128)S(1)}, f32[16,128]{1,0:T(8,128)S(1)}, u32[]{:S(2)}, u32[]{:S(2)}) collective-permute-start(f32[16,128]{1,0:T(8,128)S(1)} %get-tuple-element.34), channel_id=1, source_target_pairs={{0,16},{4,20},{8,24},{12,28},{16,0},{20,4},{24,8},{28,12},{1,17},{... | collective-permute-start | bytes 24584 | tf_op jit(solution)/shard_map/ppermute | solution.py:570
  59.9 25.1 %collective-permute-start.3 = (f32[16,128]{1,0:T(8,128)S(1)}, f32[16,128]{1,0:T(8,128)S(1)}, u32[]{:S(2)}, u32[]{:S(2)}) collective-permute-start(f32[16,128]{1,0:T(8,128)S(1)} %log_add_fusion.12), channel_id=1, source_target_pairs={{0,8},{4,12},{8,0},{12,4},{16,24},{20,28},{24,16},{28,20},{1,9},{5... | collective-permute-start | bytes 24584 | tf_op jit(solution)/shard_map/ppermute | solution.py:570
  82.4 4.6 %collective-permute-start.7 = (f32[16,128]{1,0:T(8,128)S(1)}, f32[16,128]{1,0:T(8,128)S(1)}, u32[]{:S(2)}, u32[]{:S(2)}) collective-permute-start(f32[16,128]{1,0:T(8,128)S(1)} %get-tuple-element.38), channel_id=1, source_target_pairs={{0,16},{4,20},{8,24},{12,28},{16,0},{20,4},{24,8},{28,12},{1,17},{... | collective-permute-start | bytes 24584 | tf_op jit(solution)/shard_map/ppermute | solution.py:570
  85.0 3.7 %collective-permute-start.4 = (f32[16,128]{1,0:T(8,128)S(1)}, f32[16,128]{1,0:T(8,128)S(1)}, u32[]{:S(2)}, u32[]{:S(2)}) collective-permute-start(f32[16,128]{1,0:T(8,128)S(1)} %log_add_fusion.11), channel_id=1, source_target_pairs={{0,4},{4,0},{8,12},{12,8},{16,20},{20,16},{24,28},{28,24},{1,5},{5... | collective-permute-start | bytes 24584 | tf_op jit(solution)/shard_map/ppermute | solution.py:570
  87.0 26.6 %collective-permute-start.8 = (f32[16,128]{1,0:T(8,128)S(1)}, f32[16,128]{1,0:T(8,128)S(1)}, u32[]{:S(2)}, u32[]{:S(2)}) collective-permute-start(f32[16,128]{1,0:T(8,128)S(1)} %log_add_fusion.7), channel_id=1, source_target_pairs={{0,8},{4,12},{8,0},{12,4},{16,24},{20,28},{24,16},{28,20},{1,9},{5... | collective-permute-start | bytes 24584 | tf_op jit(solution)/shard_map/ppermute | solution.py:570
  113.7 4.2 %collective-permute-start.9 = (f32[16,128]{1,0:T(8,128)S(1)}, f32[16,128]{1,0:T(8,128)S(1)}, u32[]{:S(2)}, u32[]{:S(2)}) collective-permute-start(f32[16,128]{1,0:T(8,128)S(1)} %log_add_fusion.6), channel_id=1, source_target_pairs={{0,4},{4,0},{8,12},{12,8},{16,20},{20,16},{24,28},{28,24},{1,5},{5... | collective-permute-start | bytes 24584 | tf_op jit(solution)/shard_map/ppermute | solution.py:570
  116.3 26.5 %collective-permute-start.6 = (f32[16,128]{1,0:T(8,128)S(1)}, f32[16,128]{1,0:T(8,128)S(1)}, u32[]{:S(2)}, u32[]{:S(2)}) collective-permute-start(f32[16,128]{1,0:T(8,128)S(1)} %log_add_fusion.9), channel_id=1, source_target_pairs={{0,1},{1,0},{2,3},{3,2},{4,5},{5,4},{6,7},{7,6},{8,9},{9,8},{10,11... | collective-permute-start | bytes 24584 | tf_op jit(solution)/shard_map/ppermute | solution.py:570
  141.7 24.7 %collective-permute-start.10 = (f32[16,128]{1,0:T(8,128)S(1)}, f32[16,128]{1,0:T(8,128)S(1)}, u32[]{:S(2)}, u32[]{:S(2)}) collective-permute-start(f32[16,128]{1,0:T(8,128)S(1)} %get-tuple-element.39), channel_id=1, source_target_pairs={{0,2},{1,3},{2,0},{3,1},{4,6},{5,7},{6,4},{7,5},{8,10},{9,11},{10,... | collective-permute-start | bytes 24584 | tf_op jit(solution)/shard_map/ppermute | solution.py:570
  163.8 4.6 %collective-permute-start.12 = (f32[16,128]{1,0:T(8,128)S(1)}, f32[16,128]{1,0:T(8,128)S(1)}, u32[]{:S(2)}, u32[]{:S(2)}) collective-permute-start(f32[16,128]{1,0:T(8,128)S(1)} %get-tuple-element.42), channel_id=1, source_target_pairs={{0,16},{4,20},{8,24},{12,28},{16,0},{20,4},{24,8},{28,12},{1,17},{... | collective-permute-start | bytes 24584 | tf_op jit(solution)/shard_map/ppermute | solution.py:570
  168.4 33.4 %collective-permute-start.13 = (f32[16,128]{1,0:T(8,128)S(1)}, f32[16,128]{1,0:T(8,128)S(1)}, u32[]{:S(2)}, u32[]{:S(2)}) collective-permute-start(f32[16,128]{1,0:T(8,128)S(1)} %log_add_fusion.2), channel_id=1, source_target_pairs={{0,8},{4,12},{8,0},{12,4},{16,24},{20,28},{24,16},{28,20},{1,9},{5... | collective-permute-start | bytes 24584 | tf_op jit(solution)/shard_map/ppermute | solution.py:570
  204.2 74.6 %collective-permute-start.16 = (f32[72,256]{1,0:T(8,128)S(1)}, f32[72,256]{1,0:T(8,128)S(1)}, u32[]{:S(2)}, u32[]{:S(2)}) collective-permute-start(f32[72,256]{1,0:T(8,128)S(1)} %get-tuple-element.61), channel_id=1, source_target_pairs={{0,8},{4,12},{8,16},{12,20},{16,24},{20,28},{24,0},{28,4},{1,9},{5... | collective-permute-start | bytes 221192 | tf_op jit(solution)/shard_map/ppermute | solution.py:594
  204.7 74.1 %collective-permute-start.17 = (f32[72,256]{1,0:T(8,128)S(1)}, f32[72,256]{1,0:T(8,128)S(1)}, u32[]{:S(2)}, u32[]{:S(2)}) collective-permute-start(f32[72,256]{1,0:T(8,128)S(1)} %get-tuple-element.60), channel_id=1, source_target_pairs={{0,16},{4,20},{8,24},{12,28},{16,0},{20,4},{24,8},{28,12},{1,17},{... | collective-permute-start | bytes 221192 | tf_op jit(solution)/shard_map/ppermute | solution.py:594
  207.1 71.6 %collective-permute-start.18 = (f32[72,256]{1,0:T(8,128)S(1)}, f32[72,256]{1,0:T(8,128)S(1)}, u32[]{:S(2)}, u32[]{:S(2)}) collective-permute-start(f32[72,256]{1,0:T(8,128)S(1)} %get-tuple-element.59), channel_id=1, source_target_pairs={{0,24},{4,28},{8,0},{12,4},{16,8},{20,12},{24,16},{28,20},{1,25},{... | collective-permute-start | bytes 221192 | tf_op jit(solution)/shard_map/ppermute | solution.py:594
  279.4 6.7 %collective-permute-start.19 = (f32[64,256]{1,0:T(8,128)S(1)}, f32[64,256]{1,0:T(8,128)S(1)}, u32[]{:S(2)}, u32[]{:S(2)}) collective-permute-start(f32[64,256]{1,0:T(8,128)S(1)} %merge.4), channel_id=1, source_target_pairs={{0,8},{4,12},{8,16},{12,20},{16,24},{20,28},{24,0},{28,4},{1,9},{5... | collective-permute-start | bytes 196616 | tf_op jit(solution)/shard_map/ppermute | solution.py:602
  280.1 7.5 %collective-permute-start.20 = (f32[64,256]{1,0:T(8,128)S(1)}, f32[64,256]{1,0:T(8,128)S(1)}, u32[]{:S(2)}, u32[]{:S(2)}) collective-permute-start(f32[64,256]{1,0:T(8,128)S(1)} %merge.4), channel_id=1, source_target_pairs={{0,16},{4,20},{8,24},{12,28},{16,0},{20,4},{24,8},{28,12},{1,17},{... | collective-permute-start | bytes 196616 | tf_op jit(solution)/shard_map/ppermute | solution.py:602
  281.1 6.5 %collective-permute-start.21 = (f32[64,256]{1,0:T(8,128)S(1)}, f32[64,256]{1,0:T(8,128)S(1)}, u32[]{:S(2)}, u32[]{:S(2)}) collective-permute-start(f32[64,256]{1,0:T(8,128)S(1)} %merge.4), channel_id=1, source_target_pairs={{0,24},{4,28},{8,0},{12,4},{16,8},{20,12},{24,16},{28,20},{1,25},{... | collective-permute-start | bytes 196616 | tf_op jit(solution)/shard_map/ppermute | solution.py:602
  284.1 6.9 %collective-permute-start.23 = (f32[72,512]{1,0:T(8,128)S(1)}, f32[72,512]{1,0:T(8,128)S(1)}, u32[]{:S(2)}, u32[]{:S(2)}) collective-permute-start(f32[72,512]{1,0:T(8,128)S(1)} %get-tuple-element.58), channel_id=1, source_target_pairs={{0,1},{1,2},{2,3},{3,0},{4,5},{5,6},{6,7},{7,4},{8,9},{9,10},{10,1... | collective-permute-start | bytes 442376 | tf_op jit(solution)/shard_map/ppermute | solution.py:594
  284.7 7.1 %collective-permute-start.24 = (f32[72,512]{1,0:T(8,128)S(1)}, f32[72,512]{1,0:T(8,128)S(1)}, u32[]{:S(2)}, u32[]{:S(2)}) collective-permute-start(f32[72,512]{1,0:T(8,128)S(1)} %get-tuple-element.57), channel_id=1, source_target_pairs={{0,2},{1,3},{2,0},{3,1},{4,6},{5,7},{6,4},{7,5},{8,10},{9,11},{10,... | collective-permute-start | bytes 442376 | tf_op jit(solution)/shard_map/ppermute | solution.py:594
  286.1 5.8 %collective-permute-start.25 = (f32[72,512]{1,0:T(8,128)S(1)}, f32[72,512]{1,0:T(8,128)S(1)}, u32[]{:S(2)}, u32[]{:S(2)}) collective-permute-start(f32[72,512]{1,0:T(8,128)S(1)} %get-tuple-element.56), channel_id=1, source_target_pairs={{0,3},{1,0},{2,1},{3,2},{4,7},{5,4},{6,5},{7,6},{8,11},{9,8},{10,9... | collective-permute-start | bytes 442376 | tf_op jit(solution)/shard_map/ppermute | solution.py:594
  287.7 13.1 %collective-permute-start.22 = (f32[256,256]{1,0:T(8,128)S(1)}, f32[256,256]{1,0:T(8,128)S(1)}, u32[]{:S(2)}, u32[]{:S(2)}) collective-permute-start(f32[256,256]{1,0:T(8,128)S(1)} %pad_maximum_fusion.ours), channel_id=1, source_target_pairs={{0,4},{4,0},{8,12},{12,8},{16,20},{20,16},{24,28},{28,24},{1,5},{5... | collective-permute-start | bytes 786440 | tf_op jit(solution)/shard_map/ppermute | solution.py:635
  292.5 5.9 %collective-permute-start.26 = (f32[64,512]{1,0:T(8,128)S(1)}, f32[64,512]{1,0:T(8,128)S(1)}, u32[]{:S(2)}, u32[]{:S(2)}) collective-permute-start(f32[64,512]{1,0:T(8,128)S(1)} %merge.5.refs_0_), channel_id=1, source_target_pairs={{0,1},{1,2},{2,3},{3,0},{4,5},{5,6},{6,7},{7,4},{8,9},{9,10},{10,1... | collective-permute-start | bytes 393224 | tf_op jit(solution)/shard_map/ppermute | solution.py:602
  294.8 5.0 %collective-permute-start.27 = (f32[64,512]{1,0:T(8,128)S(1)}, f32[64,512]{1,0:T(8,128)S(1)}, u32[]{:S(2)}, u32[]{:S(2)}) collective-permute-start(f32[64,512]{1,0:T(8,128)S(1)} %merge.5.refs_0_), channel_id=1, source_target_pairs={{0,2},{1,3},{2,0},{3,1},{4,6},{5,7},{6,4},{7,5},{8,10},{9,11},{10,... | collective-permute-start | bytes 393224 | tf_op jit(solution)/shard_map/ppermute | solution.py:602
  295.8 5.0 %collective-permute-start.28 = (f32[64,512]{1,0:T(8,128)S(1)}, f32[64,512]{1,0:T(8,128)S(1)}, u32[]{:S(2)}, u32[]{:S(2)}) collective-permute-start(f32[64,512]{1,0:T(8,128)S(1)} %merge.5.refs_0_), channel_id=1, source_target_pairs={{0,3},{1,0},{2,1},{3,2},{4,7},{5,4},{6,5},{7,6},{8,11},{9,8},{10,9... | collective-permute-start | bytes 393224 | tf_op jit(solution)/shard_map/ppermute | solution.py:602
  (13 other events, 287.6 us)

commit v4 on v3

--- a/solution.py
+++ b/solution.py
@@ -175,7 +175,7 @@
 
 
 def form_kernel(
-    x_hbm, y_hbm, a_hbm, b_hbm, k_ref, row_ref, col_ref, x_ref, y_ref, xa, ya, ub, acc, r_s, t_s, sem, *, rows
+    x_hbm, y_hbm, a_hbm, b_hbm, k_ref, x_ref, y_ref, row_ref, col_ref, xa, ya, ub, acc, r_s, t_s, sem, *, rows
 ):
     ns, nt = x_ref.shape[1], y_ref.shape[1]
     fetch(((x_hbm, x_ref), (y_hbm, y_ref), (a_hbm, r_s), (b_hbm, t_s)), sem)
@@ -228,53 +228,41 @@
     term[...] = new_ref[...] / EPS + jnp.log(mass_ref[...])
 
 
-def cols_kernel(k_ref, x_hbm, y_hbm, f_ref, rl_ref, a_ref, fn_ref, col_ref, ub, r_s, x_ref, y_ref, sem, *, rows):
+def sums_kernel(
+    k_ref, x_ref, y_ref, f_ref, g_ref, rl_ref, cl_ref, a_ref, b_ref,
+    fn_ref, gn_ref, row_ref, col_ref, vs, r_s, t_s, ub,
+):
     update(f_ref, rl_ref, a_ref, fn_ref, r_s)
-    u, r_top, fine = factors(r_s[...])
-    spread(u, ub)
+    update(g_ref, cl_ref, b_ref, gn_ref, t_s)
+    u, r_top, u_fine = factors(r_s[...])
+    v, t_top, v_fine = factors(t_s[...])
+    row_ref[...] = u
+    vs[...] = v
     ns, nt = k_ref.shape
     tiles = nt // LANES
 
     def block(rb, cs):
-        at = pl.ds(pl.multiple_of(rb * rows, rows), rows)
-        ur = ub[at, :]
-        return tuple(
-            cs[c] + fold(k_ref[at, c * LANES : (c + 1) * LANES] * ur) for c in range(tiles)
-        )
-
-    cs = lax.fori_loop(0, ns // rows, block, (jnp.zeros((8, LANES), F32),) * tiles)
+        at = pl.ds(pl.multiple_of(rb * LANES, LANES), LANES)
+        ur = jnp.broadcast_to(row_ref[pl.ds(rb, 1), :], (LANES, LANES)).T
+        total = jnp.zeros((LANES, LANES), F32)
+        out = []
+        for c in range(tiles):
+            k = k_ref[at, c * LANES : (c + 1) * LANES]
+            total += k * vs[c : c + 1, :]
+            out.append(cs[c] + fold(k * ur))
+        row_ref[pl.ds(rb, 1), :] = jnp.sum(total.T, axis=0, keepdims=True)
+        return tuple(out)
+
+    cs = lax.fori_loop(0, ns // LANES, block, (jnp.zeros((8, LANES), F32),) * tiles, unroll=2)
     for c in range(tiles):
         col_ref[c : c + 1, :] = jnp.sum(cs[c], axis=0, keepdims=True)
-    fine = finish(col_ref, r_top, fine)
-
-    @pl.when(jnp.logical_not(fine))
+    rows_fine = finish(row_ref, t_top, v_fine)
+    cols_fine = finish(col_ref, r_top, u_fine)
+
+    @pl.when(jnp.logical_not(rows_fine & cols_fine))
     def _():
-        fetch(((x_hbm, x_ref), (y_hbm, y_ref)), sem)
+        rows_sweep(x_ref, y_ref, t_s, row_ref, None)
         cols_sweep(x_ref, y_ref, r_s, col_ref, None, ub)
-
-
-def rows_kernel(k_ref, x_hbm, y_hbm, g_ref, cl_ref, b_ref, gn_ref, row_ref, acc, vs, t_s, x_ref, y_ref, sem, *, rows):
-    update(g_ref, cl_ref, b_ref, gn_ref, t_s)
-    v, t_top, fine = factors(t_s[...])
-    vs[...] = v
-    ns, nt = k_ref.shape
-
-    def block(rb, _):
-        at = pl.ds(pl.multiple_of(rb * rows, rows), rows)
-        total = jnp.zeros((rows, LANES), F32)
-        for c in range(nt // LANES):
-            total += k_ref[at, c * LANES : (c + 1) * LANES] * vs[c : c + 1, :]
-        acc[at, :] = total
-        return 0
-
-    lax.fori_loop(0, ns // rows, block, 0)
-    lane_sums(acc, row_ref)
-    fine = finish(row_ref, t_top, fine)
-
-    @pl.when(jnp.logical_not(fine))
-    def _():
-        fetch(((x_hbm, x_ref), (y_hbm, y_ref)), sem)
-        rows_sweep(x_ref, y_ref, t_s, row_ref, None)
 
 
 def weight_rows(out, lse):
@@ -288,64 +276,34 @@
     return k1, (k - k1.astype(F32)).astype(BF16)
 
 
-def cols_map_kernel(k_ref, x_ref, y_ref, f_ref, rl_ref, a_ref, fn_ref, out_ref, lse, ub, xu, cacc, r_s, *, rows):
+def maps_kernel(
+    k_ref, x_ref, y_ref, f_ref, g_ref, rl_ref, cl_ref, a_ref, b_ref,
+    fn_ref, gn_ref, rowm_ref, colm_ref, row_s, col_s, ub, wy, xu, acc, cacc, r_s, t_s, *, rows,
+):
     d = x_ref.shape[0]
     ns, nt = k_ref.shape
     update(f_ref, rl_ref, a_ref, fn_ref, r_s)
-    u, r_top, fine = factors(r_s[...])
+    update(g_ref, cl_ref, b_ref, gn_ref, t_s)
+    u, r_top, u_fine = factors(r_s[...])
+    v, t_top, v_fine = factors(t_s[...])
+    lane = lax.broadcasted_iota(jnp.int32, (LANES, 2 * d), 1)
     sub = lax.broadcasted_iota(jnp.int32, (16, LANES), 0)
+    for b in range(nt // LANES):
+        at = slice(b * LANES, (b + 1) * LANES)
+        vb = v[b : b + 1, :]
+        yb = y_ref[:, at] * vb
+        p1, p2 = split2(jnp.concatenate([yb, yb], axis=0).T)
+        wy[at, 0 : 2 * d] = jnp.where(lane < d, p1, p2).astype(BF16)
+        p1, p2 = split2(jnp.broadcast_to(vb, (2 * d, LANES)).T)
+        wy[at, 2 * d : 4 * d] = jnp.where(lane == 0, p1, jnp.where(lane == 1, p2, 0.0)).astype(BF16)
     for b in range(ns // LANES):
         at = slice(b * LANES, (b + 1) * LANES)
-        ur = u[b : b + 1, :]
-        p1, p2 = split2(x_ref[:, at] * ur)
+        uv = u[b : b + 1, :]
+        p1, p2 = split2(x_ref[:, at] * uv)
         xu[0:d, at] = p1.astype(BF16)
         xu[d : 2 * d, at] = p2.astype(BF16)
-        p1, p2 = split2(jnp.broadcast_to(ur, (16, LANES)))
+        p1, p2 = split2(jnp.broadcast_to(uv, (16, LANES)))
         xu[2 * d : 2 * d + 16, at] = jnp.where(sub == 0, p1, jnp.where(sub == 1, p2, 0.0)).astype(BF16)
-    wide = 2 * LANES
-
-    def block(cb, _):
-        at = pl.multiple_of(cb * wide, wide)
-        total = jnp.zeros((xu.shape[0], wide), F32)
-        for r in range(0, ns, rows):
-            xr = xu[:, r : r + rows]
-            total += jnp.dot(
-                jnp.concatenate([xr, xr], axis=1),
-                jnp.concatenate(parts_of(k_ref[r : r + rows, pl.ds(at, wide)]), axis=0),
-                preferred_element_type=F32,
-            )
-        cacc[:, pl.ds(at, wide)] = total
-        return 0
-
-    lax.fori_loop(0, nt // wide, block, 0)
-    for b in range(nt // LANES):
-        at = slice(b * LANES, (b + 1) * LANES)
-        den = cacc[2 * d : 2 * d + 1, at] + cacc[2 * d + 1 : 2 * d + 2, at]
-        out_ref[0:d, at] = (cacc[0:d, at] + cacc[d : 2 * d, at]) / den
-        lse[b : b + 1, :] = den
-    fine = finish(lse, r_top, fine)
-
-    @pl.when(jnp.logical_not(fine))
-    def _():
-        cols_sweep(x_ref, y_ref, r_s, lse, out_ref, ub)
-
-    weight_rows(out_ref, lse)
-
-
-def rows_map_kernel(k_ref, x_ref, y_ref, g_ref, cl_ref, b_ref, gn_ref, out_ref, lse, wy, acc, t_s, *, rows):
-    d = x_ref.shape[0]
-    ns, nt = k_ref.shape
-    update(g_ref, cl_ref, b_ref, gn_ref, t_s)
-    v, t_top, fine = factors(t_s[...])
-    lane = lax.broadcasted_iota(jnp.int32, (LANES, 2 * d), 1)
-    for b in range(nt // LANES):
-        at = slice(b * LANES, (b + 1) * LANES)
-        vr = v[b : b + 1, :]
-        yb = y_ref[:, at] * vr
-        p1, p2 = split2(jnp.concatenate([yb, yb], axis=0).T)
-        wy[at, 0 : 2 * d] = jnp.where(lane < d, p1, p2).astype(BF16)
-        p1, p2 = split2(jnp.broadcast_to(vr, (2 * d, LANES)).T)
-        wy[at, 2 * d : 4 * d] = jnp.where(lane == 0, p1, jnp.where(lane == 1, p2, 0.0)).astype(BF16)
     wide = 2 * LANES
     acc[...] = jnp.zeros_like(acc)
 
@@ -353,9 +311,21 @@
         at = pl.multiple_of(cb * wide, wide)
         w = wy[pl.ds(at, wide), :]
         ww = jnp.concatenate([w, w], axis=0)
+        total = jnp.zeros((xu.shape[0], wide), F32)
         for r in range(0, ns, rows):
-            k = jnp.concatenate(parts_of(k_ref[r : r + rows, pl.ds(at, wide)]), axis=1)
-            acc[r : r + rows, :] += jnp.dot(k, ww, preferred_element_type=F32)
+            k = k_ref[r : r + rows, pl.ds(at, wide)]
+            k1 = k.astype(BF16)
+            k2 = (k - k1.astype(F32)).astype(BF16)
+            acc[r : r + rows, :] += jnp.dot(
+                jnp.concatenate([k1, k2], axis=1), ww, preferred_element_type=F32
+            )
+            xr = xu[:, r : r + rows]
+            total += jnp.dot(
+                jnp.concatenate([xr, xr], axis=1),
+                jnp.concatenate([k1, k2], axis=0),
+                preferred_element_type=F32,
+            )
+        cacc[:, pl.ds(at, wide)] = total
         return 0
 
     lax.fori_loop(0, nt // wide, block, 0)
@@ -364,15 +334,23 @@
         num = acc[at, 0 : 2 * d].T
         den = acc[at, 2 * d : 4 * d].T
         den = den[0:1, :] + den[1:2, :]
-        out_ref[0:d, at] = (num[0:d, :] + num[d : 2 * d, :]) / den
-        lse[b : b + 1, :] = den
-    fine = finish(lse, t_top, fine)
-
-    @pl.when(jnp.logical_not(fine))
+        rowm_ref[0:d, at] = (num[0:d, :] + num[d : 2 * d, :]) / den
+        row_s[b : b + 1, :] = den
+    for b in range(nt // LANES):
+        at = slice(b * LANES, (b + 1) * LANES)
+        den = cacc[2 * d : 2 * d + 1, at] + cacc[2 * d + 1 : 2 * d + 2, at]
+        colm_ref[0:d, at] = (cacc[0:d, at] + cacc[d : 2 * d, at]) / den
+        col_s[b : b + 1, :] = den
+    rows_fine = finish(row_s, t_top, v_fine)
+    cols_fine = finish(col_s, r_top, u_fine)
+
+    @pl.when(jnp.logical_not(rows_fine & cols_fine))
     def _():
-        rows_sweep(x_ref, y_ref, t_s, lse, out_ref)
-
-    weight_rows(out_ref, lse)
+        rows_sweep(x_ref, y_ref, t_s, row_s, rowm_ref)
+        cols_sweep(x_ref, y_ref, r_s, col_s, colm_ref, ub)
+
+    weight_rows(rowm_ref, row_s)
+    weight_rows(colm_ref, col_s)
 
 
 def merge_kernel(at_ref, whole, *refs, place):
@@ -416,8 +394,9 @@
 
 
 VM = pl.BlockSpec(memory_space=pltpu.VMEM)
-ANY = pl.BlockSpec(memory_space=pl.ANY)
+ANY = pl.BlockSpec(memory_space=pltpu.HBM)
 PARAMS = pltpu.CompilerParams(vmem_limit_bytes=24 * 2**20)
+FULL = pltpu.CompilerParams(vmem_limit_bytes=46 * 2**20 + 3 * 2**18)
 
 
 def cost(flops, size):
@@ -426,6 +405,10 @@
 
 def vector(n):
     return jax.ShapeDtypeStruct((n // LANES, LANES), F32)
+
+
+def near(n):
+    return pltpu.VMEM((n // LANES, LANES), F32)
 
 
 def scratch(n):
@@ -437,12 +420,16 @@
     nt = y.shape[1]
     return pl.pallas_call(
         functools.partial(form_kernel, rows=256),
-        out_shape=(pltpu.VMEM((ns, nt), F32), vector(ns), vector(nt)),
-        in_specs=[ANY] * 4,
-        out_specs=(VM,) * 3,
-        scratch_shapes=[
+        out_shape=(
+            pltpu.VMEM((ns, nt), F32),
             pltpu.VMEM((d, ns), F32),
             pltpu.VMEM((d, nt), F32),
+            near(ns),
+            near(nt),
+        ),
+        in_specs=[ANY] * 4,
+        out_specs=(VM,) * 5,
+        scratch_shapes=[
             pltpu.VMEM((ns, 8 * d), BF16),
             pltpu.VMEM((8 * d, nt), BF16),
             pltpu.VMEM((ns, LANES), F32),
@@ -451,84 +438,54 @@
             scratch(nt),
             pltpu.SemaphoreType.DMA((4,)),
         ],
-        compiler_params=PARAMS,
+        compiler_params=FULL,
         cost_estimate=cost(20 * d * ns * nt, 4 * ns * nt),
         name="form",
     )(x, y, a, b)
 
 
-def sweep_scratch(d, ns, nt):
-    return [pltpu.VMEM((d, ns), F32), pltpu.VMEM((d, nt), F32), pltpu.SemaphoreType.DMA((2,))]
-
-
-def cols_sums(k, x, y, f, row_lse, a):
+def sums(k, x, y, *vectors):
     ns, nt = k.shape
     return pl.pallas_call(
-        functools.partial(cols_kernel, rows=64),
-        out_shape=(vector(ns), vector(nt)),
-        in_specs=[VM, ANY, ANY, VM, VM, VM],
-        out_specs=(VM,) * 2,
-        scratch_shapes=[pltpu.VMEM((ns, LANES), F32), scratch(ns)] + sweep_scratch(x.shape[0], ns, nt),
+        sums_kernel,
+        out_shape=(near(ns), near(nt), near(ns), near(nt)),
+        in_specs=[VM] * 9,
+        out_specs=(VM,) * 4,
+        scratch_shapes=[scratch(nt), scratch(ns), scratch(nt), pltpu.VMEM((ns, LANES), F32)],
         compiler_params=PARAMS,
-        cost_estimate=cost(2 * ns * nt, 2 * ns * nt),
-        name="cols_sums",
-    )(k, x, y, f, row_lse, a)
-
-
-def rows_sums(k, x, y, g, col_lse, b):
-    ns, nt = k.shape
-    return pl.pallas_call(
-        functools.partial(rows_kernel, rows=64),
-        out_shape=(vector(nt), vector(ns)),
-        in_specs=[VM, ANY, ANY, VM, VM, VM],
-        out_specs=(VM,) * 2,
-        scratch_shapes=[pltpu.VMEM((ns, LANES), F32), scratch(nt), scratch(nt)]
-        + sweep_scratch(x.shape[0], ns, nt),
-        compiler_params=PARAMS,
-        cost_estimate=cost(2 * ns * nt, 2 * ns * nt),
-        name="rows_sums",
-    )(k, x, y, g, col_lse, b)
-
-
-def cols_map(k, x, y, f, row_lse, a):
+        cost_estimate=cost(4 * ns * nt, 4 * ns * nt),
+        name="sums",
+    )(k, x, y, *vectors)
+
+
+def maps(k, x, y, *vectors):
     d = x.shape[0]
     ns, nt = k.shape
     return pl.pallas_call(
-        functools.partial(cols_map_kernel, rows=512),
-        out_shape=(vector(ns), jax.ShapeDtypeStruct((d + 8, nt), F32)),
-        in_specs=[VM] * 6,
-        out_specs=(VM,) * 2,
+        functools.partial(maps_kernel, rows=512),
+        out_shape=(
+            vector(ns),
+            vector(nt),
+            jax.ShapeDtypeStruct((d + 8, ns), F32),
+            jax.ShapeDtypeStruct((d + 8, nt), F32),
+        ),
+        in_specs=[VM] * 9,
+        out_specs=(VM,) * 4,
         scratch_shapes=[
+            scratch(ns),
             scratch(nt),
             pltpu.VMEM((ns, LANES), F32),
+            pltpu.VMEM((nt, 4 * d), BF16),
             pltpu.VMEM((2 * d + 16, ns), BF16),
+            pltpu.VMEM((ns, 4 * d), F32),
             pltpu.VMEM((2 * d + 16, nt), F32),
             scratch(ns),
-        ],
-        compiler_params=PARAMS,
-        cost_estimate=cost(16 * d * ns * nt, 4 * ns * nt),
-        name="cols_map",
-    )(k, x, y, f, row_lse, a)
-
-
-def rows_map(k, x, y, g, col_lse, b):
-    d = x.shape[0]
-    ns, nt = k.shape
-    return pl.pallas_call(
-        functools.partial(rows_map_kernel, rows=512),
-        out_shape=(vector(nt), jax.ShapeDtypeStruct((d + 8, ns), F32)),
-        in_specs=[VM] * 6,
-        out_specs=(VM,) * 2,
-        scratch_shapes=[
-            scratch(ns),
-            pltpu.VMEM((nt, 4 * d), BF16),
-            pltpu.VMEM((ns, 4 * d), F32),
             scratch(nt),
         ],
         compiler_params=PARAMS,
-        cost_estimate=cost(16 * d * ns * nt, 4 * ns * nt),
-        name="rows_map",
-    )(k, x, y, g, col_lse, b)
+        cost_estimate=cost(32 * d * ns * nt, 4 * ns * nt),
+        name="maps",
+    )(k, x, y, *vectors)
 
 
 def merge(at, place, whole, others, keep):
@@ -572,13 +529,28 @@
     return part
 
 
+def partner(place, k, group):
+    return place ^ k if group & (group - 1) == 0 else (place + k) % group
+
+
+def source(place, k, group):
+    return place ^ k if group & (group - 1) == 0 else (place - k) % group
+
+
 def pairs(n, group, stride, k):
-    return [(i, i + (((i // stride) + k) % group - (i // stride) % group) * stride) for i in range(n)]
+    out = []
+    for i in range(n):
+        place = (i // stride) % group
+        out.append((i, i + (partner(place, k, group) - place) * stride))
+    return out
 
 
 def places(index, group, stride, width):
     own = (index // stride) % group
-    return [(own + k) % group * width for k in range(group)]
+    return (
+        [partner(own, k, group) * width for k in range(group)],
+        [source(own, k, group) * width for k in range(group)],
+    )
 
 
 def piece(a, at, count):
@@ -588,13 +560,12 @@
     )
 
 
-def merged_piece(axis, place, stride, part, at, own):
+def pieces_of(axis, place, stride, part):
     n, group = lax.axis_size(axis), len(place)
-    got = [
+    return [
         lax.ppermute(piece(part, place[k], group), axis, pairs(n, group, stride, k))
         for k in range(1, group)
     ]
-    return merge(at, own, part, got, False)
 
 
 def all_pieces(axis, group, stride, own):
@@ -606,35 +577,39 @@
     rows, cols = lax.axis_size("row"), lax.axis_size("col")
     ns, nt = sources.shape[1], targets.shape[1]
     index = lax.axis_index("row")
-    halves = places(index, 2, 1, nt // 2)
-    row_places = places(index, rows // 2, 2, nt // rows)
-    col_places = places(lax.axis_index("col"), cols, 1, ns // cols)
-    laid = [half + row_places[-k] for half in halves for k in range(rows // 2)]
-    laid = [halves[0], row_places[0], col_places[0]] + laid + [col_places[-k] for k in range(cols)]
+    halves, _ = places(index, 2, 1, nt // 2)
+    row_places, row_sources = places(index, rows // 2, 2, nt // rows)
+    col_places, col_sources = places(lax.axis_index("col"), cols, 1, ns // cols)
+    laid = [halves[0], row_places[0], col_places[0]]
+    laid += [half + at for half in halves for at in row_sources] + col_sources
     laid = jnp.stack(laid)
     sources, halves, row_places, col_places, laid = lax.optimization_barrier(
         (sources, halves, row_places, col_places, laid)
     )
-    x, y = sources, targets
     a = source_mass.reshape(-1, LANES)
     b = target_mass.reshape(-1, LANES)
     f = jnp.zeros_like(a)
     g = jnp.zeros_like(b)
-    k, row_part, col_part = form(x, y, a, b)
+    k, x, y, row_part, col_part = form(sources, targets, a, b)
     for sweep in range(ITERS):
         row_lse = lse_over("col", row_part)
         col_lse = lse_over("row", col_part)
-        last = sweep == ITERS - 1
-        f, col_part = (cols_map if last else cols_sums)(k, x, y, f, row_lse, a)
-        g, row_part = (rows_map if last else rows_sums)(k, x, y, g, col_lse, b)
+        if sweep < ITERS - 1:
+            f, g, row_part, col_part = sums(k, x, y, f, g, row_lse, col_lse, a, b)
+    f, g, row_part, col_part = maps(k, x, y, f, g, row_lse, col_lse, a, b)
     pair = pairs(rows, 2, 1, 1)
     other = lax.ppermute(piece(col_part, halves[1], 2), "row", pair)
     chip = merge(laid, 0, col_part, [other], True)
-    ours = merged_piece("row", row_places, 2, chip, laid, 1)
-    ours = jnp.concatenate(all_pieces("row", rows // 2, 2, ours), axis=0)
+    chip, row_part = lax.optimization_barrier((chip, row_part))
+    parted = (pieces_of("row", row_places, 2, chip), pieces_of("col", col_places, 1, row_part))
+    column_pieces, row_pieces = lax.optimization_barrier(parted)
+    ours = merge(laid, 1, chip, column_pieces, False)
+    own = merge(laid, 2, row_part, row_pieces, False)
+    ours, own = lax.optimization_barrier((ours, own))
+    whole = (all_pieces("row", rows // 2, 2, ours), all_pieces("col", cols, 1, own))
+    column_pieces, source_pieces = lax.optimization_barrier(whole)
+    ours = jnp.concatenate(column_pieces, axis=0)
     theirs = lax.ppermute(ours, "row", pair)
-    own = merged_piece("col", col_places, 1, row_part, laid, 2)
-    source_pieces = all_pieces("col", cols, 1, own)
     target_map, source_map = join(laid, ours, theirs, source_pieces)
     return f.reshape(-1), g.reshape(-1), source_map, target_map
 

time: 303 us -> 297 us (0.980)
  Pallas kernels: 242 us -> 237 us
  local copies, waits for them, and re-layouts: 4.05 us -> 0.6 us
    pallas_call x6 -> x3, Pallas kernels: 191 us -> 184 us  [the longest x1 97.9 us: maps(): pl.pallas_call(functools.partial(maps_kernel, rows=512), out_shape=(vecto...]
    unnamed x16 -> x7, local copies, waits for them, and re-layouts: 3.5 us -> 0.03 us
  transfers between devices with their start and end apart: 29 -> 29, of which waited for: 13 -> 17; matrix products, arithmetic and copies ran while one was open for 0% -> 0% of each run, Pallas kernels for 63% -> 0%
where the time goes in v4:
time: 297 us
  Pallas kernels  237 us (80%)
  starting transfers between devices  38.3 us (13%)
  waiting for transfers between devices  19.5 us (7%)
    pallas_call x1, Pallas kernels, maps(): pl.pallas_call(functools.partial(maps_kernel, rows=512), out_shape=(vecto...  97.9 us
    pallas_call x2, Pallas kernels, sums(): pl.pallas_call(sums_kernel, out_shape=(near(ns), near(nt), near(ns), near...  86.4 us
    pallas_call x1, Pallas kernels, form(): pl.pallas_call(functools.partial(form_kernel, rows=256), out_shape=(pltpu...  49.1 us
    ppermute x15, starting transfers between devices, lse_over(): lax.ppermute(part, axis, [(i, i ^ step) for i in range(n)])  23.2 us
    ppermute x6, starting transfers between devices, pieces_of(): lax.ppermute(piece(part, place[k], group), axis, pairs(n, group, stride, k))  8.01 us
    ppermute x15, waiting for transfers between devices, lse_over(): lax.ppermute(part, axis, [(i, i ^ step) for i in range(n)])  7.75 us
    ppermute x6, starting transfers between devices, all_pieces(): lax.ppermute(own, axis, pairs(n, group, stride, k))  6.82 us
  transfers between devices with their start and end apart: 29, of which 17 were waited for; matrix products, arithmetic and copies ran while one was open for 0% of the time, Pallas kernels for 0%

profile of v4, /device:TPU:0, one launch (start us, length us, event | category | flops | bytes accessed | tf_op | source)
XLA Modules:
  0.0 296.5 jit_solution(14892028811971405983)
XLA Ops:
  0.8 49.1 %form.1 = (f32[2048,2048]{1,0:T(8,128)S(1)}, f32[64,2048]{1,0:T(8,128)S(1)}, f32[64,2048]{1,0:T(8,128)S(1)}, f32[16,128]{1,0:T(8,128)S(1)}, f32[16,128]{1,0:T(8,128)S(1)}) custom-call(f32[64,2048]{1,0:T(8,128)} %x_hbm, f32[64,2048]{1,0:T(8,128)} %y_hbm.1, f32[16,128]{1,0:T(8,128)} %bitcast.18, f32[16,128]{1,0:T(8,128)} %bitcast.22), custom_call_target="tpu_custom_call" | custom-call | flops 5368709120 | bytes 16777216 | tf_op jit(solution)/shard_map/form/pallas_call | solution.py:421
  49.9 4.1 %collective-permute-start.2 = (f32[16,128]{1,0:T(8,128)S(1)}, f32[16,128]{1,0:T(8,128)S(1)}, u32[]{:S(2)}, u32[]{:S(2)}) collective-permute-start(f32[16,128]{1,0:T(8,128)S(1)} %get-tuple-element.55), channel_id=1, source_target_pairs={{0,16},{4,20},{8,24},{12,28},{16,0},{20,4},{24,8},{28,12},{1,17},{... | collective-permute-start | bytes 24584 | tf_op jit(solution)/shard_map/ppermute | solution.py:527
  54.0 1.5 collective-permute-start
  55.7 2.0 collective-permute-start.3
  57.7 1.6 collective-permute-start.1
  59.5 1.9 collective-permute-done.1
  61.5 43.1 %sums.2 = (f32[16,128]{1,0:T(8,128)S(1)}, f32[16,128]{1,0:T(8,128)S(1)}, f32[16,128]{1,0:T(8,128)S(1)}, f32[16,128]{1,0:T(8,128)S(1)}) custom-call(f32[2048,2048]{1,0:T(8,128)S(1)} %get-tuple-element.51.k_ref, f32[64,2048]{1,0:T(8,128)S(1)} %get-tuple-element.52.x_ref, f32[64,2048]{1,0:T(8,128)S(1)} %get-tuple-element.53.y_ref, ...), custom_call_target="tpu_custom_call" | custom-call | flops 16777216 | bytes 16777216 | tf_op jit(solution)/shard_map/sums/pallas_call | solution.py:449
  104.6 2.6 collective-permute-start.7
  109.2 1.6 collective-permute-start.8
  110.9 1.6 collective-permute-start.6
  113.1 1.6 collective-permute-done.6
  114.7 43.3 %sums.3 = (f32[16,128]{1,0:T(8,128)S(1)}, f32[16,128]{1,0:T(8,128)S(1)}, f32[16,128]{1,0:T(8,128)S(1)}, f32[16,128]{1,0:T(8,128)S(1)}) custom-call(f32[2048,2048]{1,0:T(8,128)S(1)} %get-tuple-element.51.k_ref, f32[64,2048]{1,0:T(8,128)S(1)} %get-tuple-element.52.x_ref, f32[64,2048]{1,0:T(8,128)S(1)} %get-tuple-element.53.y_ref, ...), custom_call_target="tpu_custom_call" | custom-call | flops 16777216 | bytes 16777216 | tf_op jit(solution)/shard_map/sums/pallas_call | solution.py:449
  158.0 2.2 collective-permute-start.12
  163.8 1.6 collective-permute-start.11
  167.6 97.9 %maps.1 = (f32[16,128]{1,0:T(8,128)}, f32[16,128]{1,0:T(8,128)}, f32[72,2048]{1,0:T(8,128)S(1)}, f32[72,2048]{1,0:T(8,128)S(1)}) custom-call(f32[2048,2048]{1,0:T(8,128)S(1)} %get-tuple-element.51.k_ref, f32[64,2048]{1,0:T(8,128)S(1)} %get-tuple-element.52.x_ref, f32[64,2048]{1,0:T(8,128)S(1)} %get-tuple-element.53.y_ref, ...), custom_call_target="tpu_custom_call" | custom-call | flops 8589934592 | bytes 16777216 | tf_op jit(solution)/shard_map/maps/pallas_call | solution.py:464
  268.0 2.8 collective-permute-start.18
  271.0 2.5 collective-permute-start.21
  274.6 1.7 collective-permute-start.16
  276.2 4.1 %collective-permute-done.17.refs_1_ = f32[72,256]{1,0:T(8,128)S(1)} collective-permute-done((f32[72,256]{1,0:T(8,128)S(1)}, f32[72,256]{1,0:T(8,128)S(1)}, u32[]{:S(2)}, u32[]{:S(2)}) %collective-permute-start.17) | collective-permute-done | bytes 73760 | tf_op jit(solution)/shard_map/ppermute | solution.py:566
  283.2 2.4 collective-permute-start.27
  288.2 1.8 collective-permute-start.22
  290.0 2.6 collective-permute-done.23
  293.3 1.5 collective-permute-done.28.theirs
  294.8 1.6 join.1
  (70 shorter events, 18.9 us)
Async XLA Ops:
  49.9 5.7 %collective-permute-start.2 = (f32[16,128]{1,0:T(8,128)S(1)}, f32[16,128]{1,0:T(8,128)S(1)}, u32[]{:S(2)}, u32[]{:S(2)}) collective-permute-start(f32[16,128]{1,0:T(8,128)S(1)} %get-tuple-element.55), channel_id=1, source_target_pairs={{0,16},{4,20},{8,24},{12,28},{16,0},{20,4},{24,8},{28,12},{1,17},{... | collective-permute-start | bytes 24584 | tf_op jit(solution)/shard_map/ppermute | solution.py:527
  54.0 3.7 %collective-permute-start = (f32[16,128]{1,0:T(8,128)S(1)}, f32[16,128]{1,0:T(8,128)S(1)}, u32[]{:S(2)}, u32[]{:S(2)}) collective-permute-start(f32[16,128]{1,0:T(8,128)S(1)} %get-tuple-element.54), channel_id=1, source_target_pairs={{0,2},{1,3},{2,0},{3,1},{4,6},{5,7},{6,4},{7,5},{8,10},{9,11},{10,... | collective-permute-start | bytes 24584 | tf_op jit(solution)/shard_map/ppermute | solution.py:527
  55.7 3.7 %collective-permute-start.3 = (f32[16,128]{1,0:T(8,128)S(1)}, f32[16,128]{1,0:T(8,128)S(1)}, u32[]{:S(2)}, u32[]{:S(2)}) collective-permute-start(f32[16,128]{1,0:T(8,128)S(1)} %log_add_fusion.12), channel_id=1, source_target_pairs={{0,8},{4,12},{8,0},{12,4},{16,24},{20,28},{24,16},{28,20},{1,9},{5... | collective-permute-start | bytes 24584 | tf_op jit(solution)/shard_map/ppermute | solution.py:527
  57.7 3.7 %collective-permute-start.1 = (f32[16,128]{1,0:T(8,128)S(1)}, f32[16,128]{1,0:T(8,128)S(1)}, u32[]{:S(2)}, u32[]{:S(2)}) collective-permute-start(f32[16,128]{1,0:T(8,128)S(1)} %log_add_fusion.14), channel_id=1, source_target_pairs={{0,1},{1,0},{2,3},{3,2},{4,5},{5,4},{6,7},{7,6},{8,9},{9,8},{10,11... | collective-permute-start | bytes 24584 | tf_op jit(solution)/shard_map/ppermute | solution.py:527
  104.6 4.6 %collective-permute-start.7 = (f32[16,128]{1,0:T(8,128)S(1)}, f32[16,128]{1,0:T(8,128)S(1)}, u32[]{:S(2)}, u32[]{:S(2)}) collective-permute-start(f32[16,128]{1,0:T(8,128)S(1)} %get-tuple-element.59), channel_id=1, source_target_pairs={{0,16},{4,20},{8,24},{12,28},{16,0},{20,4},{24,8},{28,12},{1,17},{... | collective-permute-start | bytes 24584 | tf_op jit(solution)/shard_map/ppermute | solution.py:527
  107.2 3.7 %collective-permute-start.5 = (f32[16,128]{1,0:T(8,128)S(1)}, f32[16,128]{1,0:T(8,128)S(1)}, u32[]{:S(2)}, u32[]{:S(2)}) collective-permute-start(f32[16,128]{1,0:T(8,128)S(1)} %get-tuple-element.58), channel_id=1, source_target_pairs={{0,2},{1,3},{2,0},{3,1},{4,6},{5,7},{6,4},{7,5},{8,10},{9,11},{10,... | collective-permute-start | bytes 24584 | tf_op jit(solution)/shard_map/ppermute | solution.py:527
  109.2 3.7 %collective-permute-start.8 = (f32[16,128]{1,0:T(8,128)S(1)}, f32[16,128]{1,0:T(8,128)S(1)}, u32[]{:S(2)}, u32[]{:S(2)}) collective-permute-start(f32[16,128]{1,0:T(8,128)S(1)} %log_add_fusion.7), channel_id=1, source_target_pairs={{0,8},{4,12},{8,0},{12,4},{16,24},{20,28},{24,16},{28,20},{1,9},{5... | collective-permute-start | bytes 24584 | tf_op jit(solution)/shard_map/ppermute | solution.py:527
  110.9 3.7 %collective-permute-start.6 = (f32[16,128]{1,0:T(8,128)S(1)}, f32[16,128]{1,0:T(8,128)S(1)}, u32[]{:S(2)}, u32[]{:S(2)}) collective-permute-start(f32[16,128]{1,0:T(8,128)S(1)} %log_add_fusion.9), channel_id=1, source_target_pairs={{0,1},{1,0},{2,3},{3,2},{4,5},{5,4},{6,7},{7,6},{8,9},{9,8},{10,11... | collective-permute-start | bytes 24584 | tf_op jit(solution)/shard_map/ppermute | solution.py:527
  158.0 4.6 %collective-permute-start.12 = (f32[16,128]{1,0:T(8,128)S(1)}, f32[16,128]{1,0:T(8,128)S(1)}, u32[]{:S(2)}, u32[]{:S(2)}) collective-permute-start(f32[16,128]{1,0:T(8,128)S(1)} %get-tuple-element.63), channel_id=1, source_target_pairs={{0,16},{4,20},{8,24},{12,28},{16,0},{20,4},{24,8},{28,12},{1,17},{... | collective-permute-start | bytes 24584 | tf_op jit(solution)/shard_map/ppermute | solution.py:527
  160.1 3.7 %collective-permute-start.10 = (f32[16,128]{1,0:T(8,128)S(1)}, f32[16,128]{1,0:T(8,128)S(1)}, u32[]{:S(2)}, u32[]{:S(2)}) collective-permute-start(f32[16,128]{1,0:T(8,128)S(1)} %get-tuple-element.62), channel_id=1, source_target_pairs={{0,2},{1,3},{2,0},{3,1},{4,6},{5,7},{6,4},{7,5},{8,10},{9,11},{10,... | collective-permute-start | bytes 24584 | tf_op jit(solution)/shard_map/ppermute | solution.py:527
  162.6 3.7 %collective-permute-start.13 = (f32[16,128]{1,0:T(8,128)S(1)}, f32[16,128]{1,0:T(8,128)S(1)}, u32[]{:S(2)}, u32[]{:S(2)}) collective-permute-start(f32[16,128]{1,0:T(8,128)S(1)} %log_add_fusion.2), channel_id=1, source_target_pairs={{0,8},{4,12},{8,0},{12,4},{16,24},{20,28},{24,16},{28,20},{1,9},{5... | collective-permute-start | bytes 24584 | tf_op jit(solution)/shard_map/ppermute | solution.py:527
  163.8 3.7 %collective-permute-start.11 = (f32[16,128]{1,0:T(8,128)S(1)}, f32[16,128]{1,0:T(8,128)S(1)}, u32[]{:S(2)}, u32[]{:S(2)}) collective-permute-start(f32[16,128]{1,0:T(8,128)S(1)} %log_add_fusion.4), channel_id=1, source_target_pairs={{0,1},{1,0},{2,3},{3,2},{4,5},{5,4},{6,7},{7,6},{8,9},{9,8},{10,11... | collective-permute-start | bytes 24584 | tf_op jit(solution)/shard_map/ppermute | solution.py:527
  268.0 6.5 %collective-permute-start.18 = (f32[72,256]{1,0:T(8,128)S(1)}, f32[72,256]{1,0:T(8,128)S(1)}, u32[]{:S(2)}, u32[]{:S(2)}) collective-permute-start(f32[72,256]{1,0:T(8,128)S(1)} %get-tuple-element.99), channel_id=1, source_target_pairs={{0,24},{4,28},{8,16},{12,20},{16,8},{20,12},{24,0},{28,4},{1,25},{... | collective-permute-start | bytes 221192 | tf_op jit(solution)/shard_map/ppermute | solution.py:566
  271.0 9.3 %collective-permute-start.21 = (f32[72,512]{1,0:T(8,128)S(1)}, f32[72,512]{1,0:T(8,128)S(1)}, u32[]{:S(2)}, u32[]{:S(2)}) collective-permute-start(f32[72,512]{1,0:T(8,128)S(1)} %get-tuple-element.96), channel_id=1, source_target_pairs={{0,3},{1,2},{2,1},{3,0},{4,7},{5,6},{6,5},{7,4},{8,11},{9,10},{10,... | collective-permute-start | bytes 442376 | tf_op jit(solution)/shard_map/ppermute | solution.py:566
  273.5 7.2 %collective-permute-start.20 = (f32[72,512]{1,0:T(8,128)S(1)}, f32[72,512]{1,0:T(8,128)S(1)}, u32[]{:S(2)}, u32[]{:S(2)}) collective-permute-start(f32[72,512]{1,0:T(8,128)S(1)} %get-tuple-element.97), channel_id=1, source_target_pairs={{0,2},{1,3},{2,0},{3,1},{4,6},{5,7},{6,4},{7,5},{8,10},{9,11},{10,... | collective-permute-start | bytes 442376 | tf_op jit(solution)/shard_map/ppermute | solution.py:566
  274.0 6.8 %collective-permute-start.19 = (f32[72,512]{1,0:T(8,128)S(1)}, f32[72,512]{1,0:T(8,128)S(1)}, u32[]{:S(2)}, u32[]{:S(2)}) collective-permute-start(f32[72,512]{1,0:T(8,128)S(1)} %get-tuple-element.98), channel_id=1, source_target_pairs={{0,1},{1,0},{2,3},{3,2},{4,5},{5,4},{6,7},{7,6},{8,9},{9,8},{10,11... | collective-permute-start | bytes 442376 | tf_op jit(solution)/shard_map/ppermute | solution.py:566
  274.5 5.8 %collective-permute-start.17 = (f32[72,256]{1,0:T(8,128)S(1)}, f32[72,256]{1,0:T(8,128)S(1)}, u32[]{:S(2)}, u32[]{:S(2)}) collective-permute-start(f32[72,256]{1,0:T(8,128)S(1)} %get-tuple-element.100), channel_id=1, source_target_pairs={{0,16},{4,20},{8,24},{12,28},{16,0},{20,4},{24,8},{28,12},{1,17},{... | collective-permute-start | bytes 221192 | tf_op jit(solution)/shard_map/ppermute | solution.py:566
  274.6 5.8 %collective-permute-start.16 = (f32[72,256]{1,0:T(8,128)S(1)}, f32[72,256]{1,0:T(8,128)S(1)}, u32[]{:S(2)}, u32[]{:S(2)}) collective-permute-start(f32[72,256]{1,0:T(8,128)S(1)} %get-tuple-element.101), channel_id=1, source_target_pairs={{0,8},{4,12},{8,0},{12,4},{16,24},{20,28},{24,16},{28,20},{1,9},{5... | collective-permute-start | bytes 221192 | tf_op jit(solution)/shard_map/ppermute | solution.py:566
  282.1 6.1 %collective-permute-start.24 = (f32[64,256]{1,0:T(8,128)S(1)}, f32[64,256]{1,0:T(8,128)S(1)}, u32[]{:S(2)}, u32[]{:S(2)}) collective-permute-start(f32[64,256]{1,0:T(8,128)S(1)} %merge.4), channel_id=1, source_target_pairs={{0,24},{4,28},{8,16},{12,20},{16,8},{20,12},{24,0},{28,4},{1,25},{... | collective-permute-start | bytes 196616 | tf_op jit(solution)/shard_map/ppermute | solution.py:573
  283.2 9.9 %collective-permute-start.27 = (f32[64,512]{1,0:T(8,128)S(1)}, f32[64,512]{1,0:T(8,128)S(1)}, u32[]{:S(2)}, u32[]{:S(2)}) collective-permute-start(f32[64,512]{1,0:T(8,128)S(1)} %merge.5.refs_0_), channel_id=1, source_target_pairs={{0,3},{1,2},{2,1},{3,0},{4,7},{5,6},{6,5},{7,4},{8,11},{9,10},{10,... | collective-permute-start | bytes 393224 | tf_op jit(solution)/shard_map/ppermute | solution.py:573
  285.7 7.5 %collective-permute-start.26 = (f32[64,512]{1,0:T(8,128)S(1)}, f32[64,512]{1,0:T(8,128)S(1)}, u32[]{:S(2)}, u32[]{:S(2)}) collective-permute-start(f32[64,512]{1,0:T(8,128)S(1)} %merge.5.refs_0_), channel_id=1, source_target_pairs={{0,2},{1,3},{2,0},{3,1},{4,6},{5,7},{6,4},{7,5},{8,10},{9,11},{10,... | collective-permute-start | bytes 393224 | tf_op jit(solution)/shard_map/ppermute | solution.py:573
  286.2 6.9 %collective-permute-start.25 = (f32[64,512]{1,0:T(8,128)S(1)}, f32[64,512]{1,0:T(8,128)S(1)}, u32[]{:S(2)}, u32[]{:S(2)}) collective-permute-start(f32[64,512]{1,0:T(8,128)S(1)} %merge.5.refs_0_), channel_id=1, source_target_pairs={{0,1},{1,0},{2,3},{3,2},{4,5},{5,4},{6,7},{7,6},{8,9},{9,8},{10,11... | collective-permute-start | bytes 393224 | tf_op jit(solution)/shard_map/ppermute | solution.py:573
  286.7 5.8 %collective-permute-start.23 = (f32[64,256]{1,0:T(8,128)S(1)}, f32[64,256]{1,0:T(8,128)S(1)}, u32[]{:S(2)}, u32[]{:S(2)}) collective-permute-start(f32[64,256]{1,0:T(8,128)S(1)} %merge.4), channel_id=1, source_target_pairs={{0,16},{4,20},{8,24},{12,28},{16,0},{20,4},{24,8},{28,12},{1,17},{... | collective-permute-start | bytes 196616 | tf_op jit(solution)/shard_map/ppermute | solution.py:573
  288.2 4.9 %collective-permute-start.22 = (f32[64,256]{1,0:T(8,128)S(1)}, f32[64,256]{1,0:T(8,128)S(1)}, u32[]{:S(2)}, u32[]{:S(2)}) collective-permute-start(f32[64,256]{1,0:T(8,128)S(1)} %merge.4), channel_id=1, source_target_pairs={{0,8},{4,12},{8,0},{12,4},{16,24},{20,28},{24,16},{28,20},{1,9},{5... | collective-permute-start | bytes 196616 | tf_op jit(solution)/shard_map/ppermute | solution.py:573
  (7 other events, 129.9 us)

commit v5 on v4

--- a/solution.py
+++ b/solution.py
@@ -276,71 +276,67 @@
     return k1, (k - k1.astype(F32)).astype(BF16)
 
 
+def weighted_points(points, factor, out):
+    d = points.shape[0]
+    sub = lax.broadcasted_iota(jnp.int32, (16, LANES), 0)
+    for b in range(factor.shape[0]):
+        at = slice(b * LANES, (b + 1) * LANES)
+        row = factor[b : b + 1, :]
+        p1, p2 = split2(points[:, at] * row)
+        out[0:d, at] = p1.astype(BF16)
+        out[d : 2 * d, at] = p2.astype(BF16)
+        p1, p2 = split2(jnp.broadcast_to(row, (16, LANES)))
+        out[2 * d : 2 * d + 16, at] = jnp.where(sub == 0, p1, jnp.where(sub == 1, p2, 0.0)).astype(BF16)
+
+
+def means(acc, out, total):
+    d = out.shape[0] - 8
+    for b in range(total.shape[0]):
+        at = slice(b * LANES, (b + 1) * LANES)
+        den = acc[2 * d : 2 * d + 1, at] + acc[2 * d + 1 : 2 * d + 2, at]
+        out[0:d, at] = (acc[0:d, at] + acc[d : 2 * d, at]) * (1.0 / den)
+        total[b : b + 1, :] = den
+
+
 def maps_kernel(
     k_ref, x_ref, y_ref, f_ref, g_ref, rl_ref, cl_ref, a_ref, b_ref,
-    fn_ref, gn_ref, rowm_ref, colm_ref, row_s, col_s, ub, wy, xu, acc, cacc, r_s, t_s, *, rows,
+    fn_ref, gn_ref, rowm_ref, colm_ref, row_s, col_s, ub, yv, xu, racc, cacc, r_s, t_s, *, rows,
 ):
-    d = x_ref.shape[0]
     ns, nt = k_ref.shape
     update(f_ref, rl_ref, a_ref, fn_ref, r_s)
     update(g_ref, cl_ref, b_ref, gn_ref, t_s)
     u, r_top, u_fine = factors(r_s[...])
     v, t_top, v_fine = factors(t_s[...])
-    lane = lax.broadcasted_iota(jnp.int32, (LANES, 2 * d), 1)
-    sub = lax.broadcasted_iota(jnp.int32, (16, LANES), 0)
-    for b in range(nt // LANES):
-        at = slice(b * LANES, (b + 1) * LANES)
-        vb = v[b : b + 1, :]
-        yb = y_ref[:, at] * vb
-        p1, p2 = split2(jnp.concatenate([yb, yb], axis=0).T)
-        wy[at, 0 : 2 * d] = jnp.where(lane < d, p1, p2).astype(BF16)
-        p1, p2 = split2(jnp.broadcast_to(vb, (2 * d, LANES)).T)
-        wy[at, 2 * d : 4 * d] = jnp.where(lane == 0, p1, jnp.where(lane == 1, p2, 0.0)).astype(BF16)
-    for b in range(ns // LANES):
-        at = slice(b * LANES, (b + 1) * LANES)
-        uv = u[b : b + 1, :]
-        p1, p2 = split2(x_ref[:, at] * uv)
-        xu[0:d, at] = p1.astype(BF16)
-        xu[d : 2 * d, at] = p2.astype(BF16)
-        p1, p2 = split2(jnp.broadcast_to(uv, (16, LANES)))
-        xu[2 * d : 2 * d + 16, at] = jnp.where(sub == 0, p1, jnp.where(sub == 1, p2, 0.0)).astype(BF16)
+    weighted_points(y_ref, v, yv)
+    weighted_points(x_ref, u, xu)
     wide = 2 * LANES
-    acc[...] = jnp.zeros_like(acc)
+    racc[...] = jnp.zeros_like(racc)
 
     def block(cb, _):
         at = pl.multiple_of(cb * wide, wide)
-        w = wy[pl.ds(at, wide), :]
-        ww = jnp.concatenate([w, w], axis=0)
+        yc = yv[:, pl.ds(at, wide)]
+        yc = jnp.concatenate([yc, yc], axis=1)
         total = jnp.zeros((xu.shape[0], wide), F32)
         for r in range(0, ns, rows):
-            k = k_ref[r : r + rows, pl.ds(at, wide)]
-            k1 = k.astype(BF16)
-            k2 = (k - k1.astype(F32)).astype(BF16)
-            acc[r : r + rows, :] += jnp.dot(
-                jnp.concatenate([k1, k2], axis=1), ww, preferred_element_type=F32
-            )
+            k1, k2 = parts_of(k_ref[r : r + rows, pl.ds(at, wide)])
             xr = xu[:, r : r + rows]
             total += jnp.dot(
                 jnp.concatenate([xr, xr], axis=1),
                 jnp.concatenate([k1, k2], axis=0),
                 preferred_element_type=F32,
             )
+            racc[:, r : r + rows] += lax.dot_general(
+                yc,
+                jnp.concatenate([k1, k2], axis=1),
+                (((1,), (1,)), ((), ())),
+                preferred_element_type=F32,
+            )
         cacc[:, pl.ds(at, wide)] = total
         return 0
 
     lax.fori_loop(0, nt // wide, block, 0)
-    for b in range(ns // LANES):
-        at = slice(b * LANES, (b + 1) * LANES)
-        num = acc[at, 0 : 2 * d].T
-        den = acc[at, 2 * d : 4 * d].T
-        den = den[0:1, :] + den[1:2, :]
-        rowm_ref[0:d, at] = (num[0:d, :] + num[d : 2 * d, :]) / den
-        row_s[b : b + 1, :] = den
-    for b in range(nt // LANES):
-        at = slice(b * LANES, (b + 1) * LANES)
-        den = cacc[2 * d : 2 * d + 1, at] + cacc[2 * d + 1 : 2 * d + 2, at]
-        colm_ref[0:d, at] = (cacc[0:d, at] + cacc[d : 2 * d, at]) / den
-        col_s[b : b + 1, :] = den
+    means(racc, rowm_ref, row_s)
+    means(cacc, colm_ref, col_s)
     rows_fine = finish(row_s, t_top, v_fine)
     cols_fine = finish(col_s, r_top, u_fine)
 
@@ -462,7 +458,7 @@
     d = x.shape[0]
     ns, nt = k.shape
     return pl.pallas_call(
-        functools.partial(maps_kernel, rows=512),
+        functools.partial(maps_kernel, rows=256),
         out_shape=(
             vector(ns),
             vector(nt),
@@ -475,9 +471,9 @@
             scratch(ns),
             scratch(nt),
             pltpu.VMEM((ns, LANES), F32),
-            pltpu.VMEM((nt, 4 * d), BF16),
+            pltpu.VMEM((2 * d + 16, nt), BF16),
             pltpu.VMEM((2 * d + 16, ns), BF16),
-            pltpu.VMEM((ns, 4 * d), F32),
+            pltpu.VMEM((2 * d + 16, ns), F32),
             pltpu.VMEM((2 * d + 16, nt), F32),
             scratch(ns),
             scratch(nt),
@@ -600,12 +596,11 @@
     pair = pairs(rows, 2, 1, 1)
     other = lax.ppermute(piece(col_part, halves[1], 2), "row", pair)
     chip = merge(laid, 0, col_part, [other], True)
-    chip, row_part = lax.optimization_barrier((chip, row_part))
     parted = (pieces_of("row", row_places, 2, chip), pieces_of("col", col_places, 1, row_part))
-    column_pieces, row_pieces = lax.optimization_barrier(parted)
+    column_pieces, row_pieces = parted
+    own = merge(laid, 2, row_part, row_pieces, False)
+    column_pieces, own = lax.optimization_barrier((column_pieces, own))
     ours = merge(laid, 1, chip, column_pieces, False)
-    own = merge(laid, 2, row_part, row_pieces, False)
-    ours, own = lax.optimization_barrier((ours, own))
     whole = (all_pieces("row", rows // 2, 2, ours), all_pieces("col", cols, 1, own))
     column_pieces, source_pieces = lax.optimization_barrier(whole)
     ours = jnp.concatenate(column_pieces, axis=0)

time: 297 us -> 294 us (0.990)
  transfers between devices with their start and end apart: 29 -> 29, of which waited for: 17 -> 15; matrix products, arithmetic and copies ran while one was open for 0% -> 0% of each run, Pallas kernels for 0% -> 0%
where the time goes in v5:
time: 294 us
  Pallas kernels  236 us (80%)
  starting transfers between devices  38.9 us (13%)
  waiting for transfers between devices  17.6 us (6%)
    pallas_call x1, Pallas kernels, maps(): pl.pallas_call(functools.partial(maps_kernel, rows=256), out_shape=(vecto...  96.9 us
    pallas_call x2, Pallas kernels, sums(): pl.pallas_call(sums_kernel, out_shape=(near(ns), near(nt), near(ns), near...  86.4 us
    pallas_call x1, Pallas kernels, form(): pl.pallas_call(functools.partial(form_kernel, rows=256), out_shape=(pltpu...  49.1 us
    ppermute x15, starting transfers between devices, lse_over(): lax.ppermute(part, axis, [(i, i ^ step) for i in range(n)])  23.2 us
    ppermute x6, starting transfers between devices, all_pieces(): lax.ppermute(own, axis, pairs(n, group, stride, k))  7.94 us
    ppermute x15, waiting for transfers between devices, lse_over(): lax.ppermute(part, axis, [(i, i ^ step) for i in range(n)])  7.75 us
    ppermute x6, starting transfers between devices, pieces_of(): lax.ppermute(piece(part, place[k], group), axis, pairs(n, group, stride, k))  7.48 us
  transfers between devices with their start and end apart: 29, of which 15 were waited for; matrix products, arithmetic and copies ran while one was open for 0% of the time, Pallas kernels for 0%

profile of v5, /device:TPU:0, one launch (start us, length us, event | category | flops | bytes accessed | tf_op | source)
XLA Modules:
  0.0 294.3 jit_solution(57678769928025538)
XLA Ops:
  0.8 49.1 %form.1 = (f32[2048,2048]{1,0:T(8,128)S(1)}, f32[64,2048]{1,0:T(8,128)S(1)}, f32[64,2048]{1,0:T(8,128)S(1)}, f32[16,128]{1,0:T(8,128)S(1)}, f32[16,128]{1,0:T(8,128)S(1)}) custom-call(f32[64,2048]{1,0:T(8,128)} %x_hbm, f32[64,2048]{1,0:T(8,128)} %y_hbm.1, f32[16,128]{1,0:T(8,128)} %bitcast.18, f32[16,128]{1,0:T(8,128)} %bitcast.22), custom_call_target="tpu_custom_call" | custom-call | flops 5368709120 | bytes 16777216 | tf_op jit(solution)/shard_map/form/pallas_call | solution.py:417
  49.9 4.1 %collective-permute-start.2 = (f32[16,128]{1,0:T(8,128)S(1)}, f32[16,128]{1,0:T(8,128)S(1)}, u32[]{:S(2)}, u32[]{:S(2)}) collective-permute-start(f32[16,128]{1,0:T(8,128)S(1)} %get-tuple-element.49), channel_id=1, source_target_pairs={{0,16},{4,20},{8,24},{12,28},{16,0},{20,4},{24,8},{28,12},{1,17},{... | collective-permute-start | bytes 24584 | tf_op jit(solution)/shard_map/ppermute | solution.py:523
  54.0 1.5 collective-permute-start
  55.7 2.0 collective-permute-start.3
  57.7 1.6 collective-permute-start.1
  59.5 1.9 collective-permute-done.1
  61.5 43.1 %sums.2 = (f32[16,128]{1,0:T(8,128)S(1)}, f32[16,128]{1,0:T(8,128)S(1)}, f32[16,128]{1,0:T(8,128)S(1)}, f32[16,128]{1,0:T(8,128)S(1)}) custom-call(f32[2048,2048]{1,0:T(8,128)S(1)} %get-tuple-element.45.k_ref, f32[64,2048]{1,0:T(8,128)S(1)} %get-tuple-element.46.x_ref, f32[64,2048]{1,0:T(8,128)S(1)} %get-tuple-element.47.y_ref, ...), custom_call_target="tpu_custom_call" | custom-call | flops 16777216 | bytes 16777216 | tf_op jit(solution)/shard_map/sums/pallas_call | solution.py:445
  104.6 2.6 collective-permute-start.7
  109.2 1.6 collective-permute-start.8
  110.9 1.6 collective-permute-start.6
  113.1 1.6 collective-permute-done.6
  114.7 43.3 %sums.3 = (f32[16,128]{1,0:T(8,128)S(1)}, f32[16,128]{1,0:T(8,128)S(1)}, f32[16,128]{1,0:T(8,128)S(1)}, f32[16,128]{1,0:T(8,128)S(1)}) custom-call(f32[2048,2048]{1,0:T(8,128)S(1)} %get-tuple-element.45.k_ref, f32[64,2048]{1,0:T(8,128)S(1)} %get-tuple-element.46.x_ref, f32[64,2048]{1,0:T(8,128)S(1)} %get-tuple-element.47.y_ref, ...), custom_call_target="tpu_custom_call" | custom-call | flops 16777216 | bytes 16777216 | tf_op jit(solution)/shard_map/sums/pallas_call | solution.py:445
  158.0 2.2 collective-permute-start.12
  163.8 1.6 collective-permute-start.11
  167.6 96.9 %maps.1 = (f32[16,128]{1,0:T(8,128)}, f32[16,128]{1,0:T(8,128)}, f32[72,2048]{1,0:T(8,128)S(1)}, f32[72,2048]{1,0:T(8,128)S(1)}) custom-call(f32[2048,2048]{1,0:T(8,128)S(1)} %get-tuple-element.45.k_ref, f32[64,2048]{1,0:T(8,128)S(1)} %get-tuple-element.46.x_ref, f32[64,2048]{1,0:T(8,128)S(1)} %get-tuple-element.47.y_ref, ...), custom_call_target="tpu_custom_call" | custom-call | flops 8589934592 | bytes 16777216 | tf_op jit(solution)/shard_map/maps/pallas_call | solution.py:460
  265.1 2.5 collective-permute-start.21
  269.4 2.8 collective-permute-start.18
  276.0 2.9 collective-permute-done.17.refs_1_
  279.5 2.7 collective-permute-start.24
  282.2 2.4 collective-permute-start.27
  285.7 1.7 collective-permute-start.22
  287.4 3.4 %collective-permute-done.23 = f32[64,256]{1,0:T(8,128)S(1)} collective-permute-done((f32[64,256]{1,0:T(8,128)S(1)}, f32[64,256]{1,0:T(8,128)S(1)}, u32[]{:S(2)}, u32[]{:S(2)}) %collective-permute-start.23) | collective-permute-done | bytes 65568 | tf_op jit(solution)/shard_map/ppermute | solution.py:569
  291.0 1.5 collective-permute-done.28.theirs
  292.5 1.6 join.1
  (70 shorter events, 17.0 us)
Async XLA Ops:
  49.9 5.7 %collective-permute-start.2 = (f32[16,128]{1,0:T(8,128)S(1)}, f32[16,128]{1,0:T(8,128)S(1)}, u32[]{:S(2)}, u32[]{:S(2)}) collective-permute-start(f32[16,128]{1,0:T(8,128)S(1)} %get-tuple-element.49), channel_id=1, source_target_pairs={{0,16},{4,20},{8,24},{12,28},{16,0},{20,4},{24,8},{28,12},{1,17},{... | collective-permute-start | bytes 24584 | tf_op jit(solution)/shard_map/ppermute | solution.py:523
  55.7 3.7 %collective-permute-start.3 = (f32[16,128]{1,0:T(8,128)S(1)}, f32[16,128]{1,0:T(8,128)S(1)}, u32[]{:S(2)}, u32[]{:S(2)}) collective-permute-start(f32[16,128]{1,0:T(8,128)S(1)} %log_add_fusion.12), channel_id=1, source_target_pairs={{0,8},{4,12},{8,0},{12,4},{16,24},{20,28},{24,16},{28,20},{1,9},{5... | collective-permute-start | bytes 24584 | tf_op jit(solution)/shard_map/ppermute | solution.py:523
  57.7 3.7 %collective-permute-start.1 = (f32[16,128]{1,0:T(8,128)S(1)}, f32[16,128]{1,0:T(8,128)S(1)}, u32[]{:S(2)}, u32[]{:S(2)}) collective-permute-start(f32[16,128]{1,0:T(8,128)S(1)} %log_add_fusion.14), channel_id=1, source_target_pairs={{0,1},{1,0},{2,3},{3,2},{4,5},{5,4},{6,7},{7,6},{8,9},{9,8},{10,11... | collective-permute-start | bytes 24584 | tf_op jit(solution)/shard_map/ppermute | solution.py:523
  104.6 4.6 %collective-permute-start.7 = (f32[16,128]{1,0:T(8,128)S(1)}, f32[16,128]{1,0:T(8,128)S(1)}, u32[]{:S(2)}, u32[]{:S(2)}) collective-permute-start(f32[16,128]{1,0:T(8,128)S(1)} %get-tuple-element.53), channel_id=1, source_target_pairs={{0,16},{4,20},{8,24},{12,28},{16,0},{20,4},{24,8},{28,12},{1,17},{... | collective-permute-start | bytes 24584 | tf_op jit(solution)/shard_map/ppermute | solution.py:523
  107.2 3.7 %collective-permute-start.5 = (f32[16,128]{1,0:T(8,128)S(1)}, f32[16,128]{1,0:T(8,128)S(1)}, u32[]{:S(2)}, u32[]{:S(2)}) collective-permute-start(f32[16,128]{1,0:T(8,128)S(1)} %get-tuple-element.52), channel_id=1, source_target_pairs={{0,2},{1,3},{2,0},{3,1},{4,6},{5,7},{6,4},{7,5},{8,10},{9,11},{10,... | collective-permute-start | bytes 24584 | tf_op jit(solution)/shard_map/ppermute | solution.py:523
  109.2 3.7 %collective-permute-start.8 = (f32[16,128]{1,0:T(8,128)S(1)}, f32[16,128]{1,0:T(8,128)S(1)}, u32[]{:S(2)}, u32[]{:S(2)}) collective-permute-start(f32[16,128]{1,0:T(8,128)S(1)} %log_add_fusion.7), channel_id=1, source_target_pairs={{0,8},{4,12},{8,0},{12,4},{16,24},{20,28},{24,16},{28,20},{1,9},{5... | collective-permute-start | bytes 24584 | tf_op jit(solution)/shard_map/ppermute | solution.py:523
  110.9 3.7 %collective-permute-start.6 = (f32[16,128]{1,0:T(8,128)S(1)}, f32[16,128]{1,0:T(8,128)S(1)}, u32[]{:S(2)}, u32[]{:S(2)}) collective-permute-start(f32[16,128]{1,0:T(8,128)S(1)} %log_add_fusion.9), channel_id=1, source_target_pairs={{0,1},{1,0},{2,3},{3,2},{4,5},{5,4},{6,7},{7,6},{8,9},{9,8},{10,11... | collective-permute-start | bytes 24584 | tf_op jit(solution)/shard_map/ppermute | solution.py:523
  158.0 4.6 %collective-permute-start.12 = (f32[16,128]{1,0:T(8,128)S(1)}, f32[16,128]{1,0:T(8,128)S(1)}, u32[]{:S(2)}, u32[]{:S(2)}) collective-permute-start(f32[16,128]{1,0:T(8,128)S(1)} %get-tuple-element.57), channel_id=1, source_target_pairs={{0,16},{4,20},{8,24},{12,28},{16,0},{20,4},{24,8},{28,12},{1,17},{... | collective-permute-start | bytes 24584 | tf_op jit(solution)/shard_map/ppermute | solution.py:523
  160.1 3.7 %collective-permute-start.10 = (f32[16,128]{1,0:T(8,128)S(1)}, f32[16,128]{1,0:T(8,128)S(1)}, u32[]{:S(2)}, u32[]{:S(2)}) collective-permute-start(f32[16,128]{1,0:T(8,128)S(1)} %get-tuple-element.56), channel_id=1, source_target_pairs={{0,2},{1,3},{2,0},{3,1},{4,6},{5,7},{6,4},{7,5},{8,10},{9,11},{10,... | collective-permute-start | bytes 24584 | tf_op jit(solution)/shard_map/ppermute | solution.py:523
  162.6 3.7 %collective-permute-start.13 = (f32[16,128]{1,0:T(8,128)S(1)}, f32[16,128]{1,0:T(8,128)S(1)}, u32[]{:S(2)}, u32[]{:S(2)}) collective-permute-start(f32[16,128]{1,0:T(8,128)S(1)} %log_add_fusion.2), channel_id=1, source_target_pairs={{0,8},{4,12},{8,0},{12,4},{16,24},{20,28},{24,16},{28,20},{1,9},{5... | collective-permute-start | bytes 24584 | tf_op jit(solution)/shard_map/ppermute | solution.py:523
  163.8 3.7 %collective-permute-start.11 = (f32[16,128]{1,0:T(8,128)S(1)}, f32[16,128]{1,0:T(8,128)S(1)}, u32[]{:S(2)}, u32[]{:S(2)}) collective-permute-start(f32[16,128]{1,0:T(8,128)S(1)} %log_add_fusion.4), channel_id=1, source_target_pairs={{0,1},{1,0},{2,3},{3,2},{4,5},{5,4},{6,7},{7,6},{8,9},{9,8},{10,11... | collective-permute-start | bytes 24584 | tf_op jit(solution)/shard_map/ppermute | solution.py:523
  264.6 4.0 %collective-permute-start.15 = (f32[72,1024]{1,0:T(8,128)S(1)}, f32[72,1024]{1,0:T(8,128)S(1)}, u32[]{:S(2)}, u32[]{:S(2)}) collective-permute-start(f32[72,1024]{1,0:T(8,128)S(1)} %constant_dynamic-slice_fusion.6), channel_id=1, source_target_pairs={{0,4},{4,0},{8,12},{12,8},{16,20},{20,16},{24,28},{28,24},{1,5},{5... | collective-permute-start | bytes 884744 | tf_op jit(solution)/shard_map/ppermute | solution.py:597
  265.1 7.6 %collective-permute-start.21 = (f32[72,512]{1,0:T(8,128)S(1)}, f32[72,512]{1,0:T(8,128)S(1)}, u32[]{:S(2)}, u32[]{:S(2)}) collective-permute-start(f32[72,512]{1,0:T(8,128)S(1)} %get-tuple-element.84), channel_id=1, source_target_pairs={{0,3},{1,2},{2,1},{3,0},{4,7},{5,6},{6,5},{7,4},{8,11},{9,10},{10,... | collective-permute-start | bytes 442376 | tf_op jit(solution)/shard_map/ppermute | solution.py:562
  267.6 7.7 %collective-permute-start.20 = (f32[72,512]{1,0:T(8,128)S(1)}, f32[72,512]{1,0:T(8,128)S(1)}, u32[]{:S(2)}, u32[]{:S(2)}) collective-permute-start(f32[72,512]{1,0:T(8,128)S(1)} %get-tuple-element.85), channel_id=1, source_target_pairs={{0,2},{1,3},{2,0},{3,1},{4,6},{5,7},{6,4},{7,5},{8,10},{9,11},{10,... | collective-permute-start | bytes 442376 | tf_op jit(solution)/shard_map/ppermute | solution.py:562
  268.1 7.3 %collective-permute-start.19 = (f32[72,512]{1,0:T(8,128)S(1)}, f32[72,512]{1,0:T(8,128)S(1)}, u32[]{:S(2)}, u32[]{:S(2)}) collective-permute-start(f32[72,512]{1,0:T(8,128)S(1)} %get-tuple-element.86), channel_id=1, source_target_pairs={{0,1},{1,0},{2,3},{3,2},{4,5},{5,4},{6,7},{7,6},{8,9},{9,8},{10,11... | collective-permute-start | bytes 442376 | tf_op jit(solution)/shard_map/ppermute | solution.py:562
  269.4 6.6 %collective-permute-start.18 = (f32[72,256]{1,0:T(8,128)S(1)}, f32[72,256]{1,0:T(8,128)S(1)}, u32[]{:S(2)}, u32[]{:S(2)}) collective-permute-start(f32[72,256]{1,0:T(8,128)S(1)} %get-tuple-element.87), channel_id=1, source_target_pairs={{0,24},{4,28},{8,16},{12,20},{16,8},{20,12},{24,0},{28,4},{1,25},{... | collective-permute-start | bytes 221192 | tf_op jit(solution)/shard_map/ppermute | solution.py:562
  272.2 6.7 %collective-permute-start.17 = (f32[72,256]{1,0:T(8,128)S(1)}, f32[72,256]{1,0:T(8,128)S(1)}, u32[]{:S(2)}, u32[]{:S(2)}) collective-permute-start(f32[72,256]{1,0:T(8,128)S(1)} %get-tuple-element.88), channel_id=1, source_target_pairs={{0,16},{4,20},{8,24},{12,28},{16,0},{20,4},{24,8},{28,12},{1,17},{... | collective-permute-start | bytes 221192 | tf_op jit(solution)/shard_map/ppermute | solution.py:562
  272.7 6.2 %collective-permute-start.16 = (f32[72,256]{1,0:T(8,128)S(1)}, f32[72,256]{1,0:T(8,128)S(1)}, u32[]{:S(2)}, u32[]{:S(2)}) collective-permute-start(f32[72,256]{1,0:T(8,128)S(1)} %get-tuple-element.89), channel_id=1, source_target_pairs={{0,8},{4,12},{8,0},{12,4},{16,24},{20,28},{24,16},{28,20},{1,9},{5... | collective-permute-start | bytes 221192 | tf_op jit(solution)/shard_map/ppermute | solution.py:562
  279.5 6.2 %collective-permute-start.24 = (f32[64,256]{1,0:T(8,128)S(1)}, f32[64,256]{1,0:T(8,128)S(1)}, u32[]{:S(2)}, u32[]{:S(2)}) collective-permute-start(f32[64,256]{1,0:T(8,128)S(1)} %merge.5), channel_id=1, source_target_pairs={{0,24},{4,28},{8,16},{12,20},{16,8},{20,12},{24,0},{28,4},{1,25},{... | collective-permute-start | bytes 196616 | tf_op jit(solution)/shard_map/ppermute | solution.py:569
  282.2 8.7 %collective-permute-start.27 = (f32[64,512]{1,0:T(8,128)S(1)}, f32[64,512]{1,0:T(8,128)S(1)}, u32[]{:S(2)}, u32[]{:S(2)}) collective-permute-start(f32[64,512]{1,0:T(8,128)S(1)} %merge.4.refs_0_), channel_id=1, source_target_pairs={{0,3},{1,2},{2,1},{3,0},{4,7},{5,6},{6,5},{7,4},{8,11},{9,10},{10,... | collective-permute-start | bytes 393224 | tf_op jit(solution)/shard_map/ppermute | solution.py:569
  284.6 6.2 %collective-permute-start.26 = (f32[64,512]{1,0:T(8,128)S(1)}, f32[64,512]{1,0:T(8,128)S(1)}, u32[]{:S(2)}, u32[]{:S(2)}) collective-permute-start(f32[64,512]{1,0:T(8,128)S(1)} %merge.4.refs_0_), channel_id=1, source_target_pairs={{0,2},{1,3},{2,0},{3,1},{4,6},{5,7},{6,4},{7,5},{8,10},{9,11},{10,... | collective-permute-start | bytes 393224 | tf_op jit(solution)/shard_map/ppermute | solution.py:569
  285.1 5.7 %collective-permute-start.25 = (f32[64,512]{1,0:T(8,128)S(1)}, f32[64,512]{1,0:T(8,128)S(1)}, u32[]{:S(2)}, u32[]{:S(2)}) collective-permute-start(f32[64,512]{1,0:T(8,128)S(1)} %merge.4.refs_0_), channel_id=1, source_target_pairs={{0,1},{1,0},{2,3},{3,2},{4,5},{5,4},{6,7},{7,6},{8,9},{9,8},{10,11... | collective-permute-start | bytes 393224 | tf_op jit(solution)/shard_map/ppermute | solution.py:569
  285.7 5.2 %collective-permute-start.23 = (f32[64,256]{1,0:T(8,128)S(1)}, f32[64,256]{1,0:T(8,128)S(1)}, u32[]{:S(2)}, u32[]{:S(2)}) collective-permute-start(f32[64,256]{1,0:T(8,128)S(1)} %merge.5), channel_id=1, source_target_pairs={{0,16},{4,20},{8,24},{12,28},{16,0},{20,4},{24,8},{28,12},{1,17},{... | collective-permute-start | bytes 196616 | tf_op jit(solution)/shard_map/ppermute | solution.py:569
  285.7 5.2 %collective-permute-start.22 = (f32[64,256]{1,0:T(8,128)S(1)}, f32[64,256]{1,0:T(8,128)S(1)}, u32[]{:S(2)}, u32[]{:S(2)}) collective-permute-start(f32[64,256]{1,0:T(8,128)S(1)} %merge.5), channel_id=1, source_target_pairs={{0,8},{4,12},{8,0},{12,4},{16,24},{20,28},{24,16},{28,20},{1,9},{5... | collective-permute-start | bytes 196616 | tf_op jit(solution)/shard_map/ppermute | solution.py:569
  (7 other events, 131.9 us)

commit v6 on v5

--- a/solution.py
+++ b/solution.py
@@ -45,20 +45,19 @@
     return jnp.sum(a.reshape(a.shape[0] // 8, 8, a.shape[1]), axis=0)
 
 
-def build_operands(x_ref, y_ref, xa, ya):
-    d, ns = x_ref.shape
-    nt = y_ref.shape[1]
+def tail(row, parts):
+    out = jnp.zeros(row.shape, F32)
+    for at, part in enumerate(parts):
+        out = jnp.where(row == at, part, out)
+    return out
+
+
+def targets_operand(y_ref, ya):
+    d, nt = y_ref.shape
     wide = 2 * LANES
     sub = lax.broadcasted_iota(jnp.int32, (16, wide), 0)
-    lane = lax.broadcasted_iota(jnp.int32, (LANES, 2 * d), 1)
-
-    def tail(row, parts):
-        out = jnp.zeros(row.shape, F32)
-        for at, part in enumerate(parts):
-            out = jnp.where(row == at, part, out)
-        return out
-
-    def target_block(b, _):
+
+    def block(b, _):
         cols = pl.ds(pl.multiple_of(b * wide, wide), wide)
         y = y_ref[:, cols]
         norm = split3(SHIFT - jnp.sum(y * y, axis=0, keepdims=True) * (LOG2E / EPS))
@@ -69,22 +68,19 @@
         ya[6 * d + 16 : 8 * d, cols] = jnp.zeros((2 * d - 16, wide), BF16)
         return 0
 
-    lax.fori_loop(0, nt // wide, target_block, 0, unroll=4)
-
-    def source_block(b, _):
-        rows = pl.ds(pl.multiple_of(b * LANES, LANES), LANES)
-        x = x_ref[:, rows]
-        norm = split3(jnp.sum(x * x, axis=0, keepdims=True) * (-LOG2E / EPS))
-        x1, x2, x3 = split3(jnp.concatenate([x, x], axis=0).T)
-        xa[rows, 0 : 2 * d] = x1.astype(BF16)
-        xa[rows, 2 * d : 4 * d] = x2.astype(BF16)
-        xa[rows, 4 * d : 6 * d] = jnp.where(lane < d, x1, x3).astype(BF16)
-        last = tail(sub[:8, :LANES], (1.0, 1.0, 1.0) + norm)
-        last = jnp.concatenate([last, jnp.zeros((2 * d - 8, LANES), F32)], axis=0)
-        xa[rows, 6 * d : 8 * d] = last.T.astype(BF16)
-        return 0
-
-    lax.fori_loop(0, ns // LANES, source_block, 0, unroll=4)
+    lax.fori_loop(0, nt // wide, block, 0, unroll=4)
+
+
+def sources_operand(x):
+    d = x.shape[0]
+    lane = lax.broadcasted_iota(jnp.int32, (LANES, 2 * d), 1)
+    sub = lax.broadcasted_iota(jnp.int32, (8, LANES), 0)
+    norm = split3(jnp.sum(x * x, axis=0, keepdims=True) * (-LOG2E / EPS))
+    x1, x2, x3 = split3(jnp.concatenate([x, x], axis=0).T)
+    last = tail(sub, (1.0, 1.0, 1.0) + norm)
+    last = jnp.concatenate([last, jnp.zeros((2 * d - 8, LANES), F32)], axis=0).T
+    parts = (x1, x2, jnp.where(lane < d, x1, x3), last)
+    return jnp.concatenate([part.astype(BF16) for part in parts], axis=1)
 
 
 def as_row(ref):
@@ -175,7 +171,7 @@
 
 
 def form_kernel(
-    x_hbm, y_hbm, a_hbm, b_hbm, k_ref, x_ref, y_ref, row_ref, col_ref, xa, ya, ub, acc, r_s, t_s, sem, *, rows
+    x_hbm, y_hbm, a_hbm, b_hbm, k_ref, x_ref, y_ref, row_ref, col_ref, xa, ya, ub, r_s, t_s, vs, cs, sem, *, tiles
 ):
     ns, nt = x_ref.shape[1], y_ref.shape[1]
     fetch(((x_hbm, x_ref), (y_hbm, y_ref), (a_hbm, r_s), (b_hbm, t_s)), sem)
@@ -183,34 +179,51 @@
     t_s[...] = jnp.log(t_s[...])
     u, r_top, u_fine = factors(r_s[...])
     v, t_top, v_fine = factors(t_s[...])
-    build_operands(x_ref, y_ref, xa, ya)
-    spread(u, ub)
-    col_ref[...] = v
-    acc[...] = jnp.zeros_like(acc)
-    tiles = 4 if nt % (4 * LANES) == 0 else 1
+    row_ref[...] = u
+    vs[...] = v
+    targets_operand(y_ref, ya)
+    cs[...] = jnp.zeros_like(cs)
     wide = tiles * LANES
-
-    def block(cb, _):
-        at = pl.multiple_of(cb * wide, wide)
-        vs = [col_ref[pl.ds(cb * tiles + t, 1), :] for t in range(tiles)]
-        cs = [jnp.zeros((8, LANES), F32)] * tiles
-        for r in range(0, ns, rows):
-            z = jnp.dot(xa[r : r + rows, :], ya[:, pl.ds(at, wide)], preferred_element_type=F32)
+    tall = xa.shape[1]
+
+    def operand(rb, slot):
+        for b in range(tall // LANES):
+            at = pl.ds(pl.multiple_of(rb * tall + b * LANES, LANES), LANES)
+            xa[slot, b * LANES : (b + 1) * LANES, :] = sources_operand(x_ref[:, at])
+
+    def block(rb, slot):
+        at = pl.ds(pl.multiple_of(rb * tall, tall), tall)
+        lanes = tall // LANES
+        ur = [
+            jnp.broadcast_to(row_ref[pl.ds(rb * lanes + b, 1), :], (LANES, LANES)).T for b in range(lanes)
+        ]
+        ur = jnp.concatenate(ur, axis=0)
+        total = jnp.zeros((tall, LANES), F32)
+        for c in range(0, nt, wide):
+            z = jnp.dot(xa[slot], ya[:, c : c + wide], preferred_element_type=F32)
             k = jnp.exp2(z)
-            k_ref[r : r + rows, pl.ds(at, wide)] = k
-            ur = ub[r : r + rows, :]
-            total = acc[r : r + rows, :]
+            k_ref[at, c : c + wide] = k
             for t in range(tiles):
                 kt = k[:, t * LANES : (t + 1) * LANES]
-                total += kt * vs[t]
-                cs[t] += fold(kt * ur)
-            acc[r : r + rows, :] = total
-        for t in range(tiles):
-            col_ref[pl.ds(cb * tiles + t, 1), :] = jnp.sum(cs[t], axis=0, keepdims=True)
+                total += kt * vs[c // LANES + t : c // LANES + t + 1, :]
+                cs[:, c + t * LANES : c + (t + 1) * LANES] += fold(kt * ur)
+        for b in range(lanes):
+            part = total[b * LANES : (b + 1) * LANES, :]
+            row_ref[pl.ds(rb * lanes + b, 1), :] = jnp.sum(part.T, axis=0, keepdims=True)
+
+    count = ns // tall
+    operand(0, 0)
+
+    def two(pair, _):
+        first = pair * 2
+        operand(first + 1, 1)
+        block(first, 0)
+        operand(jnp.minimum(first + 2, count - 1), 0)
+        block(first + 1, 1)
         return 0
 
-    lax.fori_loop(0, nt // wide, block, 0)
-    lane_sums(acc, row_ref)
+    lax.fori_loop(0, count // 2, two, 0)
+    put_row(jnp.sum(cs[...], axis=0, keepdims=True), col_ref)
     rows_fine = finish(row_ref, t_top, v_fine)
     cols_fine = finish(col_ref, r_top, u_fine)
 
@@ -230,7 +243,7 @@
 
 def sums_kernel(
     k_ref, x_ref, y_ref, f_ref, g_ref, rl_ref, cl_ref, a_ref, b_ref,
-    fn_ref, gn_ref, row_ref, col_ref, vs, r_s, t_s, ub,
+    fn_ref, gn_ref, row_ref, col_ref, vs, r_s, t_s, ub, cs,
 ):
     update(f_ref, rl_ref, a_ref, fn_ref, r_s)
     update(g_ref, cl_ref, b_ref, gn_ref, t_s)
@@ -241,21 +254,20 @@
     ns, nt = k_ref.shape
     tiles = nt // LANES
 
-    def block(rb, cs):
+    def block(rb, _):
         at = pl.ds(pl.multiple_of(rb * LANES, LANES), LANES)
         ur = jnp.broadcast_to(row_ref[pl.ds(rb, 1), :], (LANES, LANES)).T
         total = jnp.zeros((LANES, LANES), F32)
-        out = []
         for c in range(tiles):
             k = k_ref[at, c * LANES : (c + 1) * LANES]
             total += k * vs[c : c + 1, :]
-            out.append(cs[c] + fold(k * ur))
+            cs[:, c * LANES : (c + 1) * LANES] += fold(k * ur)
         row_ref[pl.ds(rb, 1), :] = jnp.sum(total.T, axis=0, keepdims=True)
-        return tuple(out)
-
-    cs = lax.fori_loop(0, ns // LANES, block, (jnp.zeros((8, LANES), F32),) * tiles, unroll=2)
-    for c in range(tiles):
-        col_ref[c : c + 1, :] = jnp.sum(cs[c], axis=0, keepdims=True)
+        return 0
+
+    cs[...] = jnp.zeros_like(cs)
+    lax.fori_loop(0, ns // LANES, block, 0, unroll=2)
+    put_row(jnp.sum(cs[...], axis=0, keepdims=True), col_ref)
     rows_fine = finish(row_ref, t_top, v_fine)
     cols_fine = finish(col_ref, r_top, u_fine)
 
@@ -309,32 +321,23 @@
     v, t_top, v_fine = factors(t_s[...])
     weighted_points(y_ref, v, yv)
     weighted_points(x_ref, u, xu)
-    wide = 2 * LANES
-    racc[...] = jnp.zeros_like(racc)
-
-    def block(cb, _):
-        at = pl.multiple_of(cb * wide, wide)
-        yc = yv[:, pl.ds(at, wide)]
-        yc = jnp.concatenate([yc, yc], axis=1)
-        total = jnp.zeros((xu.shape[0], wide), F32)
-        for r in range(0, ns, rows):
-            k1, k2 = parts_of(k_ref[r : r + rows, pl.ds(at, wide)])
-            xr = xu[:, r : r + rows]
-            total += jnp.dot(
-                jnp.concatenate([xr, xr], axis=1),
-                jnp.concatenate([k1, k2], axis=0),
-                preferred_element_type=F32,
-            )
-            racc[:, r : r + rows] += lax.dot_general(
-                yc,
-                jnp.concatenate([k1, k2], axis=1),
-                (((1,), (1,)), ((), ())),
-                preferred_element_type=F32,
-            )
-        cacc[:, pl.ds(at, wide)] = total
-        return 0
-
-    lax.fori_loop(0, nt // wide, block, 0)
+    yc = jnp.concatenate([yv[...], yv[...]], axis=1)
+    total = jnp.zeros(cacc.shape, F32)
+    for r in range(0, ns, rows):
+        k1, k2 = parts_of(k_ref[r : r + rows, :])
+        xr = xu[:, r : r + rows]
+        total += jnp.dot(
+            jnp.concatenate([xr, xr], axis=1),
+            jnp.concatenate([k1, k2], axis=0),
+            preferred_element_type=F32,
+        )
+        racc[:, r : r + rows] = lax.dot_general(
+            yc,
+            jnp.concatenate([k1, k2], axis=1),
+            (((1,), (1,)), ((), ())),
+            preferred_element_type=F32,
+        )
+    cacc[...] = total
     means(racc, rowm_ref, row_s)
     means(cacc, colm_ref, col_s)
     rows_fine = finish(row_s, t_top, v_fine)
@@ -415,7 +418,7 @@
     d, ns = x.shape
     nt = y.shape[1]
     return pl.pallas_call(
-        functools.partial(form_kernel, rows=256),
+        functools.partial(form_kernel, tiles=4),
         out_shape=(
             pltpu.VMEM((ns, nt), F32),
             pltpu.VMEM((d, ns), F32),
@@ -426,12 +429,13 @@
         in_specs=[ANY] * 4,
         out_specs=(VM,) * 5,
         scratch_shapes=[
-            pltpu.VMEM((ns, 8 * d), BF16),
+            pltpu.VMEM((2, 256, 8 * d), BF16),
             pltpu.VMEM((8 * d, nt), BF16),
-            pltpu.VMEM((ns, LANES), F32),
             pltpu.VMEM((ns, LANES), F32),
             scratch(ns),
             scratch(nt),
+            scratch(nt),
+            pltpu.VMEM((8, nt), F32),
             pltpu.SemaphoreType.DMA((4,)),
         ],
         compiler_params=FULL,
@@ -447,7 +451,13 @@
         out_shape=(near(ns), near(nt), near(ns), near(nt)),
         in_specs=[VM] * 9,
         out_specs=(VM,) * 4,
-        scratch_shapes=[scratch(nt), scratch(ns), scratch(nt), pltpu.VMEM((ns, LANES), F32)],
+        scratch_shapes=[
+            scratch(nt),
+            scratch(ns),
+            scratch(nt),
+            pltpu.VMEM((ns, LANES), F32),
+            pltpu.VMEM((8, nt), F32),
+        ],
         compiler_params=PARAMS,
         cost_estimate=cost(4 * ns * nt, 4 * ns * nt),
         name="sums",

time: 294 us -> 291 us (0.990)
  Pallas kernels: 236 us -> 233 us
  transfers between devices with their start and end apart: 29 -> 29, of which waited for: 15 -> 16; matrix products, arithmetic and copies ran while one was open for 0% -> 0% of each run, Pallas kernels for 0% -> 0%
where the time goes in v6:
time: 291 us
  Pallas kernels  233 us (80%)
  starting transfers between devices  38.8 us (13%)
  waiting for transfers between devices  17.7 us (6%)
    pallas_call x1, Pallas kernels, maps(): pl.pallas_call(functools.partial(maps_kernel, rows=256), out_shape=(vecto...  95.3 us
    pallas_call x2, Pallas kernels, sums(): pl.pallas_call(sums_kernel, out_shape=(near(ns), near(nt), near(ns), near...  85.9 us
    pallas_call x1, Pallas kernels, form(): pl.pallas_call(functools.partial(form_kernel, tiles=4), out_shape=(pltpu....  48.2 us
    ppermute x15, starting transfers between devices, lse_over(): lax.ppermute(part, axis, [(i, i ^ step) for i in range(n)])  23.1 us
    ppermute x6, starting transfers between devices, all_pieces(): lax.ppermute(own, axis, pairs(n, group, stride, k))  7.94 us
    ppermute x15, waiting for transfers between devices, lse_over(): lax.ppermute(part, axis, [(i, i ^ step) for i in range(n)])  7.78 us
    ppermute x6, starting transfers between devices, pieces_of(): lax.ppermute(piece(part, place[k], group), axis, pairs(n, group, stride, k))  7.48 us
  transfers between devices with their start and end apart: 29, of which 16 were waited for; matrix products, arithmetic and copies ran while one was open for 0% of the time, Pallas kernels for 0%

profile of v6, /device:TPU:0, one launch (start us, length us, event | category | flops | bytes accessed | tf_op | source)
XLA Modules:
  0.0 291.3 jit_solution(13222116613978833659)
XLA Ops:
  0.8 48.2 %form.1 = (f32[2048,2048]{1,0:T(8,128)S(1)}, f32[64,2048]{1,0:T(8,128)S(1)}, f32[64,2048]{1,0:T(8,128)S(1)}, f32[16,128]{1,0:T(8,128)S(1)}, f32[16,128]{1,0:T(8,128)S(1)}) custom-call(f32[64,2048]{1,0:T(8,128)} %x_hbm, f32[64,2048]{1,0:T(8,128)} %y_hbm.1, f32[16,128]{1,0:T(8,128)} %bitcast.18, f32[16,128]{1,0:T(8,128)} %bitcast.22), custom_call_target="tpu_custom_call" | custom-call | flops 5368709120 | bytes 16777216 | tf_op jit(solution)/shard_map/form/pallas_call | solution.py:420
  49.0 4.1 %collective-permute-start.2 = (f32[16,128]{1,0:T(8,128)S(1)}, f32[16,128]{1,0:T(8,128)S(1)}, u32[]{:S(2)}, u32[]{:S(2)}) collective-permute-start(f32[16,128]{1,0:T(8,128)S(1)} %get-tuple-element.49), channel_id=1, source_target_pairs={{0,16},{4,20},{8,24},{12,28},{16,0},{20,4},{24,8},{28,12},{1,17},{... | collective-permute-start | bytes 24584 | tf_op jit(solution)/shard_map/ppermute | solution.py:533
  54.8 1.9 collective-permute-start.3
  56.8 1.5 collective-permute-start.1
  58.6 1.9 collective-permute-done.1
  60.6 42.9 %sums.2 = (f32[16,128]{1,0:T(8,128)S(1)}, f32[16,128]{1,0:T(8,128)S(1)}, f32[16,128]{1,0:T(8,128)S(1)}, f32[16,128]{1,0:T(8,128)S(1)}) custom-call(f32[2048,2048]{1,0:T(8,128)S(1)} %get-tuple-element.45.k_ref, f32[64,2048]{1,0:T(8,128)S(1)} %get-tuple-element.46.x_ref, f32[64,2048]{1,0:T(8,128)S(1)} %get-tuple-element.47.y_ref, ...), custom_call_target="tpu_custom_call" | custom-call | flops 16777216 | bytes 16777216 | tf_op jit(solution)/shard_map/sums/pallas_call | solution.py:449
  103.5 2.6 collective-permute-start.7
  106.1 1.5 collective-permute-start.5
  108.1 1.6 collective-permute-start.8
  109.7 1.6 collective-permute-start.6
  111.9 1.5 collective-permute-done.6
  113.5 43.0 %sums.3 = (f32[16,128]{1,0:T(8,128)S(1)}, f32[16,128]{1,0:T(8,128)S(1)}, f32[16,128]{1,0:T(8,128)S(1)}, f32[16,128]{1,0:T(8,128)S(1)}) custom-call(f32[2048,2048]{1,0:T(8,128)S(1)} %get-tuple-element.45.k_ref, f32[64,2048]{1,0:T(8,128)S(1)} %get-tuple-element.46.x_ref, f32[64,2048]{1,0:T(8,128)S(1)} %get-tuple-element.47.y_ref, ...), custom_call_target="tpu_custom_call" | custom-call | flops 16777216 | bytes 16777216 | tf_op jit(solution)/shard_map/sums/pallas_call | solution.py:449
  156.6 2.2 collective-permute-start.12
  158.8 1.5 collective-permute-start.10
  162.4 1.6 collective-permute-start.11
  166.2 95.3 %maps.1 = (f32[16,128]{1,0:T(8,128)}, f32[16,128]{1,0:T(8,128)}, f32[72,2048]{1,0:T(8,128)S(1)}, f32[72,2048]{1,0:T(8,128)S(1)}) custom-call(f32[2048,2048]{1,0:T(8,128)S(1)} %get-tuple-element.45.k_ref, f32[64,2048]{1,0:T(8,128)S(1)} %get-tuple-element.46.x_ref, f32[64,2048]{1,0:T(8,128)S(1)} %get-tuple-element.47.y_ref, ...), custom_call_target="tpu_custom_call" | custom-call | flops 8589934592 | bytes 16777216 | tf_op jit(solution)/shard_map/maps/pallas_call | solution.py:470
  262.0 2.5 collective-permute-start.21
  266.4 2.8 collective-permute-start.18
  273.0 2.8 collective-permute-done.17.refs_1_
  276.4 2.7 collective-permute-start.24
  279.2 2.5 collective-permute-start.27
  282.6 1.7 collective-permute-start.22
  284.4 3.4 %collective-permute-done.23 = f32[64,256]{1,0:T(8,128)S(1)} collective-permute-done((f32[64,256]{1,0:T(8,128)S(1)}, f32[64,256]{1,0:T(8,128)S(1)}, u32[]{:S(2)}, u32[]{:S(2)}) %collective-permute-start.23) | collective-permute-done | bytes 65568 | tf_op jit(solution)/shard_map/ppermute | solution.py:579
  289.5 1.6 join.1
  (70 shorter events, 17.1 us)
Async XLA Ops:
  49.0 5.7 %collective-permute-start.2 = (f32[16,128]{1,0:T(8,128)S(1)}, f32[16,128]{1,0:T(8,128)S(1)}, u32[]{:S(2)}, u32[]{:S(2)}) collective-permute-start(f32[16,128]{1,0:T(8,128)S(1)} %get-tuple-element.49), channel_id=1, source_target_pairs={{0,16},{4,20},{8,24},{12,28},{16,0},{20,4},{24,8},{28,12},{1,17},{... | collective-permute-start | bytes 24584 | tf_op jit(solution)/shard_map/ppermute | solution.py:533
  54.8 3.7 %collective-permute-start.3 = (f32[16,128]{1,0:T(8,128)S(1)}, f32[16,128]{1,0:T(8,128)S(1)}, u32[]{:S(2)}, u32[]{:S(2)}) collective-permute-start(f32[16,128]{1,0:T(8,128)S(1)} %log_add_fusion.12), channel_id=1, source_target_pairs={{0,8},{4,12},{8,0},{12,4},{16,24},{20,28},{24,16},{28,20},{1,9},{5... | collective-permute-start | bytes 24584 | tf_op jit(solution)/shard_map/ppermute | solution.py:533
  56.8 3.7 %collective-permute-start.1 = (f32[16,128]{1,0:T(8,128)S(1)}, f32[16,128]{1,0:T(8,128)S(1)}, u32[]{:S(2)}, u32[]{:S(2)}) collective-permute-start(f32[16,128]{1,0:T(8,128)S(1)} %log_add_fusion.14), channel_id=1, source_target_pairs={{0,1},{1,0},{2,3},{3,2},{4,5},{5,4},{6,7},{7,6},{8,9},{9,8},{10,11... | collective-permute-start | bytes 24584 | tf_op jit(solution)/shard_map/ppermute | solution.py:533
  103.5 4.6 %collective-permute-start.7 = (f32[16,128]{1,0:T(8,128)S(1)}, f32[16,128]{1,0:T(8,128)S(1)}, u32[]{:S(2)}, u32[]{:S(2)}) collective-permute-start(f32[16,128]{1,0:T(8,128)S(1)} %get-tuple-element.53), channel_id=1, source_target_pairs={{0,16},{4,20},{8,24},{12,28},{16,0},{20,4},{24,8},{28,12},{1,17},{... | collective-permute-start | bytes 24584 | tf_op jit(solution)/shard_map/ppermute | solution.py:533
  106.1 3.7 %collective-permute-start.5 = (f32[16,128]{1,0:T(8,128)S(1)}, f32[16,128]{1,0:T(8,128)S(1)}, u32[]{:S(2)}, u32[]{:S(2)}) collective-permute-start(f32[16,128]{1,0:T(8,128)S(1)} %get-tuple-element.52), channel_id=1, source_target_pairs={{0,2},{1,3},{2,0},{3,1},{4,6},{5,7},{6,4},{7,5},{8,10},{9,11},{10,... | collective-permute-start | bytes 24584 | tf_op jit(solution)/shard_map/ppermute | solution.py:533
  108.1 3.7 %collective-permute-start.8 = (f32[16,128]{1,0:T(8,128)S(1)}, f32[16,128]{1,0:T(8,128)S(1)}, u32[]{:S(2)}, u32[]{:S(2)}) collective-permute-start(f32[16,128]{1,0:T(8,128)S(1)} %log_add_fusion.7), channel_id=1, source_target_pairs={{0,8},{4,12},{8,0},{12,4},{16,24},{20,28},{24,16},{28,20},{1,9},{5... | collective-permute-start | bytes 24584 | tf_op jit(solution)/shard_map/ppermute | solution.py:533
  109.7 3.7 %collective-permute-start.6 = (f32[16,128]{1,0:T(8,128)S(1)}, f32[16,128]{1,0:T(8,128)S(1)}, u32[]{:S(2)}, u32[]{:S(2)}) collective-permute-start(f32[16,128]{1,0:T(8,128)S(1)} %log_add_fusion.9), channel_id=1, source_target_pairs={{0,1},{1,0},{2,3},{3,2},{4,5},{5,4},{6,7},{7,6},{8,9},{9,8},{10,11... | collective-permute-start | bytes 24584 | tf_op jit(solution)/shard_map/ppermute | solution.py:533
  156.6 4.6 %collective-permute-start.12 = (f32[16,128]{1,0:T(8,128)S(1)}, f32[16,128]{1,0:T(8,128)S(1)}, u32[]{:S(2)}, u32[]{:S(2)}) collective-permute-start(f32[16,128]{1,0:T(8,128)S(1)} %get-tuple-element.57), channel_id=1, source_target_pairs={{0,16},{4,20},{8,24},{12,28},{16,0},{20,4},{24,8},{28,12},{1,17},{... | collective-permute-start | bytes 24584 | tf_op jit(solution)/shard_map/ppermute | solution.py:533
  158.8 3.7 %collective-permute-start.10 = (f32[16,128]{1,0:T(8,128)S(1)}, f32[16,128]{1,0:T(8,128)S(1)}, u32[]{:S(2)}, u32[]{:S(2)}) collective-permute-start(f32[16,128]{1,0:T(8,128)S(1)} %get-tuple-element.56), channel_id=1, source_target_pairs={{0,2},{1,3},{2,0},{3,1},{4,6},{5,7},{6,4},{7,5},{8,10},{9,11},{10,... | collective-permute-start | bytes 24584 | tf_op jit(solution)/shard_map/ppermute | solution.py:533
  161.2 3.7 %collective-permute-start.13 = (f32[16,128]{1,0:T(8,128)S(1)}, f32[16,128]{1,0:T(8,128)S(1)}, u32[]{:S(2)}, u32[]{:S(2)}) collective-permute-start(f32[16,128]{1,0:T(8,128)S(1)} %log_add_fusion.2), channel_id=1, source_target_pairs={{0,8},{4,12},{8,0},{12,4},{16,24},{20,28},{24,16},{28,20},{1,9},{5... | collective-permute-start | bytes 24584 | tf_op jit(solution)/shard_map/ppermute | solution.py:533
  162.4 3.7 %collective-permute-start.11 = (f32[16,128]{1,0:T(8,128)S(1)}, f32[16,128]{1,0:T(8,128)S(1)}, u32[]{:S(2)}, u32[]{:S(2)}) collective-permute-start(f32[16,128]{1,0:T(8,128)S(1)} %log_add_fusion.4), channel_id=1, source_target_pairs={{0,1},{1,0},{2,3},{3,2},{4,5},{5,4},{6,7},{7,6},{8,9},{9,8},{10,11... | collective-permute-start | bytes 24584 | tf_op jit(solution)/shard_map/ppermute | solution.py:533
  261.6 4.0 %collective-permute-start.15 = (f32[72,1024]{1,0:T(8,128)S(1)}, f32[72,1024]{1,0:T(8,128)S(1)}, u32[]{:S(2)}, u32[]{:S(2)}) collective-permute-start(f32[72,1024]{1,0:T(8,128)S(1)} %constant_dynamic-slice_fusion.6), channel_id=1, source_target_pairs={{0,4},{4,0},{8,12},{12,8},{16,20},{20,16},{24,28},{28,24},{1,5},{5... | collective-permute-start | bytes 884744 | tf_op jit(solution)/shard_map/ppermute | solution.py:607
  262.0 7.6 %collective-permute-start.21 = (f32[72,512]{1,0:T(8,128)S(1)}, f32[72,512]{1,0:T(8,128)S(1)}, u32[]{:S(2)}, u32[]{:S(2)}) collective-permute-start(f32[72,512]{1,0:T(8,128)S(1)} %get-tuple-element.84), channel_id=1, source_target_pairs={{0,3},{1,2},{2,1},{3,0},{4,7},{5,6},{6,5},{7,4},{8,11},{9,10},{10,... | collective-permute-start | bytes 442376 | tf_op jit(solution)/shard_map/ppermute | solution.py:572
  264.5 7.7 %collective-permute-start.20 = (f32[72,512]{1,0:T(8,128)S(1)}, f32[72,512]{1,0:T(8,128)S(1)}, u32[]{:S(2)}, u32[]{:S(2)}) collective-permute-start(f32[72,512]{1,0:T(8,128)S(1)} %get-tuple-element.85), channel_id=1, source_target_pairs={{0,2},{1,3},{2,0},{3,1},{4,6},{5,7},{6,4},{7,5},{8,10},{9,11},{10,... | collective-permute-start | bytes 442376 | tf_op jit(solution)/shard_map/ppermute | solution.py:572
  265.0 7.3 %collective-permute-start.19 = (f32[72,512]{1,0:T(8,128)S(1)}, f32[72,512]{1,0:T(8,128)S(1)}, u32[]{:S(2)}, u32[]{:S(2)}) collective-permute-start(f32[72,512]{1,0:T(8,128)S(1)} %get-tuple-element.86), channel_id=1, source_target_pairs={{0,1},{1,0},{2,3},{3,2},{4,5},{5,4},{6,7},{7,6},{8,9},{9,8},{10,11... | collective-permute-start | bytes 442376 | tf_op jit(solution)/shard_map/ppermute | solution.py:572
  266.4 6.6 %collective-permute-start.18 = (f32[72,256]{1,0:T(8,128)S(1)}, f32[72,256]{1,0:T(8,128)S(1)}, u32[]{:S(2)}, u32[]{:S(2)}) collective-permute-start(f32[72,256]{1,0:T(8,128)S(1)} %get-tuple-element.87), channel_id=1, source_target_pairs={{0,24},{4,28},{8,16},{12,20},{16,8},{20,12},{24,0},{28,4},{1,25},{... | collective-permute-start | bytes 221192 | tf_op jit(solution)/shard_map/ppermute | solution.py:572
  269.1 6.7 %collective-permute-start.17 = (f32[72,256]{1,0:T(8,128)S(1)}, f32[72,256]{1,0:T(8,128)S(1)}, u32[]{:S(2)}, u32[]{:S(2)}) collective-permute-start(f32[72,256]{1,0:T(8,128)S(1)} %get-tuple-element.88), channel_id=1, source_target_pairs={{0,16},{4,20},{8,24},{12,28},{16,0},{20,4},{24,8},{28,12},{1,17},{... | collective-permute-start | bytes 221192 | tf_op jit(solution)/shard_map/ppermute | solution.py:572
  269.7 6.2 %collective-permute-start.16 = (f32[72,256]{1,0:T(8,128)S(1)}, f32[72,256]{1,0:T(8,128)S(1)}, u32[]{:S(2)}, u32[]{:S(2)}) collective-permute-start(f32[72,256]{1,0:T(8,128)S(1)} %get-tuple-element.89), channel_id=1, source_target_pairs={{0,8},{4,12},{8,0},{12,4},{16,24},{20,28},{24,16},{28,20},{1,9},{5... | collective-permute-start | bytes 221192 | tf_op jit(solution)/shard_map/ppermute | solution.py:572
  276.4 6.2 %collective-permute-start.24 = (f32[64,256]{1,0:T(8,128)S(1)}, f32[64,256]{1,0:T(8,128)S(1)}, u32[]{:S(2)}, u32[]{:S(2)}) collective-permute-start(f32[64,256]{1,0:T(8,128)S(1)} %merge.5), channel_id=1, source_target_pairs={{0,24},{4,28},{8,16},{12,20},{16,8},{20,12},{24,0},{28,4},{1,25},{... | collective-permute-start | bytes 196616 | tf_op jit(solution)/shard_map/ppermute | solution.py:579
  279.2 8.7 %collective-permute-start.27 = (f32[64,512]{1,0:T(8,128)S(1)}, f32[64,512]{1,0:T(8,128)S(1)}, u32[]{:S(2)}, u32[]{:S(2)}) collective-permute-start(f32[64,512]{1,0:T(8,128)S(1)} %merge.4.refs_0_), channel_id=1, source_target_pairs={{0,3},{1,2},{2,1},{3,0},{4,7},{5,6},{6,5},{7,4},{8,11},{9,10},{10,... | collective-permute-start | bytes 393224 | tf_op jit(solution)/shard_map/ppermute | solution.py:579
  281.6 6.2 %collective-permute-start.26 = (f32[64,512]{1,0:T(8,128)S(1)}, f32[64,512]{1,0:T(8,128)S(1)}, u32[]{:S(2)}, u32[]{:S(2)}) collective-permute-start(f32[64,512]{1,0:T(8,128)S(1)} %merge.4.refs_0_), channel_id=1, source_target_pairs={{0,2},{1,3},{2,0},{3,1},{4,6},{5,7},{6,4},{7,5},{8,10},{9,11},{10,... | collective-permute-start | bytes 393224 | tf_op jit(solution)/shard_map/ppermute | solution.py:579
  282.1 5.7 %collective-permute-start.25 = (f32[64,512]{1,0:T(8,128)S(1)}, f32[64,512]{1,0:T(8,128)S(1)}, u32[]{:S(2)}, u32[]{:S(2)}) collective-permute-start(f32[64,512]{1,0:T(8,128)S(1)} %merge.4.refs_0_), channel_id=1, source_target_pairs={{0,1},{1,0},{2,3},{3,2},{4,5},{5,4},{6,7},{7,6},{8,9},{9,8},{10,11... | collective-permute-start | bytes 393224 | tf_op jit(solution)/shard_map/ppermute | solution.py:579
  282.6 5.2 %collective-permute-start.23 = (f32[64,256]{1,0:T(8,128)S(1)}, f32[64,256]{1,0:T(8,128)S(1)}, u32[]{:S(2)}, u32[]{:S(2)}) collective-permute-start(f32[64,256]{1,0:T(8,128)S(1)} %merge.5), channel_id=1, source_target_pairs={{0,16},{4,20},{8,24},{12,28},{16,0},{20,4},{24,8},{28,12},{1,17},{... | collective-permute-start | bytes 196616 | tf_op jit(solution)/shard_map/ppermute | solution.py:579
  282.6 5.2 %collective-permute-start.22 = (f32[64,256]{1,0:T(8,128)S(1)}, f32[64,256]{1,0:T(8,128)S(1)}, u32[]{:S(2)}, u32[]{:S(2)}) collective-permute-start(f32[64,256]{1,0:T(8,128)S(1)} %merge.5), channel_id=1, source_target_pairs={{0,8},{4,12},{8,0},{12,4},{16,24},{20,28},{24,16},{28,20},{1,9},{5... | collective-permute-start | bytes 196616 | tf_op jit(solution)/shard_map/ppermute | solution.py:579
  (7 other events, 130.1 us)

commit v7 on v6

--- a/solution.py
+++ b/solution.py
@@ -371,25 +371,31 @@
             out[d:, cols] = jnp.broadcast_to(peak + jnp.log(total), (8, LANES))
 
 
-def join_kernel(at_ref, ours, theirs, *refs):
+def lay(at_ref, pieces, outs, sem):
+    copies = []
+    for (src, place), out in zip(pieces, outs):
+        at = pl.multiple_of(at_ref[place], LANES)
+        dst = out.at[:, pl.ds(at, src.shape[1])]
+        copies.append(pltpu.make_async_copy(src, dst, sem.at[len(copies)]))
+        copies[-1].start()
+    for copy in copies:
+        copy.wait()
+
+
+def join_kernel(at_ref, ours, *refs):
     *pieces, col_out, row_out, sem = refs
     d = col_out.shape[0]
     count = ours.shape[0] // d
-    copies = []
-
-    def lay(src, out, place):
-        at = pl.multiple_of(at_ref[3 + place], LANES)
-        dst = out.at[:, pl.ds(at, src.shape[1])]
-        copies.append(pltpu.make_async_copy(src, dst, sem.at[len(copies)]))
-        copies[-1].start()
-
-    for which, stack in enumerate((ours, theirs)):
-        for k in range(count):
-            lay(stack.at[k * d : (k + 1) * d, :], col_out, which * count + k)
-    for k, piece_ref in enumerate(pieces):
-        lay(piece_ref, row_out, 2 * count + k)
-    for copy in copies:
-        copy.wait()
+    laid = [(ours.at[k * d : (k + 1) * d, :], 3 + k) for k in range(count)]
+    laid += [(piece_ref, 3 + 2 * count + k) for k, piece_ref in enumerate(pieces)]
+    lay(at_ref, laid, [col_out] * count + [row_out] * len(pieces), sem)
+
+
+def rest_kernel(at_ref, theirs, _, col_out, sem):
+    d = col_out.shape[0]
+    count = theirs.shape[0] // d
+    laid = [(theirs.at[k * d : (k + 1) * d, :], 3 + count + k) for k in range(count)]
+    lay(at_ref, laid, [col_out] * count, sem)
 
 
 VM = pl.BlockSpec(memory_space=pltpu.VMEM)
@@ -506,19 +512,37 @@
     )(at, whole, *others)
 
 
-def join(at, ours, theirs, pieces):
+def join(at, ours, pieces):
     d, width = pieces[0].shape
-    nt = 2 * ours.shape[0] // d * ours.shape[1]
-    ns = width * len(pieces)
+    count = ours.shape[0] // d
+    smem = pl.BlockSpec(memory_space=pltpu.SMEM)
     return pl.pallas_call(
         join_kernel,
-        out_shape=(jax.ShapeDtypeStruct((d, nt), F32), jax.ShapeDtypeStruct((d, ns), F32)),
-        in_specs=[pl.BlockSpec(memory_space=pltpu.SMEM)] + [VM] * (2 + len(pieces)),
+        out_shape=(
+            jax.ShapeDtypeStruct((d, 2 * count * ours.shape[1]), F32),
+            jax.ShapeDtypeStruct((d, width * len(pieces)), F32),
+        ),
+        in_specs=[smem] + [VM] * (1 + len(pieces)),
         out_specs=(ANY,) * 2,
-        scratch_shapes=[pltpu.SemaphoreType.DMA((at.shape[0] - 3,))],
+        scratch_shapes=[pltpu.SemaphoreType.DMA((count + len(pieces),))],
         compiler_params=PARAMS,
+        cost_estimate=cost(0, 2**20),
         name="join",
-    )(at, ours, theirs, *pieces)
+    )(at, ours, *pieces)
+
+
+def rest(at, theirs, col):
+    count = theirs.shape[0] // col.shape[0]
+    return pl.pallas_call(
+        rest_kernel,
+        out_shape=jax.ShapeDtypeStruct(col.shape, F32),
+        in_specs=[pl.BlockSpec(memory_space=pltpu.SMEM), VM, ANY],
+        out_specs=ANY,
+        scratch_shapes=[pltpu.SemaphoreType.DMA((count,))],
+        input_output_aliases={2: 0},
+        compiler_params=PARAMS,
+        name="rest",
+    )(at, theirs, col)
 
 
 def merged(first, second):
@@ -615,7 +639,8 @@
     column_pieces, source_pieces = lax.optimization_barrier(whole)
     ours = jnp.concatenate(column_pieces, axis=0)
     theirs = lax.ppermute(ours, "row", pair)
-    target_map, source_map = join(laid, ours, theirs, source_pieces)
+    target_map, source_map = join(laid, ours, source_pieces)
+    target_map = rest(laid, theirs, target_map)
     return f.reshape(-1), g.reshape(-1), source_map, target_map
 
 

time: 291 us -> 291 us (level)
  transfers between devices with their start and end apart: 29 -> 29, of which waited for: 16 -> 15; matrix products, arithmetic and copies ran while one was open for 0% -> 0% of each run, Pallas kernels for 0% -> 1%
where the time goes in v7:
time: 291 us
  Pallas kernels  234 us (80%)
  starting transfers between devices  38.8 us (13%)
  waiting for transfers between devices  16.2 us (6%)
    pallas_call x1, Pallas kernels, maps(): pl.pallas_call(functools.partial(maps_kernel, rows=256), out_shape=(vecto...  95.3 us
    pallas_call x2, Pallas kernels, sums(): pl.pallas_call(sums_kernel, out_shape=(near(ns), near(nt), near(ns), near...  85.9 us
    pallas_call x1, Pallas kernels, form(): pl.pallas_call(functools.partial(form_kernel, tiles=4), out_shape=(pltpu....  48.2 us
    ppermute x15, starting transfers between devices, lse_over(): lax.ppermute(part, axis, [(i, i ^ step) for i in range(n)])  23.1 us
    ppermute x6, starting transfers between devices, all_pieces(): lax.ppermute(own, axis, pairs(n, group, stride, k))  7.94 us
    ppermute x15, waiting for transfers between devices, lse_over(): lax.ppermute(part, axis, [(i, i ^ step) for i in range(n)])  7.78 us
    ppermute x6, starting transfers between devices, pieces_of(): lax.ppermute(piece(part, place[k], group), axis, pairs(n, group, stride, k))  7.48 us
  transfers between devices with their start and end apart: 29, of which 15 were waited for; matrix products, arithmetic and copies ran while one was open for 0% of the time, Pallas kernels for 1%

profile of v7, /device:TPU:0, one launch (start us, length us, event | category | flops | bytes accessed | tf_op | source)
XLA Modules:
  0.0 290.9 jit_solution(1256895611113445132)
XLA Ops:
  0.8 48.2 %form.1 = (f32[2048,2048]{1,0:T(8,128)S(1)}, f32[64,2048]{1,0:T(8,128)S(1)}, f32[64,2048]{1,0:T(8,128)S(1)}, f32[16,128]{1,0:T(8,128)S(1)}, f32[16,128]{1,0:T(8,128)S(1)}) custom-call(f32[64,2048]{1,0:T(8,128)} %x_hbm, f32[64,2048]{1,0:T(8,128)} %y_hbm.1, f32[16,128]{1,0:T(8,128)} %bitcast.18, f32[16,128]{1,0:T(8,128)} %bitcast.22), custom_call_target="tpu_custom_call" | custom-call | flops 5368709120 | bytes 16777216 | tf_op jit(solution)/shard_map/form/pallas_call | solution.py:426
  49.0 4.1 %collective-permute-start.2 = (f32[16,128]{1,0:T(8,128)S(1)}, f32[16,128]{1,0:T(8,128)S(1)}, u32[]{:S(2)}, u32[]{:S(2)}) collective-permute-start(f32[16,128]{1,0:T(8,128)S(1)} %get-tuple-element.49), channel_id=1, source_target_pairs={{0,16},{4,20},{8,24},{12,28},{16,0},{20,4},{24,8},{28,12},{1,17},{... | collective-permute-start | bytes 24584 | tf_op jit(solution)/shard_map/ppermute | solution.py:557
  53.1 1.5 collective-permute-start
  54.8 1.9 collective-permute-start.3
  56.8 1.5 collective-permute-start.1
  58.6 1.9 collective-permute-done.1
  60.6 42.9 %sums.2 = (f32[16,128]{1,0:T(8,128)S(1)}, f32[16,128]{1,0:T(8,128)S(1)}, f32[16,128]{1,0:T(8,128)S(1)}, f32[16,128]{1,0:T(8,128)S(1)}) custom-call(f32[2048,2048]{1,0:T(8,128)S(1)} %get-tuple-element.45.k_ref, f32[64,2048]{1,0:T(8,128)S(1)} %get-tuple-element.46.x_ref, f32[64,2048]{1,0:T(8,128)S(1)} %get-tuple-element.47.y_ref, ...), custom_call_target="tpu_custom_call" | custom-call | flops 16777216 | bytes 16777216 | tf_op jit(solution)/shard_map/sums/pallas_call | solution.py:455
  103.5 2.6 collective-permute-start.7
  106.1 1.5 collective-permute-start.5
  108.1 1.6 collective-permute-start.8
  109.7 1.6 collective-permute-start.6
  111.9 1.5 collective-permute-done.6
  113.5 43.0 %sums.3 = (f32[16,128]{1,0:T(8,128)S(1)}, f32[16,128]{1,0:T(8,128)S(1)}, f32[16,128]{1,0:T(8,128)S(1)}, f32[16,128]{1,0:T(8,128)S(1)}) custom-call(f32[2048,2048]{1,0:T(8,128)S(1)} %get-tuple-element.45.k_ref, f32[64,2048]{1,0:T(8,128)S(1)} %get-tuple-element.46.x_ref, f32[64,2048]{1,0:T(8,128)S(1)} %get-tuple-element.47.y_ref, ...), custom_call_target="tpu_custom_call" | custom-call | flops 16777216 | bytes 16777216 | tf_op jit(solution)/shard_map/sums/pallas_call | solution.py:455
  156.6 2.2 collective-permute-start.12
  158.8 1.5 collective-permute-start.10
  162.4 1.6 collective-permute-start.11
  166.2 95.3 %maps.1 = (f32[16,128]{1,0:T(8,128)}, f32[16,128]{1,0:T(8,128)}, f32[72,2048]{1,0:T(8,128)S(1)}, f32[72,2048]{1,0:T(8,128)S(1)}) custom-call(f32[2048,2048]{1,0:T(8,128)S(1)} %get-tuple-element.45.k_ref, f32[64,2048]{1,0:T(8,128)S(1)} %get-tuple-element.46.x_ref, f32[64,2048]{1,0:T(8,128)S(1)} %get-tuple-element.47.y_ref, ...), custom_call_target="tpu_custom_call" | custom-call | flops 8589934592 | bytes 16777216 | tf_op jit(solution)/shard_map/maps/pallas_call | solution.py:476
  262.0 2.5 collective-permute-start.21
  266.4 2.8 collective-permute-start.18
  273.0 2.8 collective-permute-done.17.refs_1_
  276.4 2.7 collective-permute-start.24
  279.2 2.5 collective-permute-start.27
  282.6 1.7 collective-permute-start.22
  284.4 3.4 %collective-permute-done.23 = f32[64,256]{1,0:T(8,128)S(1)} collective-permute-done((f32[64,256]{1,0:T(8,128)S(1)}, f32[64,256]{1,0:T(8,128)S(1)}, u32[]{:S(2)}, u32[]{:S(2)}) %collective-permute-start.23) | collective-permute-done | bytes 65568 | tf_op jit(solution)/shard_map/ppermute | solution.py:603
  (71 shorter events, 16.8 us)
Async XLA Ops:
  49.0 5.7 %collective-permute-start.2 = (f32[16,128]{1,0:T(8,128)S(1)}, f32[16,128]{1,0:T(8,128)S(1)}, u32[]{:S(2)}, u32[]{:S(2)}) collective-permute-start(f32[16,128]{1,0:T(8,128)S(1)} %get-tuple-element.49), channel_id=1, source_target_pairs={{0,16},{4,20},{8,24},{12,28},{16,0},{20,4},{24,8},{28,12},{1,17},{... | collective-permute-start | bytes 24584 | tf_op jit(solution)/shard_map/ppermute | solution.py:557
  54.8 3.7 %collective-permute-start.3 = (f32[16,128]{1,0:T(8,128)S(1)}, f32[16,128]{1,0:T(8,128)S(1)}, u32[]{:S(2)}, u32[]{:S(2)}) collective-permute-start(f32[16,128]{1,0:T(8,128)S(1)} %log_add_fusion.12), channel_id=1, source_target_pairs={{0,8},{4,12},{8,0},{12,4},{16,24},{20,28},{24,16},{28,20},{1,9},{5... | collective-permute-start | bytes 24584 | tf_op jit(solution)/shard_map/ppermute | solution.py:557
  56.8 3.7 %collective-permute-start.1 = (f32[16,128]{1,0:T(8,128)S(1)}, f32[16,128]{1,0:T(8,128)S(1)}, u32[]{:S(2)}, u32[]{:S(2)}) collective-permute-start(f32[16,128]{1,0:T(8,128)S(1)} %log_add_fusion.14), channel_id=1, source_target_pairs={{0,1},{1,0},{2,3},{3,2},{4,5},{5,4},{6,7},{7,6},{8,9},{9,8},{10,11... | collective-permute-start | bytes 24584 | tf_op jit(solution)/shard_map/ppermute | solution.py:557
  103.5 4.6 %collective-permute-start.7 = (f32[16,128]{1,0:T(8,128)S(1)}, f32[16,128]{1,0:T(8,128)S(1)}, u32[]{:S(2)}, u32[]{:S(2)}) collective-permute-start(f32[16,128]{1,0:T(8,128)S(1)} %get-tuple-element.53), channel_id=1, source_target_pairs={{0,16},{4,20},{8,24},{12,28},{16,0},{20,4},{24,8},{28,12},{1,17},{... | collective-permute-start | bytes 24584 | tf_op jit(solution)/shard_map/ppermute | solution.py:557
  106.1 3.7 %collective-permute-start.5 = (f32[16,128]{1,0:T(8,128)S(1)}, f32[16,128]{1,0:T(8,128)S(1)}, u32[]{:S(2)}, u32[]{:S(2)}) collective-permute-start(f32[16,128]{1,0:T(8,128)S(1)} %get-tuple-element.52), channel_id=1, source_target_pairs={{0,2},{1,3},{2,0},{3,1},{4,6},{5,7},{6,4},{7,5},{8,10},{9,11},{10,... | collective-permute-start | bytes 24584 | tf_op jit(solution)/shard_map/ppermute | solution.py:557
  108.1 3.7 %collective-permute-start.8 = (f32[16,128]{1,0:T(8,128)S(1)}, f32[16,128]{1,0:T(8,128)S(1)}, u32[]{:S(2)}, u32[]{:S(2)}) collective-permute-start(f32[16,128]{1,0:T(8,128)S(1)} %log_add_fusion.7), channel_id=1, source_target_pairs={{0,8},{4,12},{8,0},{12,4},{16,24},{20,28},{24,16},{28,20},{1,9},{5... | collective-permute-start | bytes 24584 | tf_op jit(solution)/shard_map/ppermute | solution.py:557
  109.7 3.7 %collective-permute-start.6 = (f32[16,128]{1,0:T(8,128)S(1)}, f32[16,128]{1,0:T(8,128)S(1)}, u32[]{:S(2)}, u32[]{:S(2)}) collective-permute-start(f32[16,128]{1,0:T(8,128)S(1)} %log_add_fusion.9), channel_id=1, source_target_pairs={{0,1},{1,0},{2,3},{3,2},{4,5},{5,4},{6,7},{7,6},{8,9},{9,8},{10,11... | collective-permute-start | bytes 24584 | tf_op jit(solution)/shard_map/ppermute | solution.py:557
  156.6 4.6 %collective-permute-start.12 = (f32[16,128]{1,0:T(8,128)S(1)}, f32[16,128]{1,0:T(8,128)S(1)}, u32[]{:S(2)}, u32[]{:S(2)}) collective-permute-start(f32[16,128]{1,0:T(8,128)S(1)} %get-tuple-element.57), channel_id=1, source_target_pairs={{0,16},{4,20},{8,24},{12,28},{16,0},{20,4},{24,8},{28,12},{1,17},{... | collective-permute-start | bytes 24584 | tf_op jit(solution)/shard_map/ppermute | solution.py:557
  158.8 3.7 %collective-permute-start.10 = (f32[16,128]{1,0:T(8,128)S(1)}, f32[16,128]{1,0:T(8,128)S(1)}, u32[]{:S(2)}, u32[]{:S(2)}) collective-permute-start(f32[16,128]{1,0:T(8,128)S(1)} %get-tuple-element.56), channel_id=1, source_target_pairs={{0,2},{1,3},{2,0},{3,1},{4,6},{5,7},{6,4},{7,5},{8,10},{9,11},{10,... | collective-permute-start | bytes 24584 | tf_op jit(solution)/shard_map/ppermute | solution.py:557
  161.2 3.7 %collective-permute-start.13 = (f32[16,128]{1,0:T(8,128)S(1)}, f32[16,128]{1,0:T(8,128)S(1)}, u32[]{:S(2)}, u32[]{:S(2)}) collective-permute-start(f32[16,128]{1,0:T(8,128)S(1)} %log_add_fusion.2), channel_id=1, source_target_pairs={{0,8},{4,12},{8,0},{12,4},{16,24},{20,28},{24,16},{28,20},{1,9},{5... | collective-permute-start | bytes 24584 | tf_op jit(solution)/shard_map/ppermute | solution.py:557
  162.4 3.7 %collective-permute-start.11 = (f32[16,128]{1,0:T(8,128)S(1)}, f32[16,128]{1,0:T(8,128)S(1)}, u32[]{:S(2)}, u32[]{:S(2)}) collective-permute-start(f32[16,128]{1,0:T(8,128)S(1)} %log_add_fusion.4), channel_id=1, source_target_pairs={{0,1},{1,0},{2,3},{3,2},{4,5},{5,4},{6,7},{7,6},{8,9},{9,8},{10,11... | collective-permute-start | bytes 24584 | tf_op jit(solution)/shard_map/ppermute | solution.py:557
  261.6 4.0 %collective-permute-start.15 = (f32[72,1024]{1,0:T(8,128)S(1)}, f32[72,1024]{1,0:T(8,128)S(1)}, u32[]{:S(2)}, u32[]{:S(2)}) collective-permute-start(f32[72,1024]{1,0:T(8,128)S(1)} %constant_dynamic-slice_fusion.6), channel_id=1, source_target_pairs={{0,4},{4,0},{8,12},{12,8},{16,20},{20,16},{24,28},{28,24},{1,5},{5... | collective-permute-start | bytes 884744 | tf_op jit(solution)/shard_map/ppermute | solution.py:631
  262.0 7.6 %collective-permute-start.21 = (f32[72,512]{1,0:T(8,128)S(1)}, f32[72,512]{1,0:T(8,128)S(1)}, u32[]{:S(2)}, u32[]{:S(2)}) collective-permute-start(f32[72,512]{1,0:T(8,128)S(1)} %get-tuple-element.84), channel_id=1, source_target_pairs={{0,3},{1,2},{2,1},{3,0},{4,7},{5,6},{6,5},{7,4},{8,11},{9,10},{10,... | collective-permute-start | bytes 442376 | tf_op jit(solution)/shard_map/ppermute | solution.py:596
  264.5 7.7 %collective-permute-start.20 = (f32[72,512]{1,0:T(8,128)S(1)}, f32[72,512]{1,0:T(8,128)S(1)}, u32[]{:S(2)}, u32[]{:S(2)}) collective-permute-start(f32[72,512]{1,0:T(8,128)S(1)} %get-tuple-element.85), channel_id=1, source_target_pairs={{0,2},{1,3},{2,0},{3,1},{4,6},{5,7},{6,4},{7,5},{8,10},{9,11},{10,... | collective-permute-start | bytes 442376 | tf_op jit(solution)/shard_map/ppermute | solution.py:596
  265.0 7.3 %collective-permute-start.19 = (f32[72,512]{1,0:T(8,128)S(1)}, f32[72,512]{1,0:T(8,128)S(1)}, u32[]{:S(2)}, u32[]{:S(2)}) collective-permute-start(f32[72,512]{1,0:T(8,128)S(1)} %get-tuple-element.86), channel_id=1, source_target_pairs={{0,1},{1,0},{2,3},{3,2},{4,5},{5,4},{6,7},{7,6},{8,9},{9,8},{10,11... | collective-permute-start | bytes 442376 | tf_op jit(solution)/shard_map/ppermute | solution.py:596
  266.4 6.6 %collective-permute-start.18 = (f32[72,256]{1,0:T(8,128)S(1)}, f32[72,256]{1,0:T(8,128)S(1)}, u32[]{:S(2)}, u32[]{:S(2)}) collective-permute-start(f32[72,256]{1,0:T(8,128)S(1)} %get-tuple-element.87), channel_id=1, source_target_pairs={{0,24},{4,28},{8,16},{12,20},{16,8},{20,12},{24,0},{28,4},{1,25},{... | collective-permute-start | bytes 221192 | tf_op jit(solution)/shard_map/ppermute | solution.py:596
  269.1 6.7 %collective-permute-start.17 = (f32[72,256]{1,0:T(8,128)S(1)}, f32[72,256]{1,0:T(8,128)S(1)}, u32[]{:S(2)}, u32[]{:S(2)}) collective-permute-start(f32[72,256]{1,0:T(8,128)S(1)} %get-tuple-element.88), channel_id=1, source_target_pairs={{0,16},{4,20},{8,24},{12,28},{16,0},{20,4},{24,8},{28,12},{1,17},{... | collective-permute-start | bytes 221192 | tf_op jit(solution)/shard_map/ppermute | solution.py:596
  269.7 6.2 %collective-permute-start.16 = (f32[72,256]{1,0:T(8,128)S(1)}, f32[72,256]{1,0:T(8,128)S(1)}, u32[]{:S(2)}, u32[]{:S(2)}) collective-permute-start(f32[72,256]{1,0:T(8,128)S(1)} %get-tuple-element.89), channel_id=1, source_target_pairs={{0,8},{4,12},{8,0},{12,4},{16,24},{20,28},{24,16},{28,20},{1,9},{5... | collective-permute-start | bytes 221192 | tf_op jit(solution)/shard_map/ppermute | solution.py:596
  276.4 6.2 %collective-permute-start.24 = (f32[64,256]{1,0:T(8,128)S(1)}, f32[64,256]{1,0:T(8,128)S(1)}, u32[]{:S(2)}, u32[]{:S(2)}) collective-permute-start(f32[64,256]{1,0:T(8,128)S(1)} %merge.5), channel_id=1, source_target_pairs={{0,24},{4,28},{8,16},{12,20},{16,8},{20,12},{24,0},{28,4},{1,25},{... | collective-permute-start | bytes 196616 | tf_op jit(solution)/shard_map/ppermute | solution.py:603
  279.2 8.7 %collective-permute-start.27 = (f32[64,512]{1,0:T(8,128)S(1)}, f32[64,512]{1,0:T(8,128)S(1)}, u32[]{:S(2)}, u32[]{:S(2)}) collective-permute-start(f32[64,512]{1,0:T(8,128)S(1)} %merge.4.refs_0_), channel_id=1, source_target_pairs={{0,3},{1,2},{2,1},{3,0},{4,7},{5,6},{6,5},{7,4},{8,11},{9,10},{10,... | collective-permute-start | bytes 393224 | tf_op jit(solution)/shard_map/ppermute | solution.py:603
  281.6 6.2 %collective-permute-start.26 = (f32[64,512]{1,0:T(8,128)S(1)}, f32[64,512]{1,0:T(8,128)S(1)}, u32[]{:S(2)}, u32[]{:S(2)}) collective-permute-start(f32[64,512]{1,0:T(8,128)S(1)} %merge.4.refs_0_), channel_id=1, source_target_pairs={{0,2},{1,3},{2,0},{3,1},{4,6},{5,7},{6,4},{7,5},{8,10},{9,11},{10,... | collective-permute-start | bytes 393224 | tf_op jit(solution)/shard_map/ppermute | solution.py:603
  282.1 5.7 %collective-permute-start.25 = (f32[64,512]{1,0:T(8,128)S(1)}, f32[64,512]{1,0:T(8,128)S(1)}, u32[]{:S(2)}, u32[]{:S(2)}) collective-permute-start(f32[64,512]{1,0:T(8,128)S(1)} %merge.4.refs_0_), channel_id=1, source_target_pairs={{0,1},{1,0},{2,3},{3,2},{4,5},{5,4},{6,7},{7,6},{8,9},{9,8},{10,11... | collective-permute-start | bytes 393224 | tf_op jit(solution)/shard_map/ppermute | solution.py:603
  282.6 5.2 %collective-permute-start.23 = (f32[64,256]{1,0:T(8,128)S(1)}, f32[64,256]{1,0:T(8,128)S(1)}, u32[]{:S(2)}, u32[]{:S(2)}) collective-permute-start(f32[64,256]{1,0:T(8,128)S(1)} %merge.5), channel_id=1, source_target_pairs={{0,16},{4,20},{8,24},{12,28},{16,0},{20,4},{24,8},{28,12},{1,17},{... | collective-permute-start | bytes 196616 | tf_op jit(solution)/shard_map/ppermute | solution.py:603
  282.6 5.2 %collective-permute-start.22 = (f32[64,256]{1,0:T(8,128)S(1)}, f32[64,256]{1,0:T(8,128)S(1)}, u32[]{:S(2)}, u32[]{:S(2)}) collective-permute-start(f32[64,256]{1,0:T(8,128)S(1)} %merge.5), channel_id=1, source_target_pairs={{0,8},{4,12},{8,0},{12,4},{16,24},{20,28},{24,16},{28,20},{1,9},{5... | collective-permute-start | bytes 196616 | tf_op jit(solution)/shard_map/ppermute | solution.py:603
  (7 other events, 130.1 us)

commit v8 on v7

--- a/solution.py
+++ b/solution.py
@@ -166,23 +166,25 @@
     copies = [pltpu.make_async_copy(src, dst, sem.at[i]) for i, (src, dst) in enumerate(pairs)]
     for copy in copies:
         copy.start()
-    for copy in copies:
-        copy.wait()
+    return copies
 
 
 def form_kernel(
     x_hbm, y_hbm, a_hbm, b_hbm, k_ref, x_ref, y_ref, row_ref, col_ref, xa, ya, ub, r_s, t_s, vs, cs, sem, *, tiles
 ):
     ns, nt = x_ref.shape[1], y_ref.shape[1]
-    fetch(((x_hbm, x_ref), (y_hbm, y_ref), (a_hbm, r_s), (b_hbm, t_s)), sem)
+    targets, *others = fetch(((y_hbm, y_ref), (x_hbm, x_ref), (a_hbm, r_s), (b_hbm, t_s)), sem)
+    cs[...] = jnp.zeros_like(cs)
+    targets.wait()
+    targets_operand(y_ref, ya)
+    for copy in others:
+        copy.wait()
     r_s[...] = jnp.log(r_s[...])
     t_s[...] = jnp.log(t_s[...])
     u, r_top, u_fine = factors(r_s[...])
     v, t_top, v_fine = factors(t_s[...])
     row_ref[...] = u
     vs[...] = v
-    targets_operand(y_ref, ya)
-    cs[...] = jnp.zeros_like(cs)
     wide = tiles * LANES
     tall = xa.shape[1]
 

time: 291 us -> 291 us (level)
  transfers between devices with their start and end apart: 29 -> 29, of which waited for: 15 -> 14; matrix products, arithmetic and copies ran while one was open for 0% -> 0% of each run, Pallas kernels for 1% -> 1%
where the time goes in v8:
time: 291 us
  Pallas kernels  234 us (80%)
  starting transfers between devices  39 us (13%)
  waiting for transfers between devices  16 us (5%)
    pallas_call x1, Pallas kernels, maps(): pl.pallas_call(functools.partial(maps_kernel, rows=256), out_shape=(vecto...  95.3 us
    pallas_call x2, Pallas kernels, sums(): pl.pallas_call(sums_kernel, out_shape=(near(ns), near(nt), near(ns), near...  85.9 us
    pallas_call x1, Pallas kernels, form(): pl.pallas_call(functools.partial(form_kernel, tiles=4), out_shape=(pltpu....  47.9 us
    ppermute x15, starting transfers between devices, lse_over(): lax.ppermute(part, axis, [(i, i ^ step) for i in range(n)])  23.3 us
    ppermute x6, starting transfers between devices, all_pieces(): lax.ppermute(own, axis, pairs(n, group, stride, k))  7.94 us
    ppermute x15, waiting for transfers between devices, lse_over(): lax.ppermute(part, axis, [(i, i ^ step) for i in range(n)])  7.61 us
    ppermute x6, starting transfers between devices, pieces_of(): lax.ppermute(piece(part, place[k], group), axis, pairs(n, group, stride, k))  7.48 us
  transfers between devices with their start and end apart: 29, of which 14 were waited for; matrix products, arithmetic and copies ran while one was open for 0% of the time, Pallas kernels for 1%

profile of v8, /device:TPU:0, one launch (start us, length us, event | category | flops | bytes accessed | tf_op | source)
XLA Modules:
  0.0 290.6 jit_solution(2294747377281290783)
XLA Ops:
  0.8 47.9 %form.1 = (f32[2048,2048]{1,0:T(8,128)S(1)}, f32[64,2048]{1,0:T(8,128)S(1)}, f32[64,2048]{1,0:T(8,128)S(1)}, f32[16,128]{1,0:T(8,128)S(1)}, f32[16,128]{1,0:T(8,128)S(1)}) custom-call(f32[64,2048]{1,0:T(8,128)} %x_hbm, f32[64,2048]{1,0:T(8,128)} %y_hbm.1, f32[16,128]{1,0:T(8,128)} %bitcast.18, f32[16,128]{1,0:T(8,128)} %bitcast.22), custom_call_target="tpu_custom_call" | custom-call | flops 5368709120 | bytes 16777216 | tf_op jit(solution)/shard_map/form/pallas_call | solution.py:428
  48.8 4.1 %collective-permute-start.2 = (f32[16,128]{1,0:T(8,128)S(1)}, f32[16,128]{1,0:T(8,128)S(1)}, u32[]{:S(2)}, u32[]{:S(2)}) collective-permute-start(f32[16,128]{1,0:T(8,128)S(1)} %get-tuple-element.49), channel_id=1, source_target_pairs={{0,16},{4,20},{8,24},{12,28},{16,0},{20,4},{24,8},{28,12},{1,17},{... | collective-permute-start | bytes 24584 | tf_op jit(solution)/shard_map/ppermute | solution.py:559
  52.8 1.5 collective-permute-start
  54.5 2.0 collective-permute-start.3
  56.5 1.6 collective-permute-start.1
  58.3 1.9 collective-permute-done.1
  60.3 42.9 %sums.2 = (f32[16,128]{1,0:T(8,128)S(1)}, f32[16,128]{1,0:T(8,128)S(1)}, f32[16,128]{1,0:T(8,128)S(1)}, f32[16,128]{1,0:T(8,128)S(1)}) custom-call(f32[2048,2048]{1,0:T(8,128)S(1)} %get-tuple-element.45.k_ref, f32[64,2048]{1,0:T(8,128)S(1)} %get-tuple-element.46.x_ref, f32[64,2048]{1,0:T(8,128)S(1)} %get-tuple-element.47.y_ref, ...), custom_call_target="tpu_custom_call" | custom-call | flops 16777216 | bytes 16777216 | tf_op jit(solution)/shard_map/sums/pallas_call | solution.py:457
  103.2 2.6 collective-permute-start.7
  105.8 1.5 collective-permute-start.5
  107.8 1.6 collective-permute-start.8
  109.5 1.6 collective-permute-start.6
  111.6 1.6 collective-permute-done.6
  113.2 43.0 %sums.3 = (f32[16,128]{1,0:T(8,128)S(1)}, f32[16,128]{1,0:T(8,128)S(1)}, f32[16,128]{1,0:T(8,128)S(1)}, f32[16,128]{1,0:T(8,128)S(1)}) custom-call(f32[2048,2048]{1,0:T(8,128)S(1)} %get-tuple-element.45.k_ref, f32[64,2048]{1,0:T(8,128)S(1)} %get-tuple-element.46.x_ref, f32[64,2048]{1,0:T(8,128)S(1)} %get-tuple-element.47.y_ref, ...), custom_call_target="tpu_custom_call" | custom-call | flops 16777216 | bytes 16777216 | tf_op jit(solution)/shard_map/sums/pallas_call | solution.py:457
  156.3 2.2 collective-permute-start.12
  158.5 1.5 collective-permute-start.10
  162.2 1.6 collective-permute-start.11
  165.9 95.3 %maps.1 = (f32[16,128]{1,0:T(8,128)}, f32[16,128]{1,0:T(8,128)}, f32[72,2048]{1,0:T(8,128)S(1)}, f32[72,2048]{1,0:T(8,128)S(1)}) custom-call(f32[2048,2048]{1,0:T(8,128)S(1)} %get-tuple-element.45.k_ref, f32[64,2048]{1,0:T(8,128)S(1)} %get-tuple-element.46.x_ref, f32[64,2048]{1,0:T(8,128)S(1)} %get-tuple-element.47.y_ref, ...), custom_call_target="tpu_custom_call" | custom-call | flops 8589934592 | bytes 16777216 | tf_op jit(solution)/shard_map/maps/pallas_call | solution.py:478
  261.7 2.5 collective-permute-start.21
  266.1 2.8 collective-permute-start.18
  272.7 2.9 collective-permute-done.17.refs_1_
  276.2 2.7 collective-permute-start.24
  278.9 2.5 collective-permute-start.27
  282.4 1.7 collective-permute-start.22
  284.1 3.4 %collective-permute-done.23 = f32[64,256]{1,0:T(8,128)S(1)} collective-permute-done((f32[64,256]{1,0:T(8,128)S(1)}, f32[64,256]{1,0:T(8,128)S(1)}, u32[]{:S(2)}, u32[]{:S(2)}) %collective-permute-start.23) | collective-permute-done | bytes 65568 | tf_op jit(solution)/shard_map/ppermute | solution.py:605
  (71 shorter events, 16.6 us)
Async XLA Ops:
  48.8 5.7 %collective-permute-start.2 = (f32[16,128]{1,0:T(8,128)S(1)}, f32[16,128]{1,0:T(8,128)S(1)}, u32[]{:S(2)}, u32[]{:S(2)}) collective-permute-start(f32[16,128]{1,0:T(8,128)S(1)} %get-tuple-element.49), channel_id=1, source_target_pairs={{0,16},{4,20},{8,24},{12,28},{16,0},{20,4},{24,8},{28,12},{1,17},{... | collective-permute-start | bytes 24584 | tf_op jit(solution)/shard_map/ppermute | solution.py:559
  52.8 3.7 %collective-permute-start = (f32[16,128]{1,0:T(8,128)S(1)}, f32[16,128]{1,0:T(8,128)S(1)}, u32[]{:S(2)}, u32[]{:S(2)}) collective-permute-start(f32[16,128]{1,0:T(8,128)S(1)} %get-tuple-element.48), channel_id=1, source_target_pairs={{0,2},{1,3},{2,0},{3,1},{4,6},{5,7},{6,4},{7,5},{8,10},{9,11},{10,... | collective-permute-start | bytes 24584 | tf_op jit(solution)/shard_map/ppermute | solution.py:559
  54.5 3.7 %collective-permute-start.3 = (f32[16,128]{1,0:T(8,128)S(1)}, f32[16,128]{1,0:T(8,128)S(1)}, u32[]{:S(2)}, u32[]{:S(2)}) collective-permute-start(f32[16,128]{1,0:T(8,128)S(1)} %log_add_fusion.12), channel_id=1, source_target_pairs={{0,8},{4,12},{8,0},{12,4},{16,24},{20,28},{24,16},{28,20},{1,9},{5... | collective-permute-start | bytes 24584 | tf_op jit(solution)/shard_map/ppermute | solution.py:559
  56.5 3.7 %collective-permute-start.1 = (f32[16,128]{1,0:T(8,128)S(1)}, f32[16,128]{1,0:T(8,128)S(1)}, u32[]{:S(2)}, u32[]{:S(2)}) collective-permute-start(f32[16,128]{1,0:T(8,128)S(1)} %log_add_fusion.14), channel_id=1, source_target_pairs={{0,1},{1,0},{2,3},{3,2},{4,5},{5,4},{6,7},{7,6},{8,9},{9,8},{10,11... | collective-permute-start | bytes 24584 | tf_op jit(solution)/shard_map/ppermute | solution.py:559
  103.2 4.6 %collective-permute-start.7 = (f32[16,128]{1,0:T(8,128)S(1)}, f32[16,128]{1,0:T(8,128)S(1)}, u32[]{:S(2)}, u32[]{:S(2)}) collective-permute-start(f32[16,128]{1,0:T(8,128)S(1)} %get-tuple-element.53), channel_id=1, source_target_pairs={{0,16},{4,20},{8,24},{12,28},{16,0},{20,4},{24,8},{28,12},{1,17},{... | collective-permute-start | bytes 24584 | tf_op jit(solution)/shard_map/ppermute | solution.py:559
  107.8 3.7 %collective-permute-start.8 = (f32[16,128]{1,0:T(8,128)S(1)}, f32[16,128]{1,0:T(8,128)S(1)}, u32[]{:S(2)}, u32[]{:S(2)}) collective-permute-start(f32[16,128]{1,0:T(8,128)S(1)} %log_add_fusion.7), channel_id=1, source_target_pairs={{0,8},{4,12},{8,0},{12,4},{16,24},{20,28},{24,16},{28,20},{1,9},{5... | collective-permute-start | bytes 24584 | tf_op jit(solution)/shard_map/ppermute | solution.py:559
  109.5 3.7 %collective-permute-start.6 = (f32[16,128]{1,0:T(8,128)S(1)}, f32[16,128]{1,0:T(8,128)S(1)}, u32[]{:S(2)}, u32[]{:S(2)}) collective-permute-start(f32[16,128]{1,0:T(8,128)S(1)} %log_add_fusion.9), channel_id=1, source_target_pairs={{0,1},{1,0},{2,3},{3,2},{4,5},{5,4},{6,7},{7,6},{8,9},{9,8},{10,11... | collective-permute-start | bytes 24584 | tf_op jit(solution)/shard_map/ppermute | solution.py:559
  156.3 4.6 %collective-permute-start.12 = (f32[16,128]{1,0:T(8,128)S(1)}, f32[16,128]{1,0:T(8,128)S(1)}, u32[]{:S(2)}, u32[]{:S(2)}) collective-permute-start(f32[16,128]{1,0:T(8,128)S(1)} %get-tuple-element.57), channel_id=1, source_target_pairs={{0,16},{4,20},{8,24},{12,28},{16,0},{20,4},{24,8},{28,12},{1,17},{... | collective-permute-start | bytes 24584 | tf_op jit(solution)/shard_map/ppermute | solution.py:559
  158.5 3.7 %collective-permute-start.10 = (f32[16,128]{1,0:T(8,128)S(1)}, f32[16,128]{1,0:T(8,128)S(1)}, u32[]{:S(2)}, u32[]{:S(2)}) collective-permute-start(f32[16,128]{1,0:T(8,128)S(1)} %get-tuple-element.56), channel_id=1, source_target_pairs={{0,2},{1,3},{2,0},{3,1},{4,6},{5,7},{6,4},{7,5},{8,10},{9,11},{10,... | collective-permute-start | bytes 24584 | tf_op jit(solution)/shard_map/ppermute | solution.py:559
  160.9 3.7 %collective-permute-start.13 = (f32[16,128]{1,0:T(8,128)S(1)}, f32[16,128]{1,0:T(8,128)S(1)}, u32[]{:S(2)}, u32[]{:S(2)}) collective-permute-start(f32[16,128]{1,0:T(8,128)S(1)} %log_add_fusion.2), channel_id=1, source_target_pairs={{0,8},{4,12},{8,0},{12,4},{16,24},{20,28},{24,16},{28,20},{1,9},{5... | collective-permute-start | bytes 24584 | tf_op jit(solution)/shard_map/ppermute | solution.py:559
  162.2 3.7 %collective-permute-start.11 = (f32[16,128]{1,0:T(8,128)S(1)}, f32[16,128]{1,0:T(8,128)S(1)}, u32[]{:S(2)}, u32[]{:S(2)}) collective-permute-start(f32[16,128]{1,0:T(8,128)S(1)} %log_add_fusion.4), channel_id=1, source_target_pairs={{0,1},{1,0},{2,3},{3,2},{4,5},{5,4},{6,7},{7,6},{8,9},{9,8},{10,11... | collective-permute-start | bytes 24584 | tf_op jit(solution)/shard_map/ppermute | solution.py:559
  261.3 4.0 %collective-permute-start.15 = (f32[72,1024]{1,0:T(8,128)S(1)}, f32[72,1024]{1,0:T(8,128)S(1)}, u32[]{:S(2)}, u32[]{:S(2)}) collective-permute-start(f32[72,1024]{1,0:T(8,128)S(1)} %constant_dynamic-slice_fusion.6), channel_id=1, source_target_pairs={{0,4},{4,0},{8,12},{12,8},{16,20},{20,16},{24,28},{28,24},{1,5},{5... | collective-permute-start | bytes 884744 | tf_op jit(solution)/shard_map/ppermute | solution.py:633
  261.7 7.6 %collective-permute-start.21 = (f32[72,512]{1,0:T(8,128)S(1)}, f32[72,512]{1,0:T(8,128)S(1)}, u32[]{:S(2)}, u32[]{:S(2)}) collective-permute-start(f32[72,512]{1,0:T(8,128)S(1)} %get-tuple-element.84), channel_id=1, source_target_pairs={{0,3},{1,2},{2,1},{3,0},{4,7},{5,6},{6,5},{7,4},{8,11},{9,10},{10,... | collective-permute-start | bytes 442376 | tf_op jit(solution)/shard_map/ppermute | solution.py:598
  264.3 7.7 %collective-permute-start.20 = (f32[72,512]{1,0:T(8,128)S(1)}, f32[72,512]{1,0:T(8,128)S(1)}, u32[]{:S(2)}, u32[]{:S(2)}) collective-permute-start(f32[72,512]{1,0:T(8,128)S(1)} %get-tuple-element.85), channel_id=1, source_target_pairs={{0,2},{1,3},{2,0},{3,1},{4,6},{5,7},{6,4},{7,5},{8,10},{9,11},{10,... | collective-permute-start | bytes 442376 | tf_op jit(solution)/shard_map/ppermute | solution.py:598
  264.8 7.3 %collective-permute-start.19 = (f32[72,512]{1,0:T(8,128)S(1)}, f32[72,512]{1,0:T(8,128)S(1)}, u32[]{:S(2)}, u32[]{:S(2)}) collective-permute-start(f32[72,512]{1,0:T(8,128)S(1)} %get-tuple-element.86), channel_id=1, source_target_pairs={{0,1},{1,0},{2,3},{3,2},{4,5},{5,4},{6,7},{7,6},{8,9},{9,8},{10,11... | collective-permute-start | bytes 442376 | tf_op jit(solution)/shard_map/ppermute | solution.py:598
  266.1 6.6 %collective-permute-start.18 = (f32[72,256]{1,0:T(8,128)S(1)}, f32[72,256]{1,0:T(8,128)S(1)}, u32[]{:S(2)}, u32[]{:S(2)}) collective-permute-start(f32[72,256]{1,0:T(8,128)S(1)} %get-tuple-element.87), channel_id=1, source_target_pairs={{0,24},{4,28},{8,16},{12,20},{16,8},{20,12},{24,0},{28,4},{1,25},{... | collective-permute-start | bytes 221192 | tf_op jit(solution)/shard_map/ppermute | solution.py:598
  268.8 6.7 %collective-permute-start.17 = (f32[72,256]{1,0:T(8,128)S(1)}, f32[72,256]{1,0:T(8,128)S(1)}, u32[]{:S(2)}, u32[]{:S(2)}) collective-permute-start(f32[72,256]{1,0:T(8,128)S(1)} %get-tuple-element.88), channel_id=1, source_target_pairs={{0,16},{4,20},{8,24},{12,28},{16,0},{20,4},{24,8},{28,12},{1,17},{... | collective-permute-start | bytes 221192 | tf_op jit(solution)/shard_map/ppermute | solution.py:598
  269.4 6.2 %collective-permute-start.16 = (f32[72,256]{1,0:T(8,128)S(1)}, f32[72,256]{1,0:T(8,128)S(1)}, u32[]{:S(2)}, u32[]{:S(2)}) collective-permute-start(f32[72,256]{1,0:T(8,128)S(1)} %get-tuple-element.89), channel_id=1, source_target_pairs={{0,8},{4,12},{8,0},{12,4},{16,24},{20,28},{24,16},{28,20},{1,9},{5... | collective-permute-start | bytes 221192 | tf_op jit(solution)/shard_map/ppermute | solution.py:598
  276.2 6.2 %collective-permute-start.24 = (f32[64,256]{1,0:T(8,128)S(1)}, f32[64,256]{1,0:T(8,128)S(1)}, u32[]{:S(2)}, u32[]{:S(2)}) collective-permute-start(f32[64,256]{1,0:T(8,128)S(1)} %merge.5), channel_id=1, source_target_pairs={{0,24},{4,28},{8,16},{12,20},{16,8},{20,12},{24,0},{28,4},{1,25},{... | collective-permute-start | bytes 196616 | tf_op jit(solution)/shard_map/ppermute | solution.py:605
  278.9 8.7 %collective-permute-start.27 = (f32[64,512]{1,0:T(8,128)S(1)}, f32[64,512]{1,0:T(8,128)S(1)}, u32[]{:S(2)}, u32[]{:S(2)}) collective-permute-start(f32[64,512]{1,0:T(8,128)S(1)} %merge.4.refs_0_), channel_id=1, source_target_pairs={{0,3},{1,2},{2,1},{3,0},{4,7},{5,6},{6,5},{7,4},{8,11},{9,10},{10,... | collective-permute-start | bytes 393224 | tf_op jit(solution)/shard_map/ppermute | solution.py:605
  281.3 6.2 %collective-permute-start.26 = (f32[64,512]{1,0:T(8,128)S(1)}, f32[64,512]{1,0:T(8,128)S(1)}, u32[]{:S(2)}, u32[]{:S(2)}) collective-permute-start(f32[64,512]{1,0:T(8,128)S(1)} %merge.4.refs_0_), channel_id=1, source_target_pairs={{0,2},{1,3},{2,0},{3,1},{4,6},{5,7},{6,4},{7,5},{8,10},{9,11},{10,... | collective-permute-start | bytes 393224 | tf_op jit(solution)/shard_map/ppermute | solution.py:605
  281.9 5.7 %collective-permute-start.25 = (f32[64,512]{1,0:T(8,128)S(1)}, f32[64,512]{1,0:T(8,128)S(1)}, u32[]{:S(2)}, u32[]{:S(2)}) collective-permute-start(f32[64,512]{1,0:T(8,128)S(1)} %merge.4.refs_0_), channel_id=1, source_target_pairs={{0,1},{1,0},{2,3},{3,2},{4,5},{5,4},{6,7},{7,6},{8,9},{9,8},{10,11... | collective-permute-start | bytes 393224 | tf_op jit(solution)/shard_map/ppermute | solution.py:605
  282.4 5.2 %collective-permute-start.23 = (f32[64,256]{1,0:T(8,128)S(1)}, f32[64,256]{1,0:T(8,128)S(1)}, u32[]{:S(2)}, u32[]{:S(2)}) collective-permute-start(f32[64,256]{1,0:T(8,128)S(1)} %merge.5), channel_id=1, source_target_pairs={{0,16},{4,20},{8,24},{12,28},{16,0},{20,4},{24,8},{28,12},{1,17},{... | collective-permute-start | bytes 196616 | tf_op jit(solution)/shard_map/ppermute | solution.py:605
  282.4 5.2 %collective-permute-start.22 = (f32[64,256]{1,0:T(8,128)S(1)}, f32[64,256]{1,0:T(8,128)S(1)}, u32[]{:S(2)}, u32[]{:S(2)}) collective-permute-start(f32[64,256]{1,0:T(8,128)S(1)} %merge.5), channel_id=1, source_target_pairs={{0,8},{4,12},{8,0},{12,4},{16,24},{20,28},{24,16},{28,20},{1,9},{5... | collective-permute-start | bytes 196616 | tf_op jit(solution)/shard_map/ppermute | solution.py:605
  (7 other events, 129.5 us)
